TPU v7x, 256 devices: a whole 4x4x8 slice. The times are simulated.
256 devices in a mesh: dp: 16 (over y, x), tp: 16 (over z, core).
Axes of the slice: x: 4, y: 4, z: 8, core: 2. Of those that a mesh axis runs over, the one named last changes fastest.
Arguments:
- grads: bfloat16 [16, 2, 2560, 5120], P('dp', None, 'tp'), may hold values from -6 to 6
- errors: bfloat16 [16, 2, 2560, 5120], P('dp', None, 'tp'), may hold values from -4 to 4
- basis_in: float32 [2, 2560, 32], P(None, 'tp'), may hold values from -6 to 6
Outputs:
- update: bfloat16 [2, 2560, 5120], P(None, 'tp')
- new_errors: bfloat16 [16, 2, 2560, 5120], P('dp', None, 'tp')
- updated_right_basis: float32 [2, 2560, 32], P(None, 'tp')
All inputs are finite; a program needn't handle non-finite values.
Results may differ from a plain program's by a relative error of at most 0.012.
Values sent between devices are 32-bit elements; how exact they have to be, the bound alone decides.
No kernel may reach another device: no remote copies, remote signals or barrier semaphores. Data moves between devices by JAX's collectives and lax.ppermute only.
A program may use at most 64 MiB of HBM per device.

v0:
```python
import jax
import jax.numpy as jnp
from jax import lax
from jax.sharding import PartitionSpec as P


def triangular(gram, rows):
    lower = jnp.linalg.cholesky(gram)
    solved = jax.scipy.linalg.solve_triangular(lower, jnp.transpose(rows, (1, 2, 0)), lower=True)
    return jnp.transpose(solved, (2, 0, 1))


def gram_of(rows):
    return jnp.einsum("dmr,dms->mrs", rows, rows, precision=lax.Precision.HIGHEST)


def on_device(grads, errors, basis_in):
    error_corrected_gradient = (
        grads[0].astype(jnp.float32) + errors[0].astype(jnp.float32)
    ).astype(jnp.bfloat16)
    query_lower_factor = basis_in.astype(jnp.bfloat16)
    hosts = lax.axis_size("dp")
    summed = lax.psum(
        jnp.einsum(
            "tqj,tqw->jtw",
            error_corrected_gradient,
            query_lower_factor,
            preferred_element_type=jnp.float32,
        ),
        ("dp", "tp"),
    )
    orthonormal_left = triangular(gram_of(summed), summed)
    orthonormal_lower_factor = orthonormal_left.astype(jnp.bfloat16)
    right_local = jnp.einsum(
        "sct,tsj->scj",
        error_corrected_gradient,
        orthonormal_lower_factor,
        preferred_element_type=jnp.float32,
    )
    updated_right_basis = lax.psum(right_local, "dp") / hosts
    reconstructed_gradient = jnp.einsum(
        "viz,ibz->ibv", orthonormal_left, updated_right_basis, precision=lax.Precision.HIGHEST
    )
    update = reconstructed_gradient.astype(jnp.bfloat16)
    new_errors = (error_corrected_gradient.astype(jnp.float32) - reconstructed_gradient).astype(
        jnp.bfloat16
    )[None]
    return (update, new_errors, updated_right_basis)


def solution(mesh):
    return jax.shard_map(
        on_device,
        mesh=mesh,
        in_specs=(P("dp", None, "tp", None), P("dp", None, "tp", None), P(None, "tp", None)),
        out_specs=(P(None, "tp", None), P("dp", None, "tp", None), P(None, "tp", None)),
        check_vma=False,
    )
```

profile of v0, /device:TPU:2, one launch (start us, length us, event | category | flops | bytes accessed | tf_op | source)
XLA Modules:
  0.0 381.1 jit_solution(7811582123045979760)
XLA Ops:
  7.2 0.0 all-reduce.2.cloned.1.call-start
  7.2 5.0 %convolution_bitcast_fusion = f32[5120,2,32]{0,2,1:T(8,128)} fusion(f32[2,160,32]{1,2,0:T(8,128)} %param.5, bf16[1,2,160,5120]{3,2,1,0:T(8,128)(2,1)} %param.4, bf16[1,2,160,5120]{3,2,1,0:T(8,128)(2,1)} %param.3), kind=kOutput, calls=%fused_computation.2 | convolution fusion | flops 111421440 | bytes 7905280 | tf_op jit(solution)/shard_map/tqj,tqw->jtw/dot_general | solution.py:24
  12.3 0.0 copy-start
  12.3 0.0 all-reduce.2.cloned.1.call-update
  12.3 263.3 %all-reduce.2.cloned.1.call-done = f32[5120,2,32]{0,2,1:T(8,128)} async-done(((f32[5120,2,32]{0,2,1:T(8,128)}), f32[5120,2,32]{0,2,1:T(8,128)}) %all-reduce.2.cloned.1.call-update) | async-done | bytes 1310736 | tf_op jit(solution)/shard_map/psum | solution.py:23
  275.6 3.0 fusion.10
  278.7 0.1 copy.8
  278.8 5.9 %custom-call.8 = f32[2,32,32]{2,1,0:T(8,128)S(1)} custom-call(f32[2,32,32]{2,1,0:T(8,128)S(1)} %fusion.6), custom_call_target="Cholesky" | custom-call | tf_op jit(solution)/shard_map/jit(cholesky)/cholesky | solution.py:8
  284.7 0.1 compare_reduce_fusion
  284.8 0.1 select_bitcast_fusion
  284.9 4.9 %custom-call.9 = f32[2,1,32,32]{2,3,1,0:T(8,128)S(1)} custom-call(f32[2,1,32,32]{3,2,1,0:T(8,128)S(1)} %select_bitcast_fusion), custom_call_target="InvertDiagBlocksLowerTriangular" | custom-call | tf_op jit(solution)/shard_map/jit(_solve_triangular)/vmap()/triangular_solve | solution.py:9
  289.8 2.6 convolution_bitcast_fusion.1
  292.4 0.0 copy-start.1
  292.4 1.1 copy-done.1
  293.4 0.0 copy-done
  293.4 3.1 fusion.3
  296.5 68.1 %psum.15 = f32[2,160,32]{1,2,0:T(8,128)S(1)} all-reduce(f32[2,160,32]{1,2,0:T(8,128)S(1)} %fusion.3), channel_id=1, replica_groups=mesh['dp'=16,'tp'=16] {'dp'}, use_global_device_ids=true, to_apply=%region_3.4 | all-reduce | flops 10240 | bytes 81920 | tf_op jit(solution)/shard_map/psum | solution.py:40
  364.6 0.0 copy-start.2
  364.6 9.6 %fusion.1 = (bf16[1,2,160,5120]{3,2,1,0:T(8,128)(2,1)}, bf16[2,160,5120]{2,1,0:T(8,128)(2,1)}) fusion(bf16[1,2,160,5120]{3,2,1,0:T(8,128)(2,1)S(1)} %copy-done, bf16[1,2,160,5120]{3,2,1,0:T(8,128)(2,1)} %param.3, f32[2,160,32]{1,2,0:T(8,128)S(1)} %broadcast_multiply_fusion, f32[5120,2,32]{0,2,1:T(8,128)} %copy-done.1), kind=kOutput, calls=%fused_computation.5 | convolution fusion | flops 642252800 | bytes 14458880 | tf_op jit(solution)/shard_map/viz,ibz->ibv/dot_general | solution.py:41
  374.2 0.0 copy-done.2
  (5 shorter events, 0.1 us)
Async XLA Ops:
  7.2 268.5 %all-reduce.2.cloned.1.call-start = ((), (), s32[]{:S(2)}) async-start(), calls=%async_computation | async-start | bytes 2621440 | tf_op jit(solution)/shard_map/psum | solution.py:23
  12.3 281.2 %copy-start = (bf16[1,2,160,5120]{3,2,1,0:T(8,128)(2,1)S(1)}, bf16[1,2,160,5120]{3,2,1,0:T(8,128)(2,1)}, u32[]{:S(2)}) copy-start(bf16[1,2,160,5120]{3,2,1,0:T(8,128)(2,1)} %param.4) | copy-start | bytes 9830404
  292.4 1.1 copy-start.1
  364.6 9.6 %copy-start.2 = (f32[2,160,32]{1,2,0:T(8,128)}, f32[2,160,32]{1,2,0:T(8,128)S(1)}, u32[]{:S(2)}) copy-start(f32[2,160,32]{1,2,0:T(8,128)S(1)} %broadcast_multiply_fusion) | copy-start | bytes 122884
Sparse Core Ops, SparseCore 0:
  13.9 261.6 all-reduce.1
where the time goes:
time: 385 us; the launch traced here: 381 us
  waiting for transfers between devices  263 us (68%)
  blocking collectives  68.1 us (18%)
  matrix products  23.3 us (6%)
  between operations  14.1 us (4%)
  other arithmetic  11 us (3%)
    psum x1, waiting for transfers between devices, on_device(): lax.psum(jnp.einsum('tqj,tqw->jtw', error_corrected_gradient, query_lower...  263 us
    psum x1, blocking collectives, on_device(): updated_right_basis = lax.psum(right_local, 'dp') / hosts  68.1 us
    dot_general x1, matrix products, on_device(): jnp.einsum('viz,ibz->ibv', orthonormal_left, updated_right_basis, precisi...  9.61 us
  transfers between devices with their start and end apart: 1, of which 1 were waited for; matrix products, arithmetic and copies ran while one was open for 0% of the time, Pallas kernels for 0%

commit v1 on v0

v1 whole, which is shorter than its diff:
```python
import functools

import jax
import jax.numpy as jnp
from jax import lax
from jax.experimental import pallas as pl
from jax.experimental.pallas import tpu as pltpu
from jax.sharding import PartitionSpec as P

D = 5120
ROWS = 160
RANK = 32
HOSTS = 16
CHUNKS = 32
CHUNK_COLS = 640
COL_BLOCKS = D // CHUNK_COLS
AXES = ("dp", "tp")
MIB = 1 << 20


def device(x, y, z, c):
    return (y * 4 + x) * 16 + z * 2 + c


def everyone():
    return [(x, y, z, c) for y in range(4) for x in range(4) for z in range(8) for c in range(2)]


def pairs(move):
    return [(device(*at), device(*move(*at))) for at in everyone()]


CORE_SWAP = pairs(lambda x, y, z, c: (x, y, z, 1 - c))


def z_pairs(k):
    return pairs(lambda x, y, z, c: (x, y, z ^ (2 * k), c))


def first_pairs(k):
    return pairs(lambda x, y, z, c: (x ^ k, y, z, c) if c == 0 else (x, y ^ k, z, c))


def second_pairs(k):
    return pairs(lambda x, y, z, c: (x, y ^ k, z, c) if c == 0 else (x ^ k, y, z, c))


GROUPS = [
    [device(x, y, zz * 2 + k, c) for k in range(2) for y in range(4) for x in range(4)]
    for zz in range(4)
    for c in range(2)
]


def exchange(parts):
    return lax.all_to_all(parts, AXES, 0, 0, axis_index_groups=GROUPS, tiled=True)


def permute(a, perm):
    return lax.ppermute(a, AXES, perm)


def split3(a):
    hi = a.astype(jnp.bfloat16)
    rest = a - hi.astype(jnp.float32)
    mid = rest.astype(jnp.bfloat16)
    lo = (rest - mid.astype(jnp.float32)).astype(jnp.bfloat16)
    return hi, mid, lo


def cost(flops, nbytes):
    return pl.CostEstimate(flops=flops, bytes_accessed=nbytes, transcendentals=0)


def left_kernel(m_ref, grads_ref, errors_ref, basis_ref, corrected_ref, left_ref):
    corrected = (
        grads_ref[0, 0].astype(jnp.float32) + errors_ref[0, 0].astype(jnp.float32)
    ).astype(jnp.bfloat16)
    corrected_ref[...] = corrected
    left = lax.dot_general(
        basis_ref[0].astype(jnp.bfloat16),
        corrected,
        (((0,), (0,)), ((), ())),
        preferred_element_type=jnp.float32,
    )
    blocks = left.shape[1] // CHUNK_COLS
    for b in range(blocks):
        for g in range(4):
            left_ref[b * 4 + g] = left[8 * g : 8 * g + 8, b * CHUNK_COLS : (b + 1) * CHUNK_COLS]


def left_part(m, grads, errors, basis, steps=4):
    cols = D // steps
    return pl.pallas_call(
        left_kernel,
        grid_spec=pltpu.PrefetchScalarGridSpec(
            num_scalar_prefetch=1,
            grid=(steps,),
            in_specs=[
                pl.BlockSpec((1, 1, ROWS, cols), lambda j, m: (0, m[0], 0, j)),
                pl.BlockSpec((1, 1, ROWS, cols), lambda j, m: (0, m[0], 0, j)),
                pl.BlockSpec((1, ROWS, RANK), lambda j, m: (m[0], 0, 0)),
            ],
            out_specs=[
                pl.BlockSpec((ROWS, cols), lambda j, m: (0, j)),
                pl.BlockSpec((CHUNKS // steps, 8, CHUNK_COLS), lambda j, m: (j, 0, 0)),
            ],
        ),
        out_shape=[
            jax.ShapeDtypeStruct((ROWS, D), jnp.bfloat16),
            jax.ShapeDtypeStruct((CHUNKS, 8, CHUNK_COLS), jnp.float32),
        ],
        compiler_params=pltpu.CompilerParams(vmem_limit_bytes=16 * MIB),
        cost_estimate=cost(2 * ROWS * D * RANK, 6 * ROWS * D + 4 * RANK * D),
        name="left",
    )(m, grads, errors, basis)


def right_body(left_ref, corrected_ref, terms_ref, stack_ref):
    for b in range(COL_BLOCKS):
        cols = slice(b * CHUNK_COLS, (b + 1) * CHUNK_COLS)
        for g in range(4):
            rows = slice(8 * g, 8 * g + 8)
            stack_ref[rows, cols] = left_ref[b * 4 + g]
    for b in range(COL_BLOCKS):
        cols = slice(b * CHUNK_COLS, (b + 1) * CHUNK_COLS)
        hi, mid, lo = split3(stack_ref[:, cols])
        for i, term in enumerate((hi, mid, lo, hi, mid, hi)):
            terms_ref[i * RANK : (i + 1) * RANK, cols] = term
    terms = terms_ref[0 : 3 * RANK, :]
    nt = (((1,), (1,)), ((), ()))
    t = lax.dot_general(corrected_ref[...], terms, nt, preferred_element_type=jnp.float32)
    t = t[:, 0:RANK] + (t[:, RANK : 2 * RANK] + t[:, 2 * RANK : 3 * RANK])
    packed = jnp.concatenate([t[40 * i : 40 * i + 40] for i in range(4)], axis=1)
    g = lax.dot_general(terms, terms, nt, preferred_element_type=jnp.float32)
    gram = g[0:RANK, 0:RANK]
    rest = jnp.zeros_like(gram)
    for i in range(3):
        for j in range(3):
            if i + j > 0:
                rest = rest + g[i * RANK : (i + 1) * RANK, j * RANK : (j + 1) * RANK]
    return packed, gram + rest


def right_kernel(left_ref, corrected_ref, t_ref, gram_ref, terms_ref, stack_ref):
    t_ref[...], gram_ref[...] = right_body(left_ref, corrected_ref, terms_ref, stack_ref)


def right_both_kernel(
    left_ref, corrected_ref, t_own_ref, gram_own_ref, t_ref, gram_ref, terms_ref, stack_ref
):
    t, gram = right_body(left_ref, corrected_ref, terms_ref, stack_ref)
    t_ref[0:40] = t_own_ref[...]
    t_ref[40:80] = t
    gram_ref[0] = gram_own_ref[...]
    gram_ref[1] = gram


def vmem(n):
    return [pl.BlockSpec(memory_space=pltpu.VMEM)] * n


def right_part(left, corrected, own=None):
    both = own is not None
    n = 2 if both else 1
    return pl.pallas_call(
        right_both_kernel if both else right_kernel,
        in_specs=vmem(4 if both else 2),
        out_specs=vmem(3),
        out_shape=[
            jax.ShapeDtypeStruct((40 * n, 128), jnp.float32),
            jax.ShapeDtypeStruct((2, RANK, RANK) if both else (RANK, RANK), jnp.float32),
            jax.ShapeDtypeStruct((6 * RANK, D), jnp.bfloat16),
        ],
        scratch_shapes=[pltpu.VMEM((RANK, D), jnp.float32)],
        compiler_params=pltpu.CompilerParams(vmem_limit_bytes=24 * MIB),
        cost_estimate=cost(2 * 256 * D * 96, 2 * ROWS * D + 16 * RANK * D),
        name="right",
    )(left, corrected, *(own or ()))


def inverse_kernel(gram_ref, inverse_ref):
    row = lax.broadcasted_iota(jnp.int32, (RANK, RANK), 0)
    col = lax.broadcasted_iota(jnp.int32, (RANK, RANK), 1)
    eye = jnp.where(row == col, 1.0, 0.0).astype(jnp.float32)
    a = jnp.concatenate([gram_ref[0], eye, gram_ref[1], eye], axis=1)
    rows = lax.broadcasted_iota(jnp.int32, (RANK, 4 * RANK), 0)
    lanes = lax.broadcasted_iota(jnp.int32, (RANK, 4 * RANK), 1)
    first = lanes < 2 * RANK
    for k in range(RANK):
        left = jnp.broadcast_to(a[:, k : k + 1], a.shape)
        right = jnp.broadcast_to(a[:, 2 * RANK + k : 2 * RANK + k + 1], a.shape)
        column = jnp.where(first, left, right)
        scale = lax.rsqrt(column[k : k + 1, :])
        pivot_row = a[k : k + 1, :] * scale
        below = jnp.where(rows > k, column * scale, 0.0)
        a = jnp.where(rows == k, pivot_row, a - below * pivot_row)
    inverse_ref[0] = a[:, RANK : 2 * RANK]
    inverse_ref[1] = a[:, 3 * RANK : 4 * RANK]


def inverses(gram):
    return pl.pallas_call(
        inverse_kernel,
        in_specs=vmem(1),
        out_specs=pl.BlockSpec(memory_space=pltpu.VMEM),
        out_shape=jax.ShapeDtypeStruct((2, RANK, RANK), jnp.float32),
        compiler_params=pltpu.CompilerParams(vmem_limit_bytes=4 * MIB),
        cost_estimate=cost(10_000_000, 8_000_000),
        name="inverse",
    )(gram)


def final_kernel(
    c_ref,
    t0_ref,
    t1_ref,
    t2_ref,
    t3_ref,
    inverse_ref,
    terms_own_ref,
    terms_other_ref,
    corrected_own_ref,
    corrected_other_ref,
    update_ref,
    errors_ref,
    right_ref,
    w_ref,
):
    high = functools.partial(
        lax.dot_general, precision=lax.Precision.HIGHEST, preferred_element_type=jnp.float32
    )
    i = pl.program_id(0)
    j = pl.program_id(1)

    @pl.when((i == 0) & (j == 0))
    def _():
        t = (t0_ref[...] + t1_ref[...]) + (t2_ref[...] + t3_ref[...])
        for n in range(2):
            mine = t[40 * n : 40 * n + 40]
            mine = jnp.concatenate(
                [mine[:, RANK * q : RANK * q + RANK] for q in range(4)], axis=0
            )
            inverse = inverse_ref[n]
            right = high(mine, inverse, (((1,), (1,)), ((), ()))) * (1.0 / HOSTS)
            right_ref[c_ref[n]] = right
            hi, mid, lo = split3(high(right, inverse, (((1,), (0,)), ((), ()))))
            w_ref[n] = jnp.concatenate([hi, hi, hi, mid, mid, lo], axis=1)

    def finish(terms_ref, corrected_ref, n):
        recon = jnp.dot(w_ref[n], terms_ref[...], preferred_element_type=jnp.float32)
        update_ref[0] = recon.astype(jnp.bfloat16)
        errors_ref[0, 0] = (corrected_ref[...].astype(jnp.float32) - recon).astype(jnp.bfloat16)

    @pl.when(i == 0)
    def _():
        finish(terms_own_ref, corrected_own_ref, 0)

    @pl.when(i == 1)
    def _():
        finish(terms_other_ref, corrected_other_ref, 1)


def final_part(order, ts, inverse, terms_own, terms_other, corrected_own, corrected_other, steps=4):
    cols = D // steps
    own = lambda i, j, c: (0, jnp.where(i == 0, j, steps - 1))
    other = lambda i, j, c: (0, jnp.where(i == 0, 0, j))
    whole = [pl.BlockSpec((80, 128), lambda i, j, c: (0, 0))] * 4
    return pl.pallas_call(
        final_kernel,
        grid_spec=pltpu.PrefetchScalarGridSpec(
            num_scalar_prefetch=1,
            grid=(2, steps),
            in_specs=whole
            + [
                pl.BlockSpec((2, RANK, RANK), lambda i, j, c: (0, 0, 0)),
                pl.BlockSpec((6 * RANK, cols), own),
                pl.BlockSpec((6 * RANK, cols), other),
                pl.BlockSpec((ROWS, cols), own),
                pl.BlockSpec((ROWS, cols), other),
            ],
            out_specs=[
                pl.BlockSpec((1, ROWS, cols), lambda i, j, c: (c[i], 0, j)),
                pl.BlockSpec((1, 1, ROWS, cols), lambda i, j, c: (0, c[i], 0, j)),
                pl.BlockSpec((2, ROWS, RANK), lambda i, j, c: (0, 0, 0)),
            ],
            scratch_shapes=[pltpu.VMEM((2, ROWS, 6 * RANK), jnp.bfloat16)],
        ),
        out_shape=[
            jax.ShapeDtypeStruct((2, ROWS, D), jnp.bfloat16),
            jax.ShapeDtypeStruct((1, 2, ROWS, D), jnp.bfloat16),
            jax.ShapeDtypeStruct((2, ROWS, RANK), jnp.float32),
        ],
        compiler_params=pltpu.CompilerParams(vmem_limit_bytes=24 * MIB),
        cost_estimate=cost(2 * 2 * ROWS * 192 * D, 16 * ROWS * D),
        name="final",
    )(order, *ts, inverse, terms_own, terms_other, corrected_own, corrected_other)


def on_device(grads, errors, basis_in):
    core = lax.rem(lax.axis_index("tp"), 2).astype(jnp.int32)
    corrected_other, left_other = left_part((1 - core)[None], grads, errors, basis_in)
    with jax.named_scope("left_core_swap"):
        arrived = permute(left_other, CORE_SWAP)
    corrected_own, left_own = left_part(core[None], grads, errors, basis_in)
    with jax.named_scope("left_sum"):
        parts = exchange(left_own + arrived)
        part = jnp.sum(parts, axis=0)
        p1, p3, p2 = (permute(part, z_pairs(k)) for k in (1, 3, 2))
        part = (part + p1) + (p2 + p3)
        left_own = exchange(jnp.broadcast_to(part[None], (CHUNKS,) + part.shape))
        left_other = permute(left_own, CORE_SWAP)
    t_own, gram_own, terms_own = right_part(left_own, corrected_own)
    t, gram, terms_other = right_part(left_other, corrected_other, (t_own, gram_own))
    with jax.named_scope("right_sum"):
        t1, t3, t2 = (permute(t, first_pairs(k)) for k in (1, 3, 2))
        t = (t + t1) + (t2 + t3)
        t1, t3, t2 = (permute(t, second_pairs(k)) for k in (1, 3, 2))
    inverse = inverses(gram)
    order = jnp.stack([core, 1 - core])
    return tuple(
        final_part(
            order, (t, t1, t2, t3), inverse, terms_own, terms_other, corrected_own, corrected_other
        )
    )


def solution(mesh):
    return jax.shard_map(
        on_device,
        mesh=mesh,
        in_specs=(P("dp", None, "tp", None), P("dp", None, "tp", None), P(None, "tp", None)),
        out_specs=(P(None, "tp", None), P("dp", None, "tp", None), P(None, "tp", None)),
        check_vma=False,
    )
```

time: 385 us -> 85.8 us (0.22)
  waiting for transfers between devices: 263 us -> 10.5 us
  blocking collectives: 68.1 us -> 36 us
  matrix products: 23.3 us -> 0 us
  starting transfers between devices: 0.04 us -> 16.4 us
  Pallas kernels: 0 us -> 14.4 us
  between operations: 14.1 us -> 0.73 us
  other arithmetic: 11 us -> 1.33 us
  local copies, waits for them, and re-layouts: 1.14 us -> 6.13 us
    psum x1 -> x0, waiting for transfers between devices: 263 us -> none  [on_device(): lax.psum(jnp.einsum('tqj,tqw->jtw', error_corrected_gradient, query_lower...]
    psum x1 -> x0, blocking collectives: 68.1 us -> none  [on_device(): updated_right_basis = lax.psum(right_local, 'dp') / hosts]
    all_to_all x0 -> x2, blocking collectives: none -> 36 us  [exchange(): lax.all_to_all(parts, AXES, 0, 0, axis_index_groups=GROUPS, tiled=True)]
    dot_general x4 -> x0, matrix products: 20.8 us -> none  [the longest x1 9.61 us: on_device(): jnp.einsum('viz,ibz->ibv', orthonormal_left, updated_right_basis, precisi...]
    ppermute x0 -> x11, starting transfers between devices: none -> 16.4 us  [permute(): return lax.ppermute(a, AXES, perm)]
    pallas_call x0 -> x6, Pallas kernels: none -> 14.4 us  [the longest x1 7.04 us: final_part(): pl.pallas_call(final_kernel, grid_spec=pltpu.PrefetchScalarGridSpec(num_s...]
    another operation x7 -> x1, other arithmetic: 11 us -> 0.07 us  [on_device(): order = jnp.stack([core, 1 - core])]
    ppermute x0 -> x11, waiting for transfers between devices: none -> 10.5 us  [permute(): return lax.ppermute(a, AXES, perm)]
  transfers between devices with their start and end apart: 1 -> 11, of which waited for: 1 -> 6; matrix products, arithmetic and copies ran while one was open for 0% -> 0% of each run, Pallas kernels for 0% -> 6%
where the time goes in v1:
time: 85.8 us; the launch traced here: 85.5 us
  blocking collectives  36 us (42%)
  starting transfers between devices  16.4 us (19%)
  Pallas kernels  14.4 us (17%)
  waiting for transfers between devices  10.5 us (12%)
  local copies, waits for them, and re-layouts  6.13 us (7%)
  other arithmetic  1.33 us (2%)
    all_to_all x2, blocking collectives, exchange(): lax.all_to_all(parts, AXES, 0, 0, axis_index_groups=GROUPS, tiled=True)  36 us
    ppermute x11, starting transfers between devices, permute(): return lax.ppermute(a, AXES, perm)  16.4 us
    ppermute x11, waiting for transfers between devices, permute(): return lax.ppermute(a, AXES, perm)  10.5 us
    pallas_call x1, Pallas kernels, final_part(): pl.pallas_call(final_kernel, grid_spec=pltpu.PrefetchScalarGridSpec(num_s...  7.04 us
    unnamed x7, local copies, waits for them, and re-layouts  5.34 us
    pallas_call x1, Pallas kernels, inverses(): pl.pallas_call(inverse_kernel, in_specs=vmem(1), out_specs=pl.BlockSpec(m...  2.76 us
    pallas_call x2, Pallas kernels, left_part(): pl.pallas_call(left_kernel, grid_spec=pltpu.PrefetchScalarGridSpec(num_sc...  2.52 us
    pallas_call x2, Pallas kernels, right_part(): pl.pallas_call(right_both_kernel if both else right_kernel, in_specs=vmem...  2.13 us
  transfers between devices with their start and end apart: 11, of which 6 were waited for; matrix products, arithmetic and copies ran while one was open for 0% of the time, Pallas kernels for 6%

profile of v1, /device:TPU:2, one launch (start us, length us, event | category | flops | bytes accessed | tf_op | source)
XLA Modules:
  0.0 85.5 jit_solution(1114108842293479144)
XLA Ops:
  0.6 0.9 %copy.6.basis_ref = f32[2,160,32]{2,1,0:T(8,128)S(1)} copy(f32[2,160,32]{1,2,0:T(8,128)} %param.5) | data formatting | bytes 81920 | tf_op args[2]
  1.6 1.9 %copy-done = bf16[1,2,160,5120]{3,2,1,0:T(8,128)(2,1)S(1)} copy-done((bf16[1,2,160,5120]{3,2,1,0:T(8,128)(2,1)S(1)}, bf16[1,2,160,5120]{3,2,1,0:T(8,128)(2,1)}, u32[]{:S(2)}) %copy-start) | copy-done | bytes 3276824
  3.5 1.9 %copy-done.2 = bf16[1,2,160,5120]{3,2,1,0:T(8,128)(2,1)S(1)} copy-done((bf16[1,2,160,5120]{3,2,1,0:T(8,128)(2,1)S(1)}, bf16[1,2,160,5120]{3,2,1,0:T(8,128)(2,1)}, u32[]{:S(2)}) %copy-start.2) | copy-done | bytes 3276824
  5.4 1.3 %left.3 = (bf16[160,5120]{1,0:T(8,128)(2,1)S(1)}, f32[32,8,640]{2,1,0:T(8,128)S(1)}) custom-call(s32[1]{0:T(128)} %bitcast.1.m_ref, bf16[1,2,160,5120]{3,2,1,0:T(8,128)(2,1)S(1)} %copy-done, bf16[1,2,160,5120]{3,2,1,0:T(8,128)(2,1)S(1)} %copy-done.2, f32[2,160,32]{2,1,0:T(8,128)S(1)} %copy.6.basis_ref), custom_call_target="tpu_custom_call" | custom-call | flops 52428800 | bytes 5570560 | tf_op jit(solution)/shard_map/left/pallas_call | solution.py:94
  6.7 0.1 collective-permute-start
  6.8 0.6 copy-done.1
  7.4 1.3 %left.2 = (bf16[160,5120]{1,0:T(8,128)(2,1)S(1)}, f32[32,8,640]{2,1,0:T(8,128)S(1)}) custom-call(s32[1]{0:T(128)} %bitcast.m_ref, bf16[1,2,160,5120]{3,2,1,0:T(8,128)(2,1)S(1)} %copy-done.1, bf16[1,2,160,5120]{3,2,1,0:T(8,128)(2,1)S(1)} %copy-done.2, f32[2,160,32]{2,1,0:T(8,128)S(1)} %copy.6.basis_ref), custom_call_target="tpu_custom_call" | custom-call | flops 52428800 | bytes 5570560 | tf_op jit(solution)/shard_map/left/pallas_call | solution.py:94
  8.6 0.3 collective-permute-done
  8.9 0.1 add.21
  9.0 20.8 %all_to_all.10 = f32[32,8,640]{2,1,0:T(8,128)} all-to-all(f32[32,8,640]{2,1,0:T(8,128)S(1)} %add.21), channel_id=1, replica_groups={{0,16,32,48,64,80,96,112,128,144,160,176,192,208,224,240,2,18,34,50,66,..., dimensions={0} | all-to-all | bytes 1310720 | tf_op jit(solution)/shard_map/left_sum/all_to_all | solution.py:56
  29.8 1.1 %reduce_sum.9 = f32[8,640]{1,0:T(8,128)S(1)} reduce(f32[32,8,640]{2,1,0:T(8,128)} %all_to_all.10, f32[]{:T(128)} %constant.11.clone.1), dimensions={0}, to_apply=%region_0.0 | reduce | flops 158720 | bytes 675844 | tf_op jit(solution)/shard_map/left_sum/reduce_sum | solution.py:308
  30.9 5.5 %collective-permute-start.3 = (f32[8,640]{1,0:T(8,128)S(1)}, f32[8,640]{1,0:T(8,128)S(1)}, u32[]{:S(2)}, u32[]{:S(2)}) collective-permute-start(f32[8,640]{1,0:T(8,128)S(1)} %reduce_sum.9), channel_id=1, source_target_pairs={{0,12},{1,13},{2,14},{3,15},{4,8},{5,9},{6,10},{7,11},{8,4},{9,5},... | collective-permute-start | bytes 61448 | tf_op jit(solution)/shard_map/left_sum/ppermute | solution.py:60
  36.4 1.4 %collective-permute-start.2 = (f32[8,640]{1,0:T(8,128)S(1)}, f32[8,640]{1,0:T(8,128)S(1)}, u32[]{:S(2)}, u32[]{:S(2)}) collective-permute-start(f32[8,640]{1,0:T(8,128)S(1)} %reduce_sum.9), channel_id=1, source_target_pairs={{0,8},{1,9},{2,10},{3,11},{4,12},{5,13},{6,14},{7,15},{8,0},{9,1},... | collective-permute-start | bytes 61448 | tf_op jit(solution)/shard_map/left_sum/ppermute | solution.py:60
  37.8 1.0 %collective-permute-start.1 = (f32[8,640]{1,0:T(8,128)S(1)}, f32[8,640]{1,0:T(8,128)S(1)}, u32[]{:S(2)}, u32[]{:S(2)}) collective-permute-start(f32[8,640]{1,0:T(8,128)S(1)} %reduce_sum.9), channel_id=1, source_target_pairs={{0,4},{1,5},{2,6},{3,7},{4,0},{5,1},{6,2},{7,3},{8,12},{9,13},{10,... | collective-permute-start | bytes 61448 | tf_op jit(solution)/shard_map/left_sum/ppermute | solution.py:60
  38.8 5.2 %collective-permute-done.2 = f32[8,640]{1,0:T(8,128)S(1)} collective-permute-done((f32[8,640]{1,0:T(8,128)S(1)}, f32[8,640]{1,0:T(8,128)S(1)}, u32[]{:S(2)}, u32[]{:S(2)}) %collective-permute-start.2) | collective-permute-done | bytes 20512 | tf_op jit(solution)/shard_map/left_sum/ppermute | solution.py:60
  44.1 15.2 %all_to_all.11.left_ref = f32[32,8,640]{2,1,0:T(8,128)S(1)} all-to-all(f32[32,8,640]{2,1,0:T(8,128)S(1)} %broadcast_in_dim.2), channel_id=1, replica_groups={{0,16,32,48,64,80,96,112,128,144,160,176,192,208,224,240,2,18,34,50,66,..., dimensions={0} | all-to-all | bytes 1310720 | tf_op jit(solution)/shard_map/left_sum/all_to_all | solution.py:56
  59.3 1.1 %right.2 = (f32[40,128]{1,0:T(8,128)S(1)}, f32[32,32]{1,0:T(8,128)S(1)}, bf16[192,5120]{1,0:T(8,128)(2,1)S(1)}) custom-call(f32[32,8,640]{2,1,0:T(8,128)S(1)} %all_to_all.11.left_ref, bf16[160,5120]{1,0:T(8,128)(2,1)S(1)} %get-tuple-element.16.corrected_ref.corrected_own_ref), custom_call_target="tpu_custom_call" | custom-call | flops 251658240 | bytes 4259840 | tf_op jit(solution)/shard_map/right/pallas_call | solution.py:166
  60.4 1.0 %collective-permute-done.4.left_ref = f32[32,8,640]{2,1,0:T(8,128)S(1)} collective-permute-done((f32[32,8,640]{2,1,0:T(8,128)S(1)}, f32[32,8,640]{2,1,0:T(8,128)S(1)}, u32[]{:S(2)}, u32[]{:S(2)}) %collective-permute-start.4) | collective-permute-done | bytes 655392 | tf_op jit(solution)/shard_map/left_sum/ppermute | solution.py:60
  61.4 1.1 %right.3 = (f32[80,128]{1,0:T(8,128)S(1)}, f32[2,32,32]{2,1,0:T(8,128)S(1)}, bf16[192,5120]{1,0:T(8,128)(2,1)S(1)}) custom-call(f32[32,8,640]{2,1,0:T(8,128)S(1)} %collective-permute-done.4.left_ref, bf16[160,5120]{1,0:T(8,128)(2,1)S(1)} %get-tuple-element.15.corrected_ref.corrected_other_ref, f32[40,128]{1,0:T(8,128)S(1)} %get-tuple-element.17.t_own_ref, ...), custom_call_target="tpu_custom_call" | custom-call | flops 251658240 | bytes 4259840 | tf_op jit(solution)/shard_map/right/pallas_call | solution.py:166
  62.5 1.3 %collective-permute-start.7 = (f32[80,128]{1,0:T(8,128)S(1)}, f32[80,128]{1,0:T(8,128)S(1)}, u32[]{:S(2)}, u32[]{:S(2)}) collective-permute-start(f32[80,128]{1,0:T(8,128)S(1)} %get-tuple-element.19), channel_id=1, source_target_pairs={{0,48},{1,193},{2,50},{3,195},{4,52},{5,197},{6,54},{7,199},{8,56}... | collective-permute-start | bytes 122888 | tf_op jit(solution)/shard_map/right_sum/ppermute | solution.py:60
  63.8 2.4 %collective-permute-start.6 = (f32[80,128]{1,0:T(8,128)S(1)}, f32[80,128]{1,0:T(8,128)S(1)}, u32[]{:S(2)}, u32[]{:S(2)}) collective-permute-start(f32[80,128]{1,0:T(8,128)S(1)} %get-tuple-element.19), channel_id=1, source_target_pairs={{0,32},{1,129},{2,34},{3,131},{4,36},{5,133},{6,38},{7,135},{8,40}... | collective-permute-start | bytes 122888 | tf_op jit(solution)/shard_map/right_sum/ppermute | solution.py:60
  66.2 0.5 collective-permute-start.5
  66.7 2.6 %collective-permute-done.6 = f32[80,128]{1,0:T(8,128)S(1)} collective-permute-done((f32[80,128]{1,0:T(8,128)S(1)}, f32[80,128]{1,0:T(8,128)S(1)}, u32[]{:S(2)}, u32[]{:S(2)}) %collective-permute-start.6) | collective-permute-done | bytes 40992 | tf_op jit(solution)/shard_map/right_sum/ppermute | solution.py:60
  69.3 0.9 %collective-permute-done.5 = f32[80,128]{1,0:T(8,128)S(1)} collective-permute-done((f32[80,128]{1,0:T(8,128)S(1)}, f32[80,128]{1,0:T(8,128)S(1)}, u32[]{:S(2)}, u32[]{:S(2)}) %collective-permute-start.5) | collective-permute-done | bytes 40992 | tf_op jit(solution)/shard_map/right_sum/ppermute | solution.py:60
  70.2 2.0 %collective-permute-start.10 = (f32[80,128]{1,0:T(8,128)S(1)}, f32[80,128]{1,0:T(8,128)S(1)}, u32[]{:S(2)}, u32[]{:S(2)}) collective-permute-start(f32[80,128]{1,0:T(8,128)S(1)} %add_add_fusion.t0_ref), channel_id=1, source_target_pairs={{0,192},{1,49},{2,194},{3,51},{4,196},{5,53},{6,198},{7,55},{8,200... | collective-permute-start | bytes 122888 | tf_op jit(solution)/shard_map/right_sum/ppermute | solution.py:60
  72.2 0.8 collective-permute-start.9
  73.0 1.4 %collective-permute-start.8 = (f32[80,128]{1,0:T(8,128)S(1)}, f32[80,128]{1,0:T(8,128)S(1)}, u32[]{:S(2)}, u32[]{:S(2)}) collective-permute-start(f32[80,128]{1,0:T(8,128)S(1)} %add_add_fusion.t0_ref), channel_id=1, source_target_pairs={{0,64},{1,17},{2,66},{3,19},{4,68},{5,21},{6,70},{7,23},{8,72},{9,... | collective-permute-start | bytes 122888 | tf_op jit(solution)/shard_map/right_sum/ppermute | solution.py:60
  74.4 0.1 pad_add_fusion.c_ref
  74.5 2.8 %inverse.1.inverse_ref = f32[2,32,32]{2,1,0:T(8,128)S(1)} custom-call(f32[2,32,32]{2,1,0:T(8,128)S(1)} %get-tuple-element.20.gram_ref), custom_call_target="tpu_custom_call" | custom-call | flops 10000000 | bytes 8000000 | tf_op jit(solution)/shard_map/inverse/pallas_call | solution.py:203
  77.2 0.4 collective-permute-done.9.t2_ref
  77.7 7.0 %final.1 = (bf16[2,160,5120]{2,1,0:T(8,128)(2,1)}, bf16[1,2,160,5120]{3,2,1,0:T(8,128)(2,1)}, f32[2,160,32]{2,1,0:T(8,128)S(1)}) custom-call(s32[2]{0:T(128)S(1)} %pad_add_fusion.c_ref, f32[80,128]{1,0:T(8,128)S(1)} %add_add_fusion.t0_ref, f32[80,128]{1,0:T(8,128)S(1)} %collective-permute-done.8.t1_ref, f32[80,128]{1,0:T(8,128)S(1)} %collective-permute-done.9.t2_ref, ...), custom_call_target="tpu_custom_call" | custom-call | flops 629145600 | bytes 13107200 | tf_op jit(solution)/shard_map/final/pallas_call | solution.py:269
  84.7 0.7 copy.8
  (12 shorter events, 0.1 us)
Async XLA Ops:
  1.6 1.9 %copy-start = (bf16[1,2,160,5120]{3,2,1,0:T(8,128)(2,1)S(1)}, bf16[1,2,160,5120]{3,2,1,0:T(8,128)(2,1)}, u32[]{:S(2)}) copy-start(bf16[1,2,160,5120]{3,2,1,0:T(8,128)(2,1)} %grads_ref.3) | copy-start | bytes 9830404
  3.5 1.9 %copy-start.2 = (bf16[1,2,160,5120]{3,2,1,0:T(8,128)(2,1)S(1)}, bf16[1,2,160,5120]{3,2,1,0:T(8,128)(2,1)}, u32[]{:S(2)}) copy-start(bf16[1,2,160,5120]{3,2,1,0:T(8,128)(2,1)} %errors_ref.3) | copy-start | bytes 9830404
  5.4 1.9 %copy-start.1 = (bf16[1,2,160,5120]{3,2,1,0:T(8,128)(2,1)S(1)}, bf16[1,2,160,5120]{3,2,1,0:T(8,128)(2,1)}, u32[]{:S(2)}) copy-start(bf16[1,2,160,5120]{3,2,1,0:T(8,128)(2,1)} %grads_ref.3) | copy-start | bytes 9830404
  6.7 2.2 %collective-permute-start = (f32[32,8,640]{2,1,0:T(8,128)S(1)}, f32[32,8,640]{2,1,0:T(8,128)S(1)}, u32[]{:S(2)}, u32[]{:S(2)}) collective-permute-start(f32[32,8,640]{2,1,0:T(8,128)S(1)} %get-tuple-element.14), channel_id=1, source_target_pairs={{0,1},{1,0},{2,3},{3,2},{4,5},{5,4},{6,7},{7,6},{8,9},{9,8},{10,11... | collective-permute-start | bytes 1966088 | tf_op jit(solution)/shard_map/left_core_swap/ppermute | solution.py:60
  30.9 7.9 %collective-permute-start.3 = (f32[8,640]{1,0:T(8,128)S(1)}, f32[8,640]{1,0:T(8,128)S(1)}, u32[]{:S(2)}, u32[]{:S(2)}) collective-permute-start(f32[8,640]{1,0:T(8,128)S(1)} %reduce_sum.9), channel_id=1, source_target_pairs={{0,12},{1,13},{2,14},{3,15},{4,8},{5,9},{6,10},{7,11},{8,4},{9,5},... | collective-permute-start | bytes 61448 | tf_op jit(solution)/shard_map/left_sum/ppermute | solution.py:60
  36.4 7.7 %collective-permute-start.2 = (f32[8,640]{1,0:T(8,128)S(1)}, f32[8,640]{1,0:T(8,128)S(1)}, u32[]{:S(2)}, u32[]{:S(2)}) collective-permute-start(f32[8,640]{1,0:T(8,128)S(1)} %reduce_sum.9), channel_id=1, source_target_pairs={{0,8},{1,9},{2,10},{3,11},{4,12},{5,13},{6,14},{7,15},{8,0},{9,1},... | collective-permute-start | bytes 61448 | tf_op jit(solution)/shard_map/left_sum/ppermute | solution.py:60
  37.8 6.3 %collective-permute-start.1 = (f32[8,640]{1,0:T(8,128)S(1)}, f32[8,640]{1,0:T(8,128)S(1)}, u32[]{:S(2)}, u32[]{:S(2)}) collective-permute-start(f32[8,640]{1,0:T(8,128)S(1)} %reduce_sum.9), channel_id=1, source_target_pairs={{0,4},{1,5},{2,6},{3,7},{4,0},{5,1},{6,2},{7,3},{8,12},{9,13},{10,... | collective-permute-start | bytes 61448 | tf_op jit(solution)/shard_map/left_sum/ppermute | solution.py:60
  59.3 2.1 %collective-permute-start.4 = (f32[32,8,640]{2,1,0:T(8,128)S(1)}, f32[32,8,640]{2,1,0:T(8,128)S(1)}, u32[]{:S(2)}, u32[]{:S(2)}) collective-permute-start(f32[32,8,640]{2,1,0:T(8,128)S(1)} %all_to_all.11.left_ref), channel_id=1, source_target_pairs={{0,1},{1,0},{2,3},{3,2},{4,5},{5,4},{6,7},{7,6},{8,9},{9,8},{10,11... | collective-permute-start | bytes 1966088 | tf_op jit(solution)/shard_map/left_sum/ppermute | solution.py:60
  62.5 4.2 %collective-permute-start.7 = (f32[80,128]{1,0:T(8,128)S(1)}, f32[80,128]{1,0:T(8,128)S(1)}, u32[]{:S(2)}, u32[]{:S(2)}) collective-permute-start(f32[80,128]{1,0:T(8,128)S(1)} %get-tuple-element.19), channel_id=1, source_target_pairs={{0,48},{1,193},{2,50},{3,195},{4,52},{5,197},{6,54},{7,199},{8,56}... | collective-permute-start | bytes 122888 | tf_op jit(solution)/shard_map/right_sum/ppermute | solution.py:60
  63.8 5.5 %collective-permute-start.6 = (f32[80,128]{1,0:T(8,128)S(1)}, f32[80,128]{1,0:T(8,128)S(1)}, u32[]{:S(2)}, u32[]{:S(2)}) collective-permute-start(f32[80,128]{1,0:T(8,128)S(1)} %get-tuple-element.19), channel_id=1, source_target_pairs={{0,32},{1,129},{2,34},{3,131},{4,36},{5,133},{6,38},{7,135},{8,40}... | collective-permute-start | bytes 122888 | tf_op jit(solution)/shard_map/right_sum/ppermute | solution.py:60
  66.2 4.0 %collective-permute-start.5 = (f32[80,128]{1,0:T(8,128)S(1)}, f32[80,128]{1,0:T(8,128)S(1)}, u32[]{:S(2)}, u32[]{:S(2)}) collective-permute-start(f32[80,128]{1,0:T(8,128)S(1)} %get-tuple-element.19), channel_id=1, source_target_pairs={{0,16},{1,65},{2,18},{3,67},{4,20},{5,69},{6,22},{7,71},{8,24},{9,... | collective-permute-start | bytes 122888 | tf_op jit(solution)/shard_map/right_sum/ppermute | solution.py:60
  70.2 7.0 %collective-permute-start.10 = (f32[80,128]{1,0:T(8,128)S(1)}, f32[80,128]{1,0:T(8,128)S(1)}, u32[]{:S(2)}, u32[]{:S(2)}) collective-permute-start(f32[80,128]{1,0:T(8,128)S(1)} %add_add_fusion.t0_ref), channel_id=1, source_target_pairs={{0,192},{1,49},{2,194},{3,51},{4,196},{5,53},{6,198},{7,55},{8,200... | collective-permute-start | bytes 122888 | tf_op jit(solution)/shard_map/right_sum/ppermute | solution.py:60
  72.2 5.5 %collective-permute-start.9 = (f32[80,128]{1,0:T(8,128)S(1)}, f32[80,128]{1,0:T(8,128)S(1)}, u32[]{:S(2)}, u32[]{:S(2)}) collective-permute-start(f32[80,128]{1,0:T(8,128)S(1)} %add_add_fusion.t0_ref), channel_id=1, source_target_pairs={{0,128},{1,33},{2,130},{3,35},{4,132},{5,37},{6,134},{7,39},{8,136... | collective-permute-start | bytes 122888 | tf_op jit(solution)/shard_map/right_sum/ppermute | solution.py:60
  73.0 4.7 %collective-permute-start.8 = (f32[80,128]{1,0:T(8,128)S(1)}, f32[80,128]{1,0:T(8,128)S(1)}, u32[]{:S(2)}, u32[]{:S(2)}) collective-permute-start(f32[80,128]{1,0:T(8,128)S(1)} %add_add_fusion.t0_ref), channel_id=1, source_target_pairs={{0,64},{1,17},{2,66},{3,19},{4,68},{5,21},{6,70},{7,23},{8,72},{9,... | collective-permute-start | bytes 122888 | tf_op jit(solution)/shard_map/right_sum/ppermute | solution.py:60

commit v2 on v1

v2 whole, which is shorter than its diff:
```python
import functools

import jax
import jax.numpy as jnp
from jax import lax
from jax.experimental import pallas as pl
from jax.experimental.pallas import tpu as pltpu
from jax.sharding import PartitionSpec as P

D = 5120
ROWS = 160
RANK = 32
HOSTS = 16
CHUNKS = 32
CHUNK_COLS = 640
COL_BLOCKS = D // CHUNK_COLS
AXES = ("dp", "tp")
MIB = 1 << 20


def device(x, y, z, c):
    return (y * 4 + x) * 16 + z * 2 + c


def everyone():
    return [(x, y, z, c) for y in range(4) for x in range(4) for z in range(8) for c in range(2)]


def pairs(move):
    return [(device(*at), device(*move(*at))) for at in everyone()]


CORE_SWAP = pairs(lambda x, y, z, c: (x, y, z, 1 - c))


def z_pairs(k):
    return pairs(lambda x, y, z, c: (x, y, z ^ (2 * k), c))


def first_pairs(k):
    return pairs(lambda x, y, z, c: (x ^ k, y, z, c) if c == 0 else (x, y ^ k, z, c))


def second_pairs(k):
    return pairs(lambda x, y, z, c: (x, y ^ k, z, c) if c == 0 else (x ^ k, y, z, c))


GROUPS = [
    [device(x, y, zz * 2 + k, c) for k in range(2) for y in range(4) for x in range(4)]
    for zz in range(4)
    for c in range(2)
]


def exchange(parts):
    return lax.all_to_all(parts, AXES, 0, 0, axis_index_groups=GROUPS, tiled=True)


def permute(a, perm):
    return lax.ppermute(a, AXES, perm)


def split3(a):
    hi = a.astype(jnp.bfloat16)
    rest = a - hi.astype(jnp.float32)
    mid = rest.astype(jnp.bfloat16)
    lo = (rest - mid.astype(jnp.float32)).astype(jnp.bfloat16)
    return hi, mid, lo


def cost(flops, nbytes):
    return pl.CostEstimate(flops=flops, bytes_accessed=nbytes, transcendentals=0)


def vmem(n):
    return [pl.BlockSpec(memory_space=pltpu.VMEM)] * n


def left_kernel(m_ref, grads_ref, errors_ref, basis_ref, corrected_ref, left_ref, *scratch):
    grads_at, errors_at, basis_at, sems, basis_sem = scratch
    m = m_ref[0]
    basis_copy = pltpu.make_async_copy(basis_ref.at[m], basis_at, basis_sem)
    basis_copy.start()
    copies = []
    for b in range(COL_BLOCKS):
        cols = pl.ds(b * CHUNK_COLS, CHUNK_COLS)
        pair = (
            pltpu.make_async_copy(grads_ref.at[0, m, :, cols], grads_at.at[b], sems.at[b, 0]),
            pltpu.make_async_copy(errors_ref.at[0, m, :, cols], errors_at.at[b], sems.at[b, 1]),
        )
        for copy in pair:
            copy.start()
        copies.append(pair)
    basis_copy.wait()
    basis = basis_at[...].astype(jnp.bfloat16)
    for b in range(COL_BLOCKS):
        for copy in copies[b]:
            copy.wait()
        corrected = (
            grads_at[b].astype(jnp.float32) + errors_at[b].astype(jnp.float32)
        ).astype(jnp.bfloat16)
        corrected_ref[:, b * CHUNK_COLS : (b + 1) * CHUNK_COLS] = corrected
        left = jnp.dot(basis, corrected, preferred_element_type=jnp.float32)
        for g in range(4):
            left_ref[b * 4 + g] = left[8 * g : 8 * g + 8]


def left_part(m, grads, errors, basis):
    return pl.pallas_call(
        left_kernel,
        in_specs=[
            pl.BlockSpec(memory_space=pltpu.SMEM),
        ]
        + [pl.BlockSpec(memory_space=pltpu.HBM)] * 3,
        out_specs=vmem(2),
        out_shape=[
            jax.ShapeDtypeStruct((ROWS, D), jnp.bfloat16),
            jax.ShapeDtypeStruct((CHUNKS, 8, CHUNK_COLS), jnp.float32),
        ],
        scratch_shapes=[
            pltpu.VMEM((COL_BLOCKS, ROWS, CHUNK_COLS), jnp.bfloat16),
            pltpu.VMEM((COL_BLOCKS, ROWS, CHUNK_COLS), jnp.bfloat16),
            pltpu.VMEM((RANK, ROWS), jnp.float32),
            pltpu.SemaphoreType.DMA((COL_BLOCKS, 2)),
            pltpu.SemaphoreType.DMA(()),
        ],
        compiler_params=pltpu.CompilerParams(vmem_limit_bytes=16 * MIB),
        cost_estimate=cost(2 * ROWS * D * RANK, 6 * ROWS * D + 4 * RANK * D),
        name="left",
    )(m, grads, errors, basis)


def add_up_kernel(parts_ref, sum_ref):
    parts = [parts_ref[k] for k in range(CHUNKS)]
    while len(parts) > 1:
        parts = [parts[k] + parts[k + 1] for k in range(0, len(parts), 2)]
    sum_ref[...] = parts[0]


def add_up(parts):
    return pl.pallas_call(
        add_up_kernel,
        in_specs=vmem(1),
        out_specs=pl.BlockSpec(memory_space=pltpu.VMEM),
        out_shape=jax.ShapeDtypeStruct((8, CHUNK_COLS), jnp.float32),
        compiler_params=pltpu.CompilerParams(vmem_limit_bytes=4 * MIB),
        cost_estimate=cost(CHUNKS * 8 * CHUNK_COLS, 4 * CHUNKS * 8 * CHUNK_COLS),
        name="add_up",
    )(parts)


def right_body(left_ref, corrected_ref, terms_ref, stack_ref):
    for b in range(COL_BLOCKS):
        cols = slice(b * CHUNK_COLS, (b + 1) * CHUNK_COLS)
        for g in range(4):
            rows = slice(8 * g, 8 * g + 8)
            stack_ref[rows, cols] = left_ref[b * 4 + g]
    for b in range(COL_BLOCKS):
        cols = slice(b * CHUNK_COLS, (b + 1) * CHUNK_COLS)
        hi, mid, lo = split3(stack_ref[:, cols])
        for i, term in enumerate((hi, mid, lo, hi, mid, hi)):
            terms_ref[i * RANK : (i + 1) * RANK, cols] = term
    terms = terms_ref[0 : 3 * RANK, :]
    nt = (((1,), (1,)), ((), ()))
    t = lax.dot_general(corrected_ref[...], terms, nt, preferred_element_type=jnp.float32)
    t = t[:, 0:RANK] + (t[:, RANK : 2 * RANK] + t[:, 2 * RANK : 3 * RANK])
    packed = jnp.concatenate([t[40 * i : 40 * i + 40] for i in range(4)], axis=1)
    g = lax.dot_general(terms, terms, nt, preferred_element_type=jnp.float32)
    gram = g[0:RANK, 0:RANK]
    rest = jnp.zeros_like(gram)
    for i in range(3):
        for j in range(3):
            if i + j > 0:
                rest = rest + g[i * RANK : (i + 1) * RANK, j * RANK : (j + 1) * RANK]
    return packed, gram + rest


def right_kernel(left_ref, corrected_ref, t_ref, gram_ref, terms_ref, stack_ref):
    t_ref[...], gram_ref[...] = right_body(left_ref, corrected_ref, terms_ref, stack_ref)


def right_both_kernel(
    left_ref, corrected_ref, t_own_ref, gram_own_ref, t_ref, gram_ref, terms_ref, stack_ref
):
    t, gram = right_body(left_ref, corrected_ref, terms_ref, stack_ref)
    t_ref[0:40] = t_own_ref[...]
    t_ref[40:80] = t
    gram_ref[0] = gram_own_ref[...]
    gram_ref[1] = gram


def right_part(left, corrected, own=None):
    both = own is not None
    n = 2 if both else 1
    return pl.pallas_call(
        right_both_kernel if both else right_kernel,
        in_specs=vmem(4 if both else 2),
        out_specs=vmem(3),
        out_shape=[
            jax.ShapeDtypeStruct((40 * n, 128), jnp.float32),
            jax.ShapeDtypeStruct((2, RANK, RANK) if both else (RANK, RANK), jnp.float32),
            jax.ShapeDtypeStruct((6 * RANK, D), jnp.bfloat16),
        ],
        scratch_shapes=[pltpu.VMEM((RANK, D), jnp.float32)],
        compiler_params=pltpu.CompilerParams(vmem_limit_bytes=24 * MIB),
        cost_estimate=cost(2 * 256 * D * 96, 2 * ROWS * D + 16 * RANK * D),
        name="right",
    )(left, corrected, *(own or ()))


def inverse_kernel(gram_ref, inverse_ref):
    row = lax.broadcasted_iota(jnp.int32, (RANK, RANK), 0)
    col = lax.broadcasted_iota(jnp.int32, (RANK, RANK), 1)
    eye = jnp.where(row == col, 1.0, 0.0).astype(jnp.float32)
    a = jnp.concatenate([gram_ref[0], eye, gram_ref[1], eye], axis=1)
    rows = lax.broadcasted_iota(jnp.int32, a.shape, 0)
    first = lax.broadcasted_iota(jnp.int32, a.shape, 1) < 2 * RANK
    for base in range(0, RANK, 4):
        below, across = [], []
        for k in range(base, base + 4):
            left = jnp.broadcast_to(a[:, k : k + 1], a.shape)
            right = jnp.broadcast_to(a[:, 2 * RANK + k : 2 * RANK + k + 1], a.shape)
            below.append(jnp.where(first, left, right))
            across.append(a[k : k + 1, :])
        done = a
        for p in range(4):
            k = base + p
            scale = lax.rsqrt(below[p][k : k + 1, :])
            below[p] = below[p] * scale
            across[p] = across[p] * scale
            for q in range(p + 1, 4):
                factor = below[p][base + q : base + q + 1, :]
                below[q] = below[q] - below[p] * factor
                across[q] = across[q] - factor * across[p]
            a = a - below[p] * across[p]
            done = jnp.where(rows == k, across[p], done)
        a = jnp.where(rows >= base + 4, a, done)
    inverse_ref[0] = a[:, RANK : 2 * RANK]
    inverse_ref[1] = a[:, 3 * RANK : 4 * RANK]


def inverses(gram):
    return pl.pallas_call(
        inverse_kernel,
        in_specs=vmem(1),
        out_specs=pl.BlockSpec(memory_space=pltpu.VMEM),
        out_shape=jax.ShapeDtypeStruct((2, RANK, RANK), jnp.float32),
        compiler_params=pltpu.CompilerParams(vmem_limit_bytes=4 * MIB),
        cost_estimate=cost(10_000_000, 8_000_000),
        name="inverse",
    )(gram)


def final_kernel(
    core_ref,
    t0_ref,
    t1_ref,
    t2_ref,
    t3_ref,
    inverse_ref,
    terms_own_ref,
    terms_other_ref,
    corrected_own_ref,
    corrected_other_ref,
    update_ref,
    errors_ref,
    right_ref,
    update_at,
    errors_at,
    sems,
):
    high = functools.partial(
        lax.dot_general, precision=lax.Precision.HIGHEST, preferred_element_type=jnp.float32
    )
    nt = (((1,), (1,)), ((), ()))
    nn = (((1,), (0,)), ((), ()))
    core = core_ref[0]
    t = (t0_ref[...] + t1_ref[...]) + (t2_ref[...] + t3_ref[...])
    t = t * (1.0 / HOSTS)
    copies = []
    for n in range(2):
        m = core if n == 0 else 1 - core
        terms_ref = (terms_own_ref, terms_other_ref)[n]
        corrected_ref = (corrected_own_ref, corrected_other_ref)[n]
        mine = t[40 * n : 40 * n + 40]
        mine = jnp.concatenate([mine[:, RANK * q : RANK * q + RANK] for q in range(4)], axis=0)
        inverse = inverse_ref[n]
        right_ref[m] = high(inverse, mine, nt)
        hi, mid, lo = split3(high(high(mine, inverse, nt), inverse, nn))
        w = jnp.concatenate([hi, hi, hi, mid, mid, lo], axis=1)
        for b in range(COL_BLOCKS):
            cols = slice(b * CHUNK_COLS, (b + 1) * CHUNK_COLS)
            recon = jnp.dot(w, terms_ref[:, cols], preferred_element_type=jnp.float32)
            update_at[n, b] = recon.astype(jnp.bfloat16)
            errors_at[n, b] = (corrected_ref[:, cols].astype(jnp.float32) - recon).astype(
                jnp.bfloat16
            )
            there = pl.ds(b * CHUNK_COLS, CHUNK_COLS)
            pair = (
                pltpu.make_async_copy(
                    update_at.at[n, b], update_ref.at[m, :, there], sems.at[n, b, 0]
                ),
                pltpu.make_async_copy(
                    errors_at.at[n, b], errors_ref.at[0, m, :, there], sems.at[n, b, 1]
                ),
            )
            for copy in pair:
                copy.start()
            copies.extend(pair)
    for copy in copies:
        copy.wait()


def final_part(core, ts, inverse, terms_own, terms_other, corrected_own, corrected_other):
    hbm = pl.BlockSpec(memory_space=pltpu.HBM)
    return pl.pallas_call(
        final_kernel,
        in_specs=[pl.BlockSpec(memory_space=pltpu.SMEM)] + vmem(9),
        out_specs=[hbm, hbm, pl.BlockSpec(memory_space=pltpu.VMEM)],
        out_shape=[
            jax.ShapeDtypeStruct((2, ROWS, D), jnp.bfloat16),
            jax.ShapeDtypeStruct((1, 2, ROWS, D), jnp.bfloat16),
            jax.ShapeDtypeStruct((2, RANK, ROWS), jnp.float32),
        ],
        scratch_shapes=[
            pltpu.VMEM((2, COL_BLOCKS, ROWS, CHUNK_COLS), jnp.bfloat16),
            pltpu.VMEM((2, COL_BLOCKS, ROWS, CHUNK_COLS), jnp.bfloat16),
            pltpu.SemaphoreType.DMA((2, COL_BLOCKS, 2)),
        ],
        compiler_params=pltpu.CompilerParams(vmem_limit_bytes=24 * MIB),
        cost_estimate=cost(2 * 2 * ROWS * 192 * D, 16 * ROWS * D),
        name="final",
    )(core, *ts, inverse, terms_own, terms_other, corrected_own, corrected_other)


def on_device(grads, errors, basis_in):
    core = lax.rem(lax.axis_index("tp"), 2).astype(jnp.int32)
    grads, errors, basis = (
        pltpu.with_memory_space_constraint(a, pltpu.HBM)
        for a in (grads, errors, jnp.swapaxes(basis_in, 1, 2))
    )
    corrected_other, left_other = left_part((1 - core)[None], grads, errors, basis)
    with jax.named_scope("left_core_swap"):
        arrived = permute(left_other, CORE_SWAP)
    corrected_own, left_own = left_part(core[None], grads, errors, basis)
    with jax.named_scope("left_sum"):
        parts = exchange(left_own + arrived)
        part = add_up(parts)
        p1, p3, p2 = (permute(part, z_pairs(k)) for k in (1, 3, 2))
        part = (part + p1) + (p2 + p3)
        left_own = exchange(jnp.broadcast_to(part[None], (CHUNKS,) + part.shape))
        left_other = permute(left_own, CORE_SWAP)
    t_own, gram_own, terms_own = right_part(left_own, corrected_own)
    t, gram, terms_other = right_part(left_other, corrected_other, (t_own, gram_own))
    with jax.named_scope("right_sum"):
        t1, t3, t2 = (permute(t, first_pairs(k)) for k in (1, 3, 2))
        t = (t + t1) + (t2 + t3)
        t1, t3, t2 = (permute(t, second_pairs(k)) for k in (1, 3, 2))
    inverse = inverses(gram)
    update, new_errors, right = final_part(
        core[None], (t, t1, t2, t3), inverse, terms_own, terms_other, corrected_own, corrected_other
    )
    return update, new_errors, jnp.swapaxes(right, 1, 2)


def solution(mesh):
    return jax.shard_map(
        on_device,
        mesh=mesh,
        in_specs=(P("dp", None, "tp", None), P("dp", None, "tp", None), P(None, "tp", None)),
        out_specs=(P(None, "tp", None), P("dp", None, "tp", None), P(None, "tp", None)),
        check_vma=False,
    )
```

time: 85.8 us -> 80.6 us (0.939)
  local copies, waits for them, and re-layouts: 6.13 us -> 0.04 us
  waiting for transfers between devices: 10.5 us -> 11.9 us
  other arithmetic: 1.33 us -> 0.09 us
    unnamed x7 -> x0, local copies, waits for them, and re-layouts: 5.34 us -> none
    pallas_call x3 -> x4, Pallas kernels: 9.56 us -> 11.5 us  [the longest x2 6.83 us: left_part(): pl.pallas_call(left_kernel, in_specs=[pl.BlockSpec(memory_space=pltpu.SME...]
    pallas_call x1, Pallas kernels: 2.76 us -> 1.18 us  [inverses(): pl.pallas_call(inverse_kernel, in_specs=vmem(1), out_specs=pl.BlockSpec(m...]
    ppermute x11, waiting for transfers between devices: 10.5 us -> 11.9 us  [permute(): return lax.ppermute(a, AXES, perm)]
    reduce_sum x1 -> x0, other arithmetic: 1.14 us -> none  [on_device(): part = jnp.sum(parts, axis=0)]
  transfers between devices with their start and end apart: 11 -> 11, of which waited for: 6 -> 5; matrix products, arithmetic and copies ran while one was open for 0% -> 0% of each run, Pallas kernels for 6% -> 7%
where the time goes in v2:
time: 80.6 us; the launch traced here: 80.4 us
  blocking collectives  36.3 us (45%)
  starting transfers between devices  16.4 us (20%)
  Pallas kernels  14.8 us (18%)
  waiting for transfers between devices  11.9 us (15%)
  between operations  0.87 us (1%)
    all_to_all x2, blocking collectives, exchange(): lax.all_to_all(parts, AXES, 0, 0, axis_index_groups=GROUPS, tiled=True)  36.3 us
    ppermute x11, starting transfers between devices, permute(): return lax.ppermute(a, AXES, perm)  16.4 us
    ppermute x11, waiting for transfers between devices, permute(): return lax.ppermute(a, AXES, perm)  11.9 us
    pallas_call x2, Pallas kernels, left_part(): pl.pallas_call(left_kernel, in_specs=[pl.BlockSpec(memory_space=pltpu.SME...  6.83 us
    pallas_call x1, Pallas kernels, final_part(): pl.pallas_call(final_kernel, in_specs=[pl.BlockSpec(memory_space=pltpu.SM...  4.63 us
    pallas_call x2, Pallas kernels, right_part(): pl.pallas_call(right_both_kernel if both else right_kernel, in_specs=vmem...  2.15 us
  transfers between devices with their start and end apart: 11, of which 5 were waited for; matrix products, arithmetic and copies ran while one was open for 0% of the time, Pallas kernels for 7%

profile of v2, /device:TPU:2, one launch (start us, length us, event | category | flops | bytes accessed | tf_op | source)
XLA Modules:
  0.0 80.4 jit_solution(13384738084621469473)
XLA Ops:
  0.6 3.4 %left.3 = (bf16[160,5120]{1,0:T(8,128)(2,1)S(1)}, f32[32,8,640]{2,1,0:T(8,128)S(1)}) custom-call(s32[1]{0:T(128)} %bitcast.2.m_ref, bf16[1,2,160,5120]{3,2,1,0:T(8,128)(2,1)} %grads_ref.3, bf16[1,2,160,5120]{3,2,1,0:T(8,128)(2,1)} %errors_ref.3, f32[2,32,160]{2,1,0:T(8,128)} %bitcast.4), custom_call_target="tpu_custom_call" | custom-call | flops 52428800 | bytes 5570560 | tf_op jit(solution)/shard_map/left/pallas_call | solution.py:109
  4.1 0.1 collective-permute-start
  4.2 3.4 %left.2 = (bf16[160,5120]{1,0:T(8,128)(2,1)S(1)}, f32[32,8,640]{2,1,0:T(8,128)S(1)}) custom-call(s32[1]{0:T(128)} %bitcast.m_ref.core_ref, bf16[1,2,160,5120]{3,2,1,0:T(8,128)(2,1)} %grads_ref.3, bf16[1,2,160,5120]{3,2,1,0:T(8,128)(2,1)} %errors_ref.3, f32[2,32,160]{2,1,0:T(8,128)} %bitcast.5), custom_call_target="tpu_custom_call" | custom-call | flops 52428800 | bytes 5570560 | tf_op jit(solution)/shard_map/left/pallas_call | solution.py:109
  7.6 0.0 collective-permute-done
  7.6 0.1 add.21
  7.7 21.0 %all_to_all.10.parts_ref = f32[32,8,640]{2,1,0:T(8,128)S(1)} all-to-all(f32[32,8,640]{2,1,0:T(8,128)S(1)} %add.21), channel_id=1, replica_groups={{0,16,32,48,64,80,96,112,128,144,160,176,192,208,224,240,2,18,34,50,66,..., dimensions={0} | all-to-all | bytes 1310720 | tf_op jit(solution)/shard_map/left_sum/all_to_all | solution.py:56
  28.7 5.5 %collective-permute-start.3 = (f32[8,640]{1,0:T(8,128)S(1)}, f32[8,640]{1,0:T(8,128)S(1)}, u32[]{:S(2)}, u32[]{:S(2)}) collective-permute-start(f32[8,640]{1,0:T(8,128)S(1)} %add_up.1), channel_id=1, source_target_pairs={{0,12},{1,13},{2,14},{3,15},{4,8},{5,9},{6,10},{7,11},{8,4},{9,5},... | collective-permute-start | bytes 61448 | tf_op jit(solution)/shard_map/left_sum/ppermute | solution.py:60
  34.2 1.4 %collective-permute-start.2 = (f32[8,640]{1,0:T(8,128)S(1)}, f32[8,640]{1,0:T(8,128)S(1)}, u32[]{:S(2)}, u32[]{:S(2)}) collective-permute-start(f32[8,640]{1,0:T(8,128)S(1)} %add_up.1), channel_id=1, source_target_pairs={{0,8},{1,9},{2,10},{3,11},{4,12},{5,13},{6,14},{7,15},{8,0},{9,1},... | collective-permute-start | bytes 61448 | tf_op jit(solution)/shard_map/left_sum/ppermute | solution.py:60
  35.6 1.0 %collective-permute-start.1 = (f32[8,640]{1,0:T(8,128)S(1)}, f32[8,640]{1,0:T(8,128)S(1)}, u32[]{:S(2)}, u32[]{:S(2)}) collective-permute-start(f32[8,640]{1,0:T(8,128)S(1)} %add_up.1), channel_id=1, source_target_pairs={{0,4},{1,5},{2,6},{3,7},{4,0},{5,1},{6,2},{7,3},{8,12},{9,13},{10,... | collective-permute-start | bytes 61448 | tf_op jit(solution)/shard_map/left_sum/ppermute | solution.py:60
  36.7 0.0 collective-permute-done.3
  36.7 5.2 %collective-permute-done.2 = f32[8,640]{1,0:T(8,128)S(1)} collective-permute-done((f32[8,640]{1,0:T(8,128)S(1)}, f32[8,640]{1,0:T(8,128)S(1)}, u32[]{:S(2)}, u32[]{:S(2)}) %collective-permute-start.2) | collective-permute-done | bytes 20512 | tf_op jit(solution)/shard_map/left_sum/ppermute | solution.py:60
  41.9 0.0 collective-permute-done.1
  42.0 15.3 %all_to_all.11.left_ref = f32[32,8,640]{2,1,0:T(8,128)S(1)} all-to-all(f32[32,8,640]{2,1,0:T(8,128)S(1)} %broadcast_in_dim.15), channel_id=1, replica_groups={{0,16,32,48,64,80,96,112,128,144,160,176,192,208,224,240,2,18,34,50,66,..., dimensions={0} | all-to-all | bytes 1310720 | tf_op jit(solution)/shard_map/left_sum/all_to_all | solution.py:56
  57.2 0.0 collective-permute-start.4
  57.2 1.1 %right.2 = (f32[40,128]{1,0:T(8,128)S(1)}, f32[32,32]{1,0:T(8,128)S(1)}, bf16[192,5120]{1,0:T(8,128)(2,1)S(1)}) custom-call(f32[32,8,640]{2,1,0:T(8,128)S(1)} %all_to_all.11.left_ref, bf16[160,5120]{1,0:T(8,128)(2,1)S(1)} %get-tuple-element.19.corrected_ref.corrected_own_ref), custom_call_target="tpu_custom_call" | custom-call | flops 251658240 | bytes 4259840 | tf_op jit(solution)/shard_map/right/pallas_call | solution.py:195
  58.3 1.0 %collective-permute-done.4.left_ref = f32[32,8,640]{2,1,0:T(8,128)S(1)} collective-permute-done((f32[32,8,640]{2,1,0:T(8,128)S(1)}, f32[32,8,640]{2,1,0:T(8,128)S(1)}, u32[]{:S(2)}, u32[]{:S(2)}) %collective-permute-start.4) | collective-permute-done | bytes 655392 | tf_op jit(solution)/shard_map/left_sum/ppermute | solution.py:60
  59.3 1.1 %right.3 = (f32[80,128]{1,0:T(8,128)S(1)}, f32[2,32,32]{2,1,0:T(8,128)S(1)}, bf16[192,5120]{1,0:T(8,128)(2,1)S(1)}) custom-call(f32[32,8,640]{2,1,0:T(8,128)S(1)} %collective-permute-done.4.left_ref, bf16[160,5120]{1,0:T(8,128)(2,1)S(1)} %get-tuple-element.18.corrected_ref.corrected_other_ref, f32[40,128]{1,0:T(8,128)S(1)} %get-tuple-element.20.t_own_ref, ...), custom_call_target="tpu_custom_call" | custom-call | flops 251658240 | bytes 4259840 | tf_op jit(solution)/shard_map/right/pallas_call | solution.py:195
  60.4 1.3 %collective-permute-start.7 = (f32[80,128]{1,0:T(8,128)S(1)}, f32[80,128]{1,0:T(8,128)S(1)}, u32[]{:S(2)}, u32[]{:S(2)}) collective-permute-start(f32[80,128]{1,0:T(8,128)S(1)} %get-tuple-element.22), channel_id=1, source_target_pairs={{0,48},{1,193},{2,50},{3,195},{4,52},{5,197},{6,54},{7,199},{8,56}... | collective-permute-start | bytes 122888 | tf_op jit(solution)/shard_map/right_sum/ppermute | solution.py:60
  61.7 2.4 %collective-permute-start.6 = (f32[80,128]{1,0:T(8,128)S(1)}, f32[80,128]{1,0:T(8,128)S(1)}, u32[]{:S(2)}, u32[]{:S(2)}) collective-permute-start(f32[80,128]{1,0:T(8,128)S(1)} %get-tuple-element.22), channel_id=1, source_target_pairs={{0,32},{1,129},{2,34},{3,131},{4,36},{5,133},{6,38},{7,135},{8,40}... | collective-permute-start | bytes 122888 | tf_op jit(solution)/shard_map/right_sum/ppermute | solution.py:60
  64.1 0.5 collective-permute-start.5
  64.6 0.0 collective-permute-done.7
  64.6 2.6 %collective-permute-done.6 = f32[80,128]{1,0:T(8,128)S(1)} collective-permute-done((f32[80,128]{1,0:T(8,128)S(1)}, f32[80,128]{1,0:T(8,128)S(1)}, u32[]{:S(2)}, u32[]{:S(2)}) %collective-permute-start.6) | collective-permute-done | bytes 40992 | tf_op jit(solution)/shard_map/right_sum/ppermute | solution.py:60
  67.2 0.9 %collective-permute-done.5 = f32[80,128]{1,0:T(8,128)S(1)} collective-permute-done((f32[80,128]{1,0:T(8,128)S(1)}, f32[80,128]{1,0:T(8,128)S(1)}, u32[]{:S(2)}, u32[]{:S(2)}) %collective-permute-start.5) | collective-permute-done | bytes 40992 | tf_op jit(solution)/shard_map/right_sum/ppermute | solution.py:60
  68.1 2.0 %collective-permute-start.10 = (f32[80,128]{1,0:T(8,128)S(1)}, f32[80,128]{1,0:T(8,128)S(1)}, u32[]{:S(2)}, u32[]{:S(2)}) collective-permute-start(f32[80,128]{1,0:T(8,128)S(1)} %add_add_fusion.t0_ref), channel_id=1, source_target_pairs={{0,192},{1,49},{2,194},{3,51},{4,196},{5,53},{6,198},{7,55},{8,200... | collective-permute-start | bytes 122888 | tf_op jit(solution)/shard_map/right_sum/ppermute | solution.py:60
  70.1 0.8 collective-permute-start.9
  70.9 1.4 %collective-permute-start.8 = (f32[80,128]{1,0:T(8,128)S(1)}, f32[80,128]{1,0:T(8,128)S(1)}, u32[]{:S(2)}, u32[]{:S(2)}) collective-permute-start(f32[80,128]{1,0:T(8,128)S(1)} %add_add_fusion.t0_ref), channel_id=1, source_target_pairs={{0,64},{1,17},{2,66},{3,19},{4,68},{5,21},{6,70},{7,23},{8,72},{9,... | collective-permute-start | bytes 122888 | tf_op jit(solution)/shard_map/right_sum/ppermute | solution.py:60
  72.3 1.2 %inverse.1.inverse_ref = f32[2,32,32]{2,1,0:T(8,128)S(1)} custom-call(f32[2,32,32]{2,1,0:T(8,128)S(1)} %get-tuple-element.23.gram_ref), custom_call_target="tpu_custom_call" | custom-call | flops 10000000 | bytes 8000000 | tf_op jit(solution)/shard_map/inverse/pallas_call | solution.py:243
  73.5 0.0 collective-permute-done.10.t3_ref
  73.5 2.1 %collective-permute-done.9.t2_ref = f32[80,128]{1,0:T(8,128)S(1)} collective-permute-done((f32[80,128]{1,0:T(8,128)S(1)}, f32[80,128]{1,0:T(8,128)S(1)}, u32[]{:S(2)}, u32[]{:S(2)}) %collective-permute-start.9) | collective-permute-done | bytes 40992 | tf_op jit(solution)/shard_map/right_sum/ppermute | solution.py:60
  75.6 0.0 collective-permute-done.8.t1_ref
  75.6 4.6 %final.1 = (bf16[2,160,5120]{2,1,0:T(8,128)(2,1)}, bf16[1,2,160,5120]{3,2,1,0:T(8,128)(2,1)}, f32[2,32,160]{2,1,0:T(8,128)}) custom-call(s32[1]{0:T(128)} %bitcast.m_ref.core_ref, f32[80,128]{1,0:T(8,128)S(1)} %add_add_fusion.t0_ref, f32[80,128]{1,0:T(8,128)S(1)} %collective-permute-done.8.t1_ref, f32[80,128]{1,0:T(8,128)S(1)} %collective-permute-done.9.t2_ref, ...), custom_call_target="tpu_custom_call" | custom-call | flops 629145600 | bytes 13107200 | tf_op jit(solution)/shard_map/final/pallas_call | solution.py:316
  (4 shorter events, 0.1 us)
Async XLA Ops:
  4.1 3.5 %collective-permute-start = (f32[32,8,640]{2,1,0:T(8,128)S(1)}, f32[32,8,640]{2,1,0:T(8,128)S(1)}, u32[]{:S(2)}, u32[]{:S(2)}) collective-permute-start(f32[32,8,640]{2,1,0:T(8,128)S(1)} %get-tuple-element.17), channel_id=1, source_target_pairs={{0,1},{1,0},{2,3},{3,2},{4,5},{5,4},{6,7},{7,6},{8,9},{9,8},{10,11... | collective-permute-start | bytes 1966088 | tf_op jit(solution)/shard_map/left_core_swap/ppermute | solution.py:60
  28.7 8.0 %collective-permute-start.3 = (f32[8,640]{1,0:T(8,128)S(1)}, f32[8,640]{1,0:T(8,128)S(1)}, u32[]{:S(2)}, u32[]{:S(2)}) collective-permute-start(f32[8,640]{1,0:T(8,128)S(1)} %add_up.1), channel_id=1, source_target_pairs={{0,12},{1,13},{2,14},{3,15},{4,8},{5,9},{6,10},{7,11},{8,4},{9,5},... | collective-permute-start | bytes 61448 | tf_op jit(solution)/shard_map/left_sum/ppermute | solution.py:60
  34.2 7.7 %collective-permute-start.2 = (f32[8,640]{1,0:T(8,128)S(1)}, f32[8,640]{1,0:T(8,128)S(1)}, u32[]{:S(2)}, u32[]{:S(2)}) collective-permute-start(f32[8,640]{1,0:T(8,128)S(1)} %add_up.1), channel_id=1, source_target_pairs={{0,8},{1,9},{2,10},{3,11},{4,12},{5,13},{6,14},{7,15},{8,0},{9,1},... | collective-permute-start | bytes 61448 | tf_op jit(solution)/shard_map/left_sum/ppermute | solution.py:60
  35.6 6.3 %collective-permute-start.1 = (f32[8,640]{1,0:T(8,128)S(1)}, f32[8,640]{1,0:T(8,128)S(1)}, u32[]{:S(2)}, u32[]{:S(2)}) collective-permute-start(f32[8,640]{1,0:T(8,128)S(1)} %add_up.1), channel_id=1, source_target_pairs={{0,4},{1,5},{2,6},{3,7},{4,0},{5,1},{6,2},{7,3},{8,12},{9,13},{10,... | collective-permute-start | bytes 61448 | tf_op jit(solution)/shard_map/left_sum/ppermute | solution.py:60
  57.2 2.1 %collective-permute-start.4 = (f32[32,8,640]{2,1,0:T(8,128)S(1)}, f32[32,8,640]{2,1,0:T(8,128)S(1)}, u32[]{:S(2)}, u32[]{:S(2)}) collective-permute-start(f32[32,8,640]{2,1,0:T(8,128)S(1)} %all_to_all.11.left_ref), channel_id=1, source_target_pairs={{0,1},{1,0},{2,3},{3,2},{4,5},{5,4},{6,7},{7,6},{8,9},{9,8},{10,11... | collective-permute-start | bytes 1966088 | tf_op jit(solution)/shard_map/left_sum/ppermute | solution.py:60
  60.4 4.2 %collective-permute-start.7 = (f32[80,128]{1,0:T(8,128)S(1)}, f32[80,128]{1,0:T(8,128)S(1)}, u32[]{:S(2)}, u32[]{:S(2)}) collective-permute-start(f32[80,128]{1,0:T(8,128)S(1)} %get-tuple-element.22), channel_id=1, source_target_pairs={{0,48},{1,193},{2,50},{3,195},{4,52},{5,197},{6,54},{7,199},{8,56}... | collective-permute-start | bytes 122888 | tf_op jit(solution)/shard_map/right_sum/ppermute | solution.py:60
  61.7 5.5 %collective-permute-start.6 = (f32[80,128]{1,0:T(8,128)S(1)}, f32[80,128]{1,0:T(8,128)S(1)}, u32[]{:S(2)}, u32[]{:S(2)}) collective-permute-start(f32[80,128]{1,0:T(8,128)S(1)} %get-tuple-element.22), channel_id=1, source_target_pairs={{0,32},{1,129},{2,34},{3,131},{4,36},{5,133},{6,38},{7,135},{8,40}... | collective-permute-start | bytes 122888 | tf_op jit(solution)/shard_map/right_sum/ppermute | solution.py:60
  64.1 4.0 %collective-permute-start.5 = (f32[80,128]{1,0:T(8,128)S(1)}, f32[80,128]{1,0:T(8,128)S(1)}, u32[]{:S(2)}, u32[]{:S(2)}) collective-permute-start(f32[80,128]{1,0:T(8,128)S(1)} %get-tuple-element.22), channel_id=1, source_target_pairs={{0,16},{1,65},{2,18},{3,67},{4,20},{5,69},{6,22},{7,71},{8,24},{9,... | collective-permute-start | bytes 122888 | tf_op jit(solution)/shard_map/right_sum/ppermute | solution.py:60
  68.1 5.4 %collective-permute-start.10 = (f32[80,128]{1,0:T(8,128)S(1)}, f32[80,128]{1,0:T(8,128)S(1)}, u32[]{:S(2)}, u32[]{:S(2)}) collective-permute-start(f32[80,128]{1,0:T(8,128)S(1)} %add_add_fusion.t0_ref), channel_id=1, source_target_pairs={{0,192},{1,49},{2,194},{3,51},{4,196},{5,53},{6,198},{7,55},{8,200... | collective-permute-start | bytes 122888 | tf_op jit(solution)/shard_map/right_sum/ppermute | solution.py:60
  70.1 5.5 %collective-permute-start.9 = (f32[80,128]{1,0:T(8,128)S(1)}, f32[80,128]{1,0:T(8,128)S(1)}, u32[]{:S(2)}, u32[]{:S(2)}) collective-permute-start(f32[80,128]{1,0:T(8,128)S(1)} %add_add_fusion.t0_ref), channel_id=1, source_target_pairs={{0,128},{1,33},{2,130},{3,35},{4,132},{5,37},{6,134},{7,39},{8,136... | collective-permute-start | bytes 122888 | tf_op jit(solution)/shard_map/right_sum/ppermute | solution.py:60
  70.9 4.7 %collective-permute-start.8 = (f32[80,128]{1,0:T(8,128)S(1)}, f32[80,128]{1,0:T(8,128)S(1)}, u32[]{:S(2)}, u32[]{:S(2)}) collective-permute-start(f32[80,128]{1,0:T(8,128)S(1)} %add_add_fusion.t0_ref), channel_id=1, source_target_pairs={{0,64},{1,17},{2,66},{3,19},{4,68},{5,21},{6,70},{7,23},{8,72},{9,... | collective-permute-start | bytes 122888 | tf_op jit(solution)/shard_map/right_sum/ppermute | solution.py:60

commit v3 on v2

--- a/solution.py
+++ b/solution.py
@@ -82,11 +82,13 @@
     basis_copy = pltpu.make_async_copy(basis_ref.at[m], basis_at, basis_sem)
     basis_copy.start()
     copies = []
-    for b in range(COL_BLOCKS):
-        cols = pl.ds(b * CHUNK_COLS, CHUNK_COLS)
+    for b in range(2):
+        cols = pl.ds(b * (D // 2), D // 2)
         pair = (
-            pltpu.make_async_copy(grads_ref.at[0, m, :, cols], grads_at.at[b], sems.at[b, 0]),
-            pltpu.make_async_copy(errors_ref.at[0, m, :, cols], errors_at.at[b], sems.at[b, 1]),
+            pltpu.make_async_copy(grads_ref.at[0, m, :, cols], grads_at.at[:, cols], sems.at[b, 0]),
+            pltpu.make_async_copy(
+                errors_ref.at[0, m, :, cols], errors_at.at[:, cols], sems.at[b, 1]
+            ),
         )
         for copy in pair:
             copy.start()
@@ -94,12 +96,14 @@
     basis_copy.wait()
     basis = basis_at[...].astype(jnp.bfloat16)
     for b in range(COL_BLOCKS):
-        for copy in copies[b]:
-            copy.wait()
+        if b % (COL_BLOCKS // 2) == 0:
+            for copy in copies[b // (COL_BLOCKS // 2)]:
+                copy.wait()
+        cols = slice(b * CHUNK_COLS, (b + 1) * CHUNK_COLS)
         corrected = (
-            grads_at[b].astype(jnp.float32) + errors_at[b].astype(jnp.float32)
+            grads_at[:, cols].astype(jnp.float32) + errors_at[:, cols].astype(jnp.float32)
         ).astype(jnp.bfloat16)
-        corrected_ref[:, b * CHUNK_COLS : (b + 1) * CHUNK_COLS] = corrected
+        corrected_ref[:, cols] = corrected
         left = jnp.dot(basis, corrected, preferred_element_type=jnp.float32)
         for g in range(4):
             left_ref[b * 4 + g] = left[8 * g : 8 * g + 8]
@@ -118,10 +122,10 @@
             jax.ShapeDtypeStruct((CHUNKS, 8, CHUNK_COLS), jnp.float32),
         ],
         scratch_shapes=[
-            pltpu.VMEM((COL_BLOCKS, ROWS, CHUNK_COLS), jnp.bfloat16),
-            pltpu.VMEM((COL_BLOCKS, ROWS, CHUNK_COLS), jnp.bfloat16),
+            pltpu.VMEM((ROWS, D), jnp.bfloat16),
+            pltpu.VMEM((ROWS, D), jnp.bfloat16),
             pltpu.VMEM((RANK, ROWS), jnp.float32),
-            pltpu.SemaphoreType.DMA((COL_BLOCKS, 2)),
+            pltpu.SemaphoreType.DMA((2, 2)),
             pltpu.SemaphoreType.DMA(()),
         ],
         compiler_params=pltpu.CompilerParams(vmem_limit_bytes=16 * MIB),
@@ -277,7 +281,7 @@
     core = core_ref[0]
     t = (t0_ref[...] + t1_ref[...]) + (t2_ref[...] + t3_ref[...])
     t = t * (1.0 / HOSTS)
-    copies = []
+    copies, rights = [], []
     for n in range(2):
         m = core if n == 0 else 1 - core
         terms_ref = (terms_own_ref, terms_other_ref)[n]
@@ -285,7 +289,7 @@
         mine = t[40 * n : 40 * n + 40]
         mine = jnp.concatenate([mine[:, RANK * q : RANK * q + RANK] for q in range(4)], axis=0)
         inverse = inverse_ref[n]
-        right_ref[m] = high(inverse, mine, nt)
+        rights.append((m, mine, inverse))
         hi, mid, lo = split3(high(high(mine, inverse, nt), inverse, nn))
         w = jnp.concatenate([hi, hi, hi, mid, mid, lo], axis=1)
         for b in range(COL_BLOCKS):
@@ -307,6 +311,8 @@
             for copy in pair:
                 copy.start()
             copies.extend(pair)
+    for m, mine, inverse in rights:
+        right_ref[m] = high(inverse, mine, nt)
     for copy in copies:
         copy.wait()
 
@@ -346,19 +352,19 @@
     with jax.named_scope("left_sum"):
         parts = exchange(left_own + arrived)
         part = add_up(parts)
-        p1, p3, p2 = (permute(part, z_pairs(k)) for k in (1, 3, 2))
-        part = (part + p1) + (p2 + p3)
+        p2, p3, p1 = (permute(part, z_pairs(k)) for k in (2, 3, 1))
+        part = (part + p1) + (p3 + p2)
         left_own = exchange(jnp.broadcast_to(part[None], (CHUNKS,) + part.shape))
         left_other = permute(left_own, CORE_SWAP)
     t_own, gram_own, terms_own = right_part(left_own, corrected_own)
     t, gram, terms_other = right_part(left_other, corrected_other, (t_own, gram_own))
     with jax.named_scope("right_sum"):
-        t1, t3, t2 = (permute(t, first_pairs(k)) for k in (1, 3, 2))
-        t = (t + t1) + (t2 + t3)
-        t1, t3, t2 = (permute(t, second_pairs(k)) for k in (1, 3, 2))
+        t2, t3, t1 = (permute(t, first_pairs(k)) for k in (2, 3, 1))
+        t = (t + t1) + (t3 + t2)
+        t2, t3, t1 = (permute(t, second_pairs(k)) for k in (2, 3, 1))
     inverse = inverses(gram)
     update, new_errors, right = final_part(
-        core[None], (t, t1, t2, t3), inverse, terms_own, terms_other, corrected_own, corrected_other
+        core[None], (t, t1, t3, t2), inverse, terms_own, terms_other, corrected_own, corrected_other
     )
     return update, new_errors, jnp.swapaxes(right, 1, 2)
 

time: 80.6 us -> 76.9 us (0.954)
  Pallas kernels: 14.8 us -> 12.7 us
  waiting for transfers between devices: 11.9 us -> 10.3 us
    pallas_call x2, Pallas kernels: 6.83 us -> 4.8 us  [left_part(): pl.pallas_call(left_kernel, in_specs=[pl.BlockSpec(memory_space=pltpu.SME...]
    ppermute x11, waiting for transfers between devices: 11.9 us -> 10.3 us  [permute(): return lax.ppermute(a, AXES, perm)]
  transfers between devices with their start and end apart: 11 -> 11, of which waited for: 5 -> 9; matrix products, arithmetic and copies ran while one was open for 0% -> 0% of each run, Pallas kernels for 7% -> 6%
where the time goes in v3:
time: 76.9 us; the launch traced here: 76.7 us
  blocking collectives  36.4 us (47%)
  starting transfers between devices  16.3 us (21%)
  Pallas kernels  12.7 us (17%)
  waiting for transfers between devices  10.3 us (13%)
  between operations  0.87 us (1%)
    all_to_all x2, blocking collectives, exchange(): lax.all_to_all(parts, AXES, 0, 0, axis_index_groups=GROUPS, tiled=True)  36.4 us
    ppermute x11, starting transfers between devices, permute(): return lax.ppermute(a, AXES, perm)  16.3 us
    ppermute x11, waiting for transfers between devices, permute(): return lax.ppermute(a, AXES, perm)  10.3 us
    pallas_call x2, Pallas kernels, left_part(): pl.pallas_call(left_kernel, in_specs=[pl.BlockSpec(memory_space=pltpu.SME...  4.8 us
    pallas_call x1, Pallas kernels, final_part(): pl.pallas_call(final_kernel, in_specs=[pl.BlockSpec(memory_space=pltpu.SM...  4.51 us
    pallas_call x2, Pallas kernels, right_part(): pl.pallas_call(right_both_kernel if both else right_kernel, in_specs=vmem...  2.15 us
  transfers between devices with their start and end apart: 11, of which 9 were waited for; matrix products, arithmetic and copies ran while one was open for 0% of the time, Pallas kernels for 6%

profile of v3, /device:TPU:2, one launch (start us, length us, event | category | flops | bytes accessed | tf_op | source)
XLA Modules:
  0.0 76.7 jit_solution(4000177965224176502)
XLA Ops:
  0.6 2.4 %left.3 = (bf16[160,5120]{1,0:T(8,128)(2,1)S(1)}, f32[32,8,640]{2,1,0:T(8,128)S(1)}) custom-call(s32[1]{0:T(128)} %bitcast.2.m_ref, bf16[1,2,160,5120]{3,2,1,0:T(8,128)(2,1)} %grads_ref.3, bf16[1,2,160,5120]{3,2,1,0:T(8,128)(2,1)} %errors_ref.3, f32[2,32,160]{2,1,0:T(8,128)} %bitcast.4), custom_call_target="tpu_custom_call" | custom-call | flops 52428800 | bytes 5570560 | tf_op jit(solution)/shard_map/left/pallas_call | solution.py:113
  3.1 0.1 collective-permute-start
  3.2 2.4 %left.2 = (bf16[160,5120]{1,0:T(8,128)(2,1)S(1)}, f32[32,8,640]{2,1,0:T(8,128)S(1)}) custom-call(s32[1]{0:T(128)} %bitcast.m_ref.core_ref, bf16[1,2,160,5120]{3,2,1,0:T(8,128)(2,1)} %grads_ref.3, bf16[1,2,160,5120]{3,2,1,0:T(8,128)(2,1)} %errors_ref.3, f32[2,32,160]{2,1,0:T(8,128)} %bitcast.5), custom_call_target="tpu_custom_call" | custom-call | flops 52428800 | bytes 5570560 | tf_op jit(solution)/shard_map/left/pallas_call | solution.py:113
  5.5 0.0 collective-permute-done
  5.6 0.1 add.21
  5.6 21.1 %all_to_all.10.parts_ref = f32[32,8,640]{2,1,0:T(8,128)S(1)} all-to-all(f32[32,8,640]{2,1,0:T(8,128)S(1)} %add.21), channel_id=1, replica_groups={{0,16,32,48,64,80,96,112,128,144,160,176,192,208,224,240,2,18,34,50,66,..., dimensions={0} | all-to-all | bytes 1310720 | tf_op jit(solution)/shard_map/left_sum/all_to_all | solution.py:56
  26.8 6.4 %collective-permute-start.3 = (f32[8,640]{1,0:T(8,128)S(1)}, f32[8,640]{1,0:T(8,128)S(1)}, u32[]{:S(2)}, u32[]{:S(2)}) collective-permute-start(f32[8,640]{1,0:T(8,128)S(1)} %add_up.1), channel_id=1, source_target_pairs={{0,8},{1,9},{2,10},{3,11},{4,12},{5,13},{6,14},{7,15},{8,0},{9,1},... | collective-permute-start | bytes 61448 | tf_op jit(solution)/shard_map/left_sum/ppermute | solution.py:60
  33.1 0.6 collective-permute-start.2
  33.7 0.9 %collective-permute-start.1 = (f32[8,640]{1,0:T(8,128)S(1)}, f32[8,640]{1,0:T(8,128)S(1)}, u32[]{:S(2)}, u32[]{:S(2)}) collective-permute-start(f32[8,640]{1,0:T(8,128)S(1)} %add_up.1), channel_id=1, source_target_pairs={{0,4},{1,5},{2,6},{3,7},{4,0},{5,1},{6,2},{7,3},{8,12},{9,13},{10,... | collective-permute-start | bytes 61448 | tf_op jit(solution)/shard_map/left_sum/ppermute | solution.py:60
  34.6 0.3 collective-permute-done.3
  34.9 4.1 %collective-permute-done.2 = f32[8,640]{1,0:T(8,128)S(1)} collective-permute-done((f32[8,640]{1,0:T(8,128)S(1)}, f32[8,640]{1,0:T(8,128)S(1)}, u32[]{:S(2)}, u32[]{:S(2)}) %collective-permute-start.2) | collective-permute-done | bytes 20512 | tf_op jit(solution)/shard_map/left_sum/ppermute | solution.py:60
  39.0 0.0 collective-permute-done.1
  39.1 15.3 %all_to_all.11.left_ref = f32[32,8,640]{2,1,0:T(8,128)S(1)} all-to-all(f32[32,8,640]{2,1,0:T(8,128)S(1)} %broadcast_in_dim.15), channel_id=1, replica_groups={{0,16,32,48,64,80,96,112,128,144,160,176,192,208,224,240,2,18,34,50,66,..., dimensions={0} | all-to-all | bytes 1310720 | tf_op jit(solution)/shard_map/left_sum/all_to_all | solution.py:56
  54.4 0.0 collective-permute-start.4
  54.4 1.1 %right.2 = (f32[40,128]{1,0:T(8,128)S(1)}, f32[32,32]{1,0:T(8,128)S(1)}, bf16[192,5120]{1,0:T(8,128)(2,1)S(1)}) custom-call(f32[32,8,640]{2,1,0:T(8,128)S(1)} %all_to_all.11.left_ref, bf16[160,5120]{1,0:T(8,128)(2,1)S(1)} %get-tuple-element.19.corrected_ref.corrected_own_ref), custom_call_target="tpu_custom_call" | custom-call | flops 251658240 | bytes 4259840 | tf_op jit(solution)/shard_map/right/pallas_call | solution.py:199
  55.5 1.0 %collective-permute-done.4.left_ref = f32[32,8,640]{2,1,0:T(8,128)S(1)} collective-permute-done((f32[32,8,640]{2,1,0:T(8,128)S(1)}, f32[32,8,640]{2,1,0:T(8,128)S(1)}, u32[]{:S(2)}, u32[]{:S(2)}) %collective-permute-start.4) | collective-permute-done | bytes 655392 | tf_op jit(solution)/shard_map/left_sum/ppermute | solution.py:60
  56.5 1.1 %right.3 = (f32[80,128]{1,0:T(8,128)S(1)}, f32[2,32,32]{2,1,0:T(8,128)S(1)}, bf16[192,5120]{1,0:T(8,128)(2,1)S(1)}) custom-call(f32[32,8,640]{2,1,0:T(8,128)S(1)} %collective-permute-done.4.left_ref, bf16[160,5120]{1,0:T(8,128)(2,1)S(1)} %get-tuple-element.18.corrected_ref.corrected_other_ref, f32[40,128]{1,0:T(8,128)S(1)} %get-tuple-element.20.t_own_ref, ...), custom_call_target="tpu_custom_call" | custom-call | flops 251658240 | bytes 4259840 | tf_op jit(solution)/shard_map/right/pallas_call | solution.py:199
  57.5 1.7 %collective-permute-start.7 = (f32[80,128]{1,0:T(8,128)S(1)}, f32[80,128]{1,0:T(8,128)S(1)}, u32[]{:S(2)}, u32[]{:S(2)}) collective-permute-start(f32[80,128]{1,0:T(8,128)S(1)} %get-tuple-element.22), channel_id=1, source_target_pairs={{0,32},{1,129},{2,34},{3,131},{4,36},{5,133},{6,38},{7,135},{8,40}... | collective-permute-start | bytes 122888 | tf_op jit(solution)/shard_map/right_sum/ppermute | solution.py:60
  59.3 1.3 %collective-permute-start.6 = (f32[80,128]{1,0:T(8,128)S(1)}, f32[80,128]{1,0:T(8,128)S(1)}, u32[]{:S(2)}, u32[]{:S(2)}) collective-permute-start(f32[80,128]{1,0:T(8,128)S(1)} %get-tuple-element.22), channel_id=1, source_target_pairs={{0,48},{1,193},{2,50},{3,195},{4,52},{5,197},{6,54},{7,199},{8,56}... | collective-permute-start | bytes 122888 | tf_op jit(solution)/shard_map/right_sum/ppermute | solution.py:60
  60.6 1.7 %collective-permute-start.5 = (f32[80,128]{1,0:T(8,128)S(1)}, f32[80,128]{1,0:T(8,128)S(1)}, u32[]{:S(2)}, u32[]{:S(2)}) collective-permute-start(f32[80,128]{1,0:T(8,128)S(1)} %get-tuple-element.22), channel_id=1, source_target_pairs={{0,16},{1,65},{2,18},{3,67},{4,20},{5,69},{6,22},{7,71},{8,24},{9,... | collective-permute-start | bytes 122888 | tf_op jit(solution)/shard_map/right_sum/ppermute | solution.py:60
  62.3 0.8 %collective-permute-done.7 = f32[80,128]{1,0:T(8,128)S(1)} collective-permute-done((f32[80,128]{1,0:T(8,128)S(1)}, f32[80,128]{1,0:T(8,128)S(1)}, u32[]{:S(2)}, u32[]{:S(2)}) %collective-permute-start.7) | collective-permute-done | bytes 40992 | tf_op jit(solution)/shard_map/right_sum/ppermute | solution.py:60
  63.2 0.4 collective-permute-done.6
  63.6 1.1 %collective-permute-done.5 = f32[80,128]{1,0:T(8,128)S(1)} collective-permute-done((f32[80,128]{1,0:T(8,128)S(1)}, f32[80,128]{1,0:T(8,128)S(1)}, u32[]{:S(2)}, u32[]{:S(2)}) %collective-permute-start.5) | collective-permute-done | bytes 40992 | tf_op jit(solution)/shard_map/right_sum/ppermute | solution.py:60
  64.7 1.4 %collective-permute-start.10 = (f32[80,128]{1,0:T(8,128)S(1)}, f32[80,128]{1,0:T(8,128)S(1)}, u32[]{:S(2)}, u32[]{:S(2)}) collective-permute-start(f32[80,128]{1,0:T(8,128)S(1)} %add_add_fusion.t0_ref), channel_id=1, source_target_pairs={{0,128},{1,33},{2,130},{3,35},{4,132},{5,37},{6,134},{7,39},{8,136... | collective-permute-start | bytes 122888 | tf_op jit(solution)/shard_map/right_sum/ppermute | solution.py:60
  66.1 1.9 %collective-permute-start.9 = (f32[80,128]{1,0:T(8,128)S(1)}, f32[80,128]{1,0:T(8,128)S(1)}, u32[]{:S(2)}, u32[]{:S(2)}) collective-permute-start(f32[80,128]{1,0:T(8,128)S(1)} %add_add_fusion.t0_ref), channel_id=1, source_target_pairs={{0,192},{1,49},{2,194},{3,51},{4,196},{5,53},{6,198},{7,55},{8,200... | collective-permute-start | bytes 122888 | tf_op jit(solution)/shard_map/right_sum/ppermute | solution.py:60
  68.0 0.2 collective-permute-start.8
  68.2 1.2 %inverse.1.inverse_ref = f32[2,32,32]{2,1,0:T(8,128)S(1)} custom-call(f32[2,32,32]{2,1,0:T(8,128)S(1)} %get-tuple-element.23.gram_ref), custom_call_target="tpu_custom_call" | custom-call | flops 10000000 | bytes 8000000 | tf_op jit(solution)/shard_map/inverse/pallas_call | solution.py:247
  69.4 0.8 %collective-permute-done.10.t3_ref = f32[80,128]{1,0:T(8,128)S(1)} collective-permute-done((f32[80,128]{1,0:T(8,128)S(1)}, f32[80,128]{1,0:T(8,128)S(1)}, u32[]{:S(2)}, u32[]{:S(2)}) %collective-permute-start.10) | collective-permute-done | bytes 40992 | tf_op jit(solution)/shard_map/right_sum/ppermute | solution.py:60
  70.2 1.0 %collective-permute-done.9.t2_ref = f32[80,128]{1,0:T(8,128)S(1)} collective-permute-done((f32[80,128]{1,0:T(8,128)S(1)}, f32[80,128]{1,0:T(8,128)S(1)}, u32[]{:S(2)}, u32[]{:S(2)}) %collective-permute-start.9) | collective-permute-done | bytes 40992 | tf_op jit(solution)/shard_map/right_sum/ppermute | solution.py:60
  71.3 0.7 collective-permute-done.8.t1_ref
  72.0 4.5 %final.1 = (bf16[2,160,5120]{2,1,0:T(8,128)(2,1)}, bf16[1,2,160,5120]{3,2,1,0:T(8,128)(2,1)}, f32[2,32,160]{2,1,0:T(8,128)}) custom-call(s32[1]{0:T(128)} %bitcast.m_ref.core_ref, f32[80,128]{1,0:T(8,128)S(1)} %add_add_fusion.t0_ref, f32[80,128]{1,0:T(8,128)S(1)} %collective-permute-done.8.t1_ref, f32[80,128]{1,0:T(8,128)S(1)} %collective-permute-done.9.t2_ref, ...), custom_call_target="tpu_custom_call" | custom-call | flops 629145600 | bytes 13107200 | tf_op jit(solution)/shard_map/final/pallas_call | solution.py:322
  (4 shorter events, 0.1 us)
Async XLA Ops:
  3.1 2.5 %collective-permute-start = (f32[32,8,640]{2,1,0:T(8,128)S(1)}, f32[32,8,640]{2,1,0:T(8,128)S(1)}, u32[]{:S(2)}, u32[]{:S(2)}) collective-permute-start(f32[32,8,640]{2,1,0:T(8,128)S(1)} %get-tuple-element.17), channel_id=1, source_target_pairs={{0,1},{1,0},{2,3},{3,2},{4,5},{5,4},{6,7},{7,6},{8,9},{9,8},{10,11... | collective-permute-start | bytes 1966088 | tf_op jit(solution)/shard_map/left_core_swap/ppermute | solution.py:60
  26.8 8.1 %collective-permute-start.3 = (f32[8,640]{1,0:T(8,128)S(1)}, f32[8,640]{1,0:T(8,128)S(1)}, u32[]{:S(2)}, u32[]{:S(2)}) collective-permute-start(f32[8,640]{1,0:T(8,128)S(1)} %add_up.1), channel_id=1, source_target_pairs={{0,8},{1,9},{2,10},{3,11},{4,12},{5,13},{6,14},{7,15},{8,0},{9,1},... | collective-permute-start | bytes 61448 | tf_op jit(solution)/shard_map/left_sum/ppermute | solution.py:60
  33.1 5.9 %collective-permute-start.2 = (f32[8,640]{1,0:T(8,128)S(1)}, f32[8,640]{1,0:T(8,128)S(1)}, u32[]{:S(2)}, u32[]{:S(2)}) collective-permute-start(f32[8,640]{1,0:T(8,128)S(1)} %add_up.1), channel_id=1, source_target_pairs={{0,12},{1,13},{2,14},{3,15},{4,8},{5,9},{6,10},{7,11},{8,4},{9,5},... | collective-permute-start | bytes 61448 | tf_op jit(solution)/shard_map/left_sum/ppermute | solution.py:60
  33.7 5.3 %collective-permute-start.1 = (f32[8,640]{1,0:T(8,128)S(1)}, f32[8,640]{1,0:T(8,128)S(1)}, u32[]{:S(2)}, u32[]{:S(2)}) collective-permute-start(f32[8,640]{1,0:T(8,128)S(1)} %add_up.1), channel_id=1, source_target_pairs={{0,4},{1,5},{2,6},{3,7},{4,0},{5,1},{6,2},{7,3},{8,12},{9,13},{10,... | collective-permute-start | bytes 61448 | tf_op jit(solution)/shard_map/left_sum/ppermute | solution.py:60
  54.4 2.1 %collective-permute-start.4 = (f32[32,8,640]{2,1,0:T(8,128)S(1)}, f32[32,8,640]{2,1,0:T(8,128)S(1)}, u32[]{:S(2)}, u32[]{:S(2)}) collective-permute-start(f32[32,8,640]{2,1,0:T(8,128)S(1)} %all_to_all.11.left_ref), channel_id=1, source_target_pairs={{0,1},{1,0},{2,3},{3,2},{4,5},{5,4},{6,7},{7,6},{8,9},{9,8},{10,11... | collective-permute-start | bytes 1966088 | tf_op jit(solution)/shard_map/left_sum/ppermute | solution.py:60
  57.5 5.6 %collective-permute-start.7 = (f32[80,128]{1,0:T(8,128)S(1)}, f32[80,128]{1,0:T(8,128)S(1)}, u32[]{:S(2)}, u32[]{:S(2)}) collective-permute-start(f32[80,128]{1,0:T(8,128)S(1)} %get-tuple-element.22), channel_id=1, source_target_pairs={{0,32},{1,129},{2,34},{3,131},{4,36},{5,133},{6,38},{7,135},{8,40}... | collective-permute-start | bytes 122888 | tf_op jit(solution)/shard_map/right_sum/ppermute | solution.py:60
  59.3 4.3 %collective-permute-start.6 = (f32[80,128]{1,0:T(8,128)S(1)}, f32[80,128]{1,0:T(8,128)S(1)}, u32[]{:S(2)}, u32[]{:S(2)}) collective-permute-start(f32[80,128]{1,0:T(8,128)S(1)} %get-tuple-element.22), channel_id=1, source_target_pairs={{0,48},{1,193},{2,50},{3,195},{4,52},{5,197},{6,54},{7,199},{8,56}... | collective-permute-start | bytes 122888 | tf_op jit(solution)/shard_map/right_sum/ppermute | solution.py:60
  60.6 4.0 %collective-permute-start.5 = (f32[80,128]{1,0:T(8,128)S(1)}, f32[80,128]{1,0:T(8,128)S(1)}, u32[]{:S(2)}, u32[]{:S(2)}) collective-permute-start(f32[80,128]{1,0:T(8,128)S(1)} %get-tuple-element.22), channel_id=1, source_target_pairs={{0,16},{1,65},{2,18},{3,67},{4,20},{5,69},{6,22},{7,71},{8,24},{9,... | collective-permute-start | bytes 122888 | tf_op jit(solution)/shard_map/right_sum/ppermute | solution.py:60
  64.7 5.6 %collective-permute-start.10 = (f32[80,128]{1,0:T(8,128)S(1)}, f32[80,128]{1,0:T(8,128)S(1)}, u32[]{:S(2)}, u32[]{:S(2)}) collective-permute-start(f32[80,128]{1,0:T(8,128)S(1)} %add_add_fusion.t0_ref), channel_id=1, source_target_pairs={{0,128},{1,33},{2,130},{3,35},{4,132},{5,37},{6,134},{7,39},{8,136... | collective-permute-start | bytes 122888 | tf_op jit(solution)/shard_map/right_sum/ppermute | solution.py:60
  66.1 5.2 %collective-permute-start.9 = (f32[80,128]{1,0:T(8,128)S(1)}, f32[80,128]{1,0:T(8,128)S(1)}, u32[]{:S(2)}, u32[]{:S(2)}) collective-permute-start(f32[80,128]{1,0:T(8,128)S(1)} %add_add_fusion.t0_ref), channel_id=1, source_target_pairs={{0,192},{1,49},{2,194},{3,51},{4,196},{5,53},{6,198},{7,55},{8,200... | collective-permute-start | bytes 122888 | tf_op jit(solution)/shard_map/right_sum/ppermute | solution.py:60
  68.0 4.0 %collective-permute-start.8 = (f32[80,128]{1,0:T(8,128)S(1)}, f32[80,128]{1,0:T(8,128)S(1)}, u32[]{:S(2)}, u32[]{:S(2)}) collective-permute-start(f32[80,128]{1,0:T(8,128)S(1)} %add_add_fusion.t0_ref), channel_id=1, source_target_pairs={{0,64},{1,17},{2,66},{3,19},{4,68},{5,21},{6,70},{7,23},{8,72},{9,... | collective-permute-start | bytes 122888 | tf_op jit(solution)/shard_map/right_sum/ppermute | solution.py:60

commit v4 on v3

--- a/solution.py
+++ b/solution.py
@@ -66,6 +66,11 @@
     mid = rest.astype(jnp.bfloat16)
     lo = (rest - mid.astype(jnp.float32)).astype(jnp.bfloat16)
     return hi, mid, lo
+
+
+high = functools.partial(
+    lax.dot_general, precision=lax.Precision.HIGHEST, preferred_element_type=jnp.float32
+)
 
 
 def cost(flops, nbytes):
@@ -153,70 +158,85 @@
     )(parts)
 
 
-def right_body(left_ref, corrected_ref, terms_ref, stack_ref):
+NT = (((1,), (1,)), ((), ()))
+
+
+def right_body(left_ref, corrected_ref, terms_ref):
     for b in range(COL_BLOCKS):
-        cols = slice(b * CHUNK_COLS, (b + 1) * CHUNK_COLS)
-        for g in range(4):
-            rows = slice(8 * g, 8 * g + 8)
-            stack_ref[rows, cols] = left_ref[b * 4 + g]
-    for b in range(COL_BLOCKS):
-        cols = slice(b * CHUNK_COLS, (b + 1) * CHUNK_COLS)
-        hi, mid, lo = split3(stack_ref[:, cols])
-        for i, term in enumerate((hi, mid, lo, hi, mid, hi)):
-            terms_ref[i * RANK : (i + 1) * RANK, cols] = term
-    terms = terms_ref[0 : 3 * RANK, :]
-    nt = (((1,), (1,)), ((), ()))
-    t = lax.dot_general(corrected_ref[...], terms, nt, preferred_element_type=jnp.float32)
+        left = jnp.concatenate([left_ref[b * 4 + g] for g in range(4)], axis=0)
+        for i, term in enumerate(split3(left)):
+            terms_ref[i * RANK : (i + 1) * RANK, b * CHUNK_COLS : (b + 1) * CHUNK_COLS] = term
+    t = lax.dot_general(
+        corrected_ref[...], terms_ref[...], NT, preferred_element_type=jnp.float32
+    )
     t = t[:, 0:RANK] + (t[:, RANK : 2 * RANK] + t[:, 2 * RANK : 3 * RANK])
-    packed = jnp.concatenate([t[40 * i : 40 * i + 40] for i in range(4)], axis=1)
-    g = lax.dot_general(terms, terms, nt, preferred_element_type=jnp.float32)
-    gram = g[0:RANK, 0:RANK]
-    rest = jnp.zeros_like(gram)
+    return jnp.concatenate([t[40 * i : 40 * i + 40] for i in range(4)], axis=1)
+
+
+def gram_body(terms_ref):
+    terms = terms_ref[...]
+    g = lax.dot_general(terms, terms, NT, preferred_element_type=jnp.float32)
+    rest = jnp.zeros((RANK, RANK), jnp.float32)
     for i in range(3):
         for j in range(3):
             if i + j > 0:
                 rest = rest + g[i * RANK : (i + 1) * RANK, j * RANK : (j + 1) * RANK]
-    return packed, gram + rest
-
-
-def right_kernel(left_ref, corrected_ref, t_ref, gram_ref, terms_ref, stack_ref):
-    t_ref[...], gram_ref[...] = right_body(left_ref, corrected_ref, terms_ref, stack_ref)
-
-
-def right_both_kernel(
-    left_ref, corrected_ref, t_own_ref, gram_own_ref, t_ref, gram_ref, terms_ref, stack_ref
-):
-    t, gram = right_body(left_ref, corrected_ref, terms_ref, stack_ref)
+    return g[0:RANK, 0:RANK] + rest
+
+
+def right_own_kernel(left_ref, corrected_ref, t_ref, terms_ref, gram_ref):
+    t_ref[...] = right_body(left_ref, corrected_ref, terms_ref)
+    gram_ref[...] = gram_body(terms_ref)
+
+
+def right_other_kernel(left_ref, corrected_ref, t_own_ref, t_ref, terms_ref):
     t_ref[0:40] = t_own_ref[...]
-    t_ref[40:80] = t
-    gram_ref[0] = gram_own_ref[...]
-    gram_ref[1] = gram
-
-
-def right_part(left, corrected, own=None):
-    both = own is not None
-    n = 2 if both else 1
-    return pl.pallas_call(
-        right_both_kernel if both else right_kernel,
-        in_specs=vmem(4 if both else 2),
-        out_specs=vmem(3),
-        out_shape=[
-            jax.ShapeDtypeStruct((40 * n, 128), jnp.float32),
-            jax.ShapeDtypeStruct((2, RANK, RANK) if both else (RANK, RANK), jnp.float32),
-            jax.ShapeDtypeStruct((6 * RANK, D), jnp.bfloat16),
-        ],
-        scratch_shapes=[pltpu.VMEM((RANK, D), jnp.float32)],
-        compiler_params=pltpu.CompilerParams(vmem_limit_bytes=24 * MIB),
-        cost_estimate=cost(2 * 256 * D * 96, 2 * ROWS * D + 16 * RANK * D),
+    t_ref[40:80] = right_body(left_ref, corrected_ref, terms_ref)
+
+
+def gram_kernel(terms_ref, gram_ref):
+    gram_ref[...] = gram_body(terms_ref)
+
+
+GRAM = jax.ShapeDtypeStruct((RANK, RANK), jnp.float32)
+
+
+def right_part(left, corrected, t_own=None):
+    own = t_own is None
+    out_shape = [
+        jax.ShapeDtypeStruct((40 if own else 80, 128), jnp.float32),
+        jax.ShapeDtypeStruct((3 * RANK, D), jnp.bfloat16),
+    ]
+    if own:
+        out_shape.append(GRAM)
+    return pl.pallas_call(
+        right_own_kernel if own else right_other_kernel,
+        in_specs=vmem(2 if own else 3),
+        out_specs=vmem(len(out_shape)),
+        out_shape=out_shape,
+        compiler_params=pltpu.CompilerParams(vmem_limit_bytes=16 * MIB),
+        cost_estimate=cost(2 * 256 * D * 96, 2 * ROWS * D + 10 * RANK * D),
         name="right",
-    )(left, corrected, *(own or ()))
-
-
-def inverse_kernel(gram_ref, inverse_ref):
+    )(left, corrected, *(() if own else (t_own,)))
+
+
+def gram_part(terms):
+    return pl.pallas_call(
+        gram_kernel,
+        in_specs=vmem(1),
+        out_specs=pl.BlockSpec(memory_space=pltpu.VMEM),
+        out_shape=GRAM,
+        compiler_params=pltpu.CompilerParams(vmem_limit_bytes=4 * MIB),
+        cost_estimate=cost(2 * 96 * D * 96, 6 * RANK * D),
+        name="gram",
+    )(terms)
+
+
+def inverse_kernel(gram_own_ref, gram_other_ref, inverse_ref, gram_inverse_ref):
     row = lax.broadcasted_iota(jnp.int32, (RANK, RANK), 0)
     col = lax.broadcasted_iota(jnp.int32, (RANK, RANK), 1)
     eye = jnp.where(row == col, 1.0, 0.0).astype(jnp.float32)
-    a = jnp.concatenate([gram_ref[0], eye, gram_ref[1], eye], axis=1)
+    a = jnp.concatenate([gram_own_ref[...], eye, gram_other_ref[...], eye], axis=1)
     rows = lax.broadcasted_iota(jnp.int32, a.shape, 0)
     first = lax.broadcasted_iota(jnp.int32, a.shape, 1) < 2 * RANK
     for base in range(0, RANK, 4):
@@ -239,20 +259,22 @@
             a = a - below[p] * across[p]
             done = jnp.where(rows == k, across[p], done)
         a = jnp.where(rows >= base + 4, a, done)
-    inverse_ref[0] = a[:, RANK : 2 * RANK]
-    inverse_ref[1] = a[:, 3 * RANK : 4 * RANK]
-
-
-def inverses(gram):
+    for n in range(2):
+        inverse = a[:, (2 * n + 1) * RANK : (2 * n + 2) * RANK]
+        inverse_ref[n] = inverse
+        gram_inverse_ref[n] = high(inverse, inverse, (((0,), (0,)), ((), ())))
+
+
+def inverses(gram_own, gram_other):
     return pl.pallas_call(
         inverse_kernel,
-        in_specs=vmem(1),
-        out_specs=pl.BlockSpec(memory_space=pltpu.VMEM),
-        out_shape=jax.ShapeDtypeStruct((2, RANK, RANK), jnp.float32),
+        in_specs=vmem(2),
+        out_specs=vmem(2),
+        out_shape=[jax.ShapeDtypeStruct((2, RANK, RANK), jnp.float32)] * 2,
         compiler_params=pltpu.CompilerParams(vmem_limit_bytes=4 * MIB),
         cost_estimate=cost(10_000_000, 8_000_000),
         name="inverse",
-    )(gram)
+    )(gram_own, gram_other)
 
 
 def final_kernel(
@@ -262,6 +284,7 @@
     t2_ref,
     t3_ref,
     inverse_ref,
+    gram_inverse_ref,
     terms_own_ref,
     terms_other_ref,
     corrected_own_ref,
@@ -273,11 +296,6 @@
     errors_at,
     sems,
 ):
-    high = functools.partial(
-        lax.dot_general, precision=lax.Precision.HIGHEST, preferred_element_type=jnp.float32
-    )
-    nt = (((1,), (1,)), ((), ()))
-    nn = (((1,), (0,)), ((), ()))
     core = core_ref[0]
     t = (t0_ref[...] + t1_ref[...]) + (t2_ref[...] + t3_ref[...])
     t = t * (1.0 / HOSTS)
@@ -288,13 +306,14 @@
         corrected_ref = (corrected_own_ref, corrected_other_ref)[n]
         mine = t[40 * n : 40 * n + 40]
         mine = jnp.concatenate([mine[:, RANK * q : RANK * q + RANK] for q in range(4)], axis=0)
-        inverse = inverse_ref[n]
-        rights.append((m, mine, inverse))
-        hi, mid, lo = split3(high(high(mine, inverse, nt), inverse, nn))
+        rights.append((m, mine, inverse_ref[n]))
+        hi, mid, lo = split3(high(mine, gram_inverse_ref[n], (((1,), (0,)), ((), ()))))
         w = jnp.concatenate([hi, hi, hi, mid, mid, lo], axis=1)
         for b in range(COL_BLOCKS):
             cols = slice(b * CHUNK_COLS, (b + 1) * CHUNK_COLS)
-            recon = jnp.dot(w, terms_ref[:, cols], preferred_element_type=jnp.float32)
+            hi, mid, lo = (terms_ref[i * RANK : (i + 1) * RANK, cols] for i in range(3))
+            terms = jnp.concatenate([hi, mid, lo, hi, mid, hi], axis=0)
+            recon = jnp.dot(w, terms, preferred_element_type=jnp.float32)
             update_at[n, b] = recon.astype(jnp.bfloat16)
             errors_at[n, b] = (corrected_ref[:, cols].astype(jnp.float32) - recon).astype(
                 jnp.bfloat16
@@ -312,16 +331,16 @@
                 copy.start()
             copies.extend(pair)
     for m, mine, inverse in rights:
-        right_ref[m] = high(inverse, mine, nt)
+        right_ref[m] = high(inverse, mine, NT)
     for copy in copies:
         copy.wait()
 
 
-def final_part(core, ts, inverse, terms_own, terms_other, corrected_own, corrected_other):
+def final_part(core, ts, *rest):
     hbm = pl.BlockSpec(memory_space=pltpu.HBM)
     return pl.pallas_call(
         final_kernel,
-        in_specs=[pl.BlockSpec(memory_space=pltpu.SMEM)] + vmem(9),
+        in_specs=[pl.BlockSpec(memory_space=pltpu.SMEM)] + vmem(10),
         out_specs=[hbm, hbm, pl.BlockSpec(memory_space=pltpu.VMEM)],
         out_shape=[
             jax.ShapeDtypeStruct((2, ROWS, D), jnp.bfloat16),
@@ -336,7 +355,7 @@
         compiler_params=pltpu.CompilerParams(vmem_limit_bytes=24 * MIB),
         cost_estimate=cost(2 * 2 * ROWS * 192 * D, 16 * ROWS * D),
         name="final",
-    )(core, *ts, inverse, terms_own, terms_other, corrected_own, corrected_other)
+    )(core, *ts, *rest)
 
 
 def on_device(grads, errors, basis_in):
@@ -356,15 +375,23 @@
         part = (part + p1) + (p3 + p2)
         left_own = exchange(jnp.broadcast_to(part[None], (CHUNKS,) + part.shape))
         left_other = permute(left_own, CORE_SWAP)
-    t_own, gram_own, terms_own = right_part(left_own, corrected_own)
-    t, gram, terms_other = right_part(left_other, corrected_other, (t_own, gram_own))
+    t_own, terms_own, gram_own = right_part(left_own, corrected_own)
+    t, terms_other = right_part(left_other, corrected_other, t_own)
     with jax.named_scope("right_sum"):
         t2, t3, t1 = (permute(t, first_pairs(k)) for k in (2, 3, 1))
+        gram_other, t2 = lax.optimization_barrier((gram_part(terms_other), t2))
         t = (t + t1) + (t3 + t2)
         t2, t3, t1 = (permute(t, second_pairs(k)) for k in (2, 3, 1))
-    inverse = inverses(gram)
+    inverse, gram_inverse = inverses(gram_own, gram_other)
     update, new_errors, right = final_part(
-        core[None], (t, t1, t3, t2), inverse, terms_own, terms_other, corrected_own, corrected_other
+        core[None],
+        (t, t1, t3, t2),
+        inverse,
+        gram_inverse,
+        terms_own,
+        terms_other,
+        corrected_own,
+        corrected_other,
     )
     return update, new_errors, jnp.swapaxes(right, 1, 2)
 

time: 76.9 us -> 76.3 us (level)
    pallas_call x3 -> x4, Pallas kernels: 3.33 us -> 3.81 us  [the longest x2 1.85 us: right_part(): pl.pallas_call(right_own_kernel if own else right_other_kernel, in_specs=...]
  transfers between devices with their start and end apart: 11 -> 11, of which waited for: 9 -> 9; matrix products, arithmetic and copies ran while one was open for 0% -> 0% of each run, Pallas kernels for 6% -> 7%
where the time goes in v4:
time: 76.3 us; the launch traced here: 76.2 us
  blocking collectives  36.4 us (48%)
  starting transfers between devices  16.3 us (21%)
  Pallas kernels  12.9 us (17%)
  waiting for transfers between devices  9.56 us (13%)
  between operations  0.87 us (1%)
    all_to_all x2, blocking collectives, exchange(): lax.all_to_all(parts, AXES, 0, 0, axis_index_groups=GROUPS, tiled=True)  36.4 us
    ppermute x11, starting transfers between devices, permute(): return lax.ppermute(a, AXES, perm)  16.3 us
    ppermute x11, waiting for transfers between devices, permute(): return lax.ppermute(a, AXES, perm)  9.56 us
    pallas_call x2, Pallas kernels, left_part(): pl.pallas_call(left_kernel, in_specs=[pl.BlockSpec(memory_space=pltpu.SME...  4.8 us
    pallas_call x1, Pallas kernels, final_part(): pl.pallas_call(final_kernel, in_specs=[pl.BlockSpec(memory_space=pltpu.SM...  4.26 us
    pallas_call x2, Pallas kernels, right_part(): pl.pallas_call(right_own_kernel if own else right_other_kernel, in_specs=...  1.85 us
  transfers between devices with their start and end apart: 11, of which 9 were waited for; matrix products, arithmetic and copies ran while one was open for 0% of the time, Pallas kernels for 7%

profile of v4, /device:TPU:2, one launch (start us, length us, event | category | flops | bytes accessed | tf_op | source)
XLA Modules:
  0.0 76.2 jit_solution(9534113916883187620)
XLA Ops:
  0.6 2.4 %left.3 = (bf16[160,5120]{1,0:T(8,128)(2,1)S(1)}, f32[32,8,640]{2,1,0:T(8,128)S(1)}) custom-call(s32[1]{0:T(128)} %bitcast.2.m_ref, bf16[1,2,160,5120]{3,2,1,0:T(8,128)(2,1)} %grads_ref.3, bf16[1,2,160,5120]{3,2,1,0:T(8,128)(2,1)} %errors_ref.3, f32[2,32,160]{2,1,0:T(8,128)} %bitcast.4), custom_call_target="tpu_custom_call" | custom-call | flops 52428800 | bytes 5570560 | tf_op jit(solution)/shard_map/left/pallas_call | solution.py:118
  3.1 0.1 collective-permute-start
  3.2 2.4 %left.2 = (bf16[160,5120]{1,0:T(8,128)(2,1)S(1)}, f32[32,8,640]{2,1,0:T(8,128)S(1)}) custom-call(s32[1]{0:T(128)} %bitcast.m_ref.core_ref, bf16[1,2,160,5120]{3,2,1,0:T(8,128)(2,1)} %grads_ref.3, bf16[1,2,160,5120]{3,2,1,0:T(8,128)(2,1)} %errors_ref.3, f32[2,32,160]{2,1,0:T(8,128)} %bitcast.5), custom_call_target="tpu_custom_call" | custom-call | flops 52428800 | bytes 5570560 | tf_op jit(solution)/shard_map/left/pallas_call | solution.py:118
  5.5 0.0 collective-permute-done
  5.6 0.1 add.21
  5.6 21.1 %all_to_all.10.parts_ref = f32[32,8,640]{2,1,0:T(8,128)S(1)} all-to-all(f32[32,8,640]{2,1,0:T(8,128)S(1)} %add.21), channel_id=1, replica_groups={{0,16,32,48,64,80,96,112,128,144,160,176,192,208,224,240,2,18,34,50,66,..., dimensions={0} | all-to-all | bytes 1310720 | tf_op jit(solution)/shard_map/left_sum/all_to_all | solution.py:56
  26.8 6.4 %collective-permute-start.3 = (f32[8,640]{1,0:T(8,128)S(1)}, f32[8,640]{1,0:T(8,128)S(1)}, u32[]{:S(2)}, u32[]{:S(2)}) collective-permute-start(f32[8,640]{1,0:T(8,128)S(1)} %add_up.1), channel_id=1, source_target_pairs={{0,8},{1,9},{2,10},{3,11},{4,12},{5,13},{6,14},{7,15},{8,0},{9,1},... | collective-permute-start | bytes 61448 | tf_op jit(solution)/shard_map/left_sum/ppermute | solution.py:60
  33.1 0.6 collective-permute-start.2
  33.7 0.9 %collective-permute-start.1 = (f32[8,640]{1,0:T(8,128)S(1)}, f32[8,640]{1,0:T(8,128)S(1)}, u32[]{:S(2)}, u32[]{:S(2)}) collective-permute-start(f32[8,640]{1,0:T(8,128)S(1)} %add_up.1), channel_id=1, source_target_pairs={{0,4},{1,5},{2,6},{3,7},{4,0},{5,1},{6,2},{7,3},{8,12},{9,13},{10,... | collective-permute-start | bytes 61448 | tf_op jit(solution)/shard_map/left_sum/ppermute | solution.py:60
  34.6 0.3 collective-permute-done.3
  34.9 4.1 %collective-permute-done.2 = f32[8,640]{1,0:T(8,128)S(1)} collective-permute-done((f32[8,640]{1,0:T(8,128)S(1)}, f32[8,640]{1,0:T(8,128)S(1)}, u32[]{:S(2)}, u32[]{:S(2)}) %collective-permute-start.2) | collective-permute-done | bytes 20512 | tf_op jit(solution)/shard_map/left_sum/ppermute | solution.py:60
  39.0 0.0 collective-permute-done.1
  39.1 15.3 %all_to_all.11.left_ref = f32[32,8,640]{2,1,0:T(8,128)S(1)} all-to-all(f32[32,8,640]{2,1,0:T(8,128)S(1)} %broadcast_in_dim.15), channel_id=1, replica_groups={{0,16,32,48,64,80,96,112,128,144,160,176,192,208,224,240,2,18,34,50,66,..., dimensions={0} | all-to-all | bytes 1310720 | tf_op jit(solution)/shard_map/left_sum/all_to_all | solution.py:56
  54.4 0.0 collective-permute-start.4
  54.4 1.1 %right.2 = (f32[40,128]{1,0:T(8,128)S(1)}, bf16[96,5120]{1,0:T(8,128)(2,1)S(1)}, f32[32,32]{1,0:T(8,128)S(1)}) custom-call(f32[32,8,640]{2,1,0:T(8,128)S(1)} %all_to_all.11.left_ref, bf16[160,5120]{1,0:T(8,128)(2,1)S(1)} %get-tuple-element.22.corrected_ref.corrected_own_ref), custom_call_target="tpu_custom_call" | custom-call | flops 251658240 | bytes 3276800 | tf_op jit(solution)/shard_map/right/pallas_call | solution.py:212
  55.4 1.0 %collective-permute-done.4.left_ref = f32[32,8,640]{2,1,0:T(8,128)S(1)} collective-permute-done((f32[32,8,640]{2,1,0:T(8,128)S(1)}, f32[32,8,640]{2,1,0:T(8,128)S(1)}, u32[]{:S(2)}, u32[]{:S(2)}) %collective-permute-start.4) | collective-permute-done | bytes 655392 | tf_op jit(solution)/shard_map/left_sum/ppermute | solution.py:60
  56.5 0.8 %right.3 = (f32[80,128]{1,0:T(8,128)S(1)}, bf16[96,5120]{1,0:T(8,128)(2,1)S(1)}) custom-call(f32[32,8,640]{2,1,0:T(8,128)S(1)} %collective-permute-done.4.left_ref, bf16[160,5120]{1,0:T(8,128)(2,1)S(1)} %get-tuple-element.21.corrected_ref.corrected_other_ref, f32[40,128]{1,0:T(8,128)S(1)} %get-tuple-element.23.t_own_ref), custom_call_target="tpu_custom_call" | custom-call | flops 251658240 | bytes 3276800 | tf_op jit(solution)/shard_map/right/pallas_call | solution.py:212
  57.3 1.8 %collective-permute-start.7 = (f32[80,128]{1,0:T(8,128)S(1)}, f32[80,128]{1,0:T(8,128)S(1)}, u32[]{:S(2)}, u32[]{:S(2)}) collective-permute-start(f32[80,128]{1,0:T(8,128)S(1)} %get-tuple-element.24), channel_id=1, source_target_pairs={{0,32},{1,129},{2,34},{3,131},{4,36},{5,133},{6,38},{7,135},{8,40}... | collective-permute-start | bytes 122888 | tf_op jit(solution)/shard_map/right_sum/ppermute | solution.py:60
  59.0 1.3 %collective-permute-start.6 = (f32[80,128]{1,0:T(8,128)S(1)}, f32[80,128]{1,0:T(8,128)S(1)}, u32[]{:S(2)}, u32[]{:S(2)}) collective-permute-start(f32[80,128]{1,0:T(8,128)S(1)} %get-tuple-element.24), channel_id=1, source_target_pairs={{0,48},{1,193},{2,50},{3,195},{4,52},{5,197},{6,54},{7,199},{8,56}... | collective-permute-start | bytes 122888 | tf_op jit(solution)/shard_map/right_sum/ppermute | solution.py:60
  60.4 1.7 %collective-permute-start.5 = (f32[80,128]{1,0:T(8,128)S(1)}, f32[80,128]{1,0:T(8,128)S(1)}, u32[]{:S(2)}, u32[]{:S(2)}) collective-permute-start(f32[80,128]{1,0:T(8,128)S(1)} %get-tuple-element.24), channel_id=1, source_target_pairs={{0,16},{1,65},{2,18},{3,67},{4,20},{5,69},{6,22},{7,71},{8,24},{9,... | collective-permute-start | bytes 122888 | tf_op jit(solution)/shard_map/right_sum/ppermute | solution.py:60
  62.1 0.5 gram.1.gram_other_ref
  62.6 0.3 collective-permute-done.7
  62.9 0.4 collective-permute-done.6
  63.3 1.1 %collective-permute-done.5 = f32[80,128]{1,0:T(8,128)S(1)} collective-permute-done((f32[80,128]{1,0:T(8,128)S(1)}, f32[80,128]{1,0:T(8,128)S(1)}, u32[]{:S(2)}, u32[]{:S(2)}) %collective-permute-start.5) | collective-permute-done | bytes 40992 | tf_op jit(solution)/shard_map/right_sum/ppermute | solution.py:60
  64.4 1.4 %collective-permute-start.10 = (f32[80,128]{1,0:T(8,128)S(1)}, f32[80,128]{1,0:T(8,128)S(1)}, u32[]{:S(2)}, u32[]{:S(2)}) collective-permute-start(f32[80,128]{1,0:T(8,128)S(1)} %add_add_fusion.t0_ref), channel_id=1, source_target_pairs={{0,128},{1,33},{2,130},{3,35},{4,132},{5,37},{6,134},{7,39},{8,136... | collective-permute-start | bytes 122888 | tf_op jit(solution)/shard_map/right_sum/ppermute | solution.py:60
  65.8 1.9 %collective-permute-start.9 = (f32[80,128]{1,0:T(8,128)S(1)}, f32[80,128]{1,0:T(8,128)S(1)}, u32[]{:S(2)}, u32[]{:S(2)}) collective-permute-start(f32[80,128]{1,0:T(8,128)S(1)} %add_add_fusion.t0_ref), channel_id=1, source_target_pairs={{0,192},{1,49},{2,194},{3,51},{4,196},{5,53},{6,198},{7,55},{8,200... | collective-permute-start | bytes 122888 | tf_op jit(solution)/shard_map/right_sum/ppermute | solution.py:60
  67.7 0.2 collective-permute-start.8
  67.9 1.4 %inverse.1 = (f32[2,32,32]{2,1,0:T(8,128)S(1)}, f32[2,32,32]{2,1,0:T(8,128)S(1)}) custom-call(f32[32,32]{1,0:T(8,128)S(1)} %get-tuple-element.27.gram_own_ref, f32[32,32]{1,0:T(8,128)S(1)} %gram.1.gram_other_ref), custom_call_target="tpu_custom_call" | custom-call | flops 10000000 | bytes 8000000 | tf_op jit(solution)/shard_map/inverse/pallas_call | solution.py:269
  69.4 0.6 collective-permute-done.10.t3_ref
  70.0 1.0 %collective-permute-done.9.t2_ref = f32[80,128]{1,0:T(8,128)S(1)} collective-permute-done((f32[80,128]{1,0:T(8,128)S(1)}, f32[80,128]{1,0:T(8,128)S(1)}, u32[]{:S(2)}, u32[]{:S(2)}) %collective-permute-start.9) | collective-permute-done | bytes 40992 | tf_op jit(solution)/shard_map/right_sum/ppermute | solution.py:60
  71.0 0.7 collective-permute-done.8.t1_ref
  71.7 4.3 %final.1 = (bf16[2,160,5120]{2,1,0:T(8,128)(2,1)}, bf16[1,2,160,5120]{3,2,1,0:T(8,128)(2,1)}, f32[2,32,160]{2,1,0:T(8,128)}) custom-call(s32[1]{0:T(128)} %bitcast.m_ref.core_ref, f32[80,128]{1,0:T(8,128)S(1)} %add_add_fusion.t0_ref, f32[80,128]{1,0:T(8,128)S(1)} %collective-permute-done.8.t1_ref, f32[80,128]{1,0:T(8,128)S(1)} %collective-permute-done.9.t2_ref, ...), custom_call_target="tpu_custom_call" | custom-call | flops 629145600 | bytes 13107200 | tf_op jit(solution)/shard_map/final/pallas_call | solution.py:341
  (4 shorter events, 0.1 us)
Async XLA Ops:
  3.1 2.5 %collective-permute-start = (f32[32,8,640]{2,1,0:T(8,128)S(1)}, f32[32,8,640]{2,1,0:T(8,128)S(1)}, u32[]{:S(2)}, u32[]{:S(2)}) collective-permute-start(f32[32,8,640]{2,1,0:T(8,128)S(1)} %get-tuple-element.20), channel_id=1, source_target_pairs={{0,1},{1,0},{2,3},{3,2},{4,5},{5,4},{6,7},{7,6},{8,9},{9,8},{10,11... | collective-permute-start | bytes 1966088 | tf_op jit(solution)/shard_map/left_core_swap/ppermute | solution.py:60
  26.8 8.1 %collective-permute-start.3 = (f32[8,640]{1,0:T(8,128)S(1)}, f32[8,640]{1,0:T(8,128)S(1)}, u32[]{:S(2)}, u32[]{:S(2)}) collective-permute-start(f32[8,640]{1,0:T(8,128)S(1)} %add_up.1), channel_id=1, source_target_pairs={{0,8},{1,9},{2,10},{3,11},{4,12},{5,13},{6,14},{7,15},{8,0},{9,1},... | collective-permute-start | bytes 61448 | tf_op jit(solution)/shard_map/left_sum/ppermute | solution.py:60
  33.1 5.9 %collective-permute-start.2 = (f32[8,640]{1,0:T(8,128)S(1)}, f32[8,640]{1,0:T(8,128)S(1)}, u32[]{:S(2)}, u32[]{:S(2)}) collective-permute-start(f32[8,640]{1,0:T(8,128)S(1)} %add_up.1), channel_id=1, source_target_pairs={{0,12},{1,13},{2,14},{3,15},{4,8},{5,9},{6,10},{7,11},{8,4},{9,5},... | collective-permute-start | bytes 61448 | tf_op jit(solution)/shard_map/left_sum/ppermute | solution.py:60
  33.7 5.3 %collective-permute-start.1 = (f32[8,640]{1,0:T(8,128)S(1)}, f32[8,640]{1,0:T(8,128)S(1)}, u32[]{:S(2)}, u32[]{:S(2)}) collective-permute-start(f32[8,640]{1,0:T(8,128)S(1)} %add_up.1), channel_id=1, source_target_pairs={{0,4},{1,5},{2,6},{3,7},{4,0},{5,1},{6,2},{7,3},{8,12},{9,13},{10,... | collective-permute-start | bytes 61448 | tf_op jit(solution)/shard_map/left_sum/ppermute | solution.py:60
  54.4 2.1 %collective-permute-start.4 = (f32[32,8,640]{2,1,0:T(8,128)S(1)}, f32[32,8,640]{2,1,0:T(8,128)S(1)}, u32[]{:S(2)}, u32[]{:S(2)}) collective-permute-start(f32[32,8,640]{2,1,0:T(8,128)S(1)} %all_to_all.11.left_ref), channel_id=1, source_target_pairs={{0,1},{1,0},{2,3},{3,2},{4,5},{5,4},{6,7},{7,6},{8,9},{9,8},{10,11... | collective-permute-start | bytes 1966088 | tf_op jit(solution)/shard_map/left_sum/ppermute | solution.py:60
  57.3 5.6 %collective-permute-start.7 = (f32[80,128]{1,0:T(8,128)S(1)}, f32[80,128]{1,0:T(8,128)S(1)}, u32[]{:S(2)}, u32[]{:S(2)}) collective-permute-start(f32[80,128]{1,0:T(8,128)S(1)} %get-tuple-element.24), channel_id=1, source_target_pairs={{0,32},{1,129},{2,34},{3,131},{4,36},{5,133},{6,38},{7,135},{8,40}... | collective-permute-start | bytes 122888 | tf_op jit(solution)/shard_map/right_sum/ppermute | solution.py:60
  59.0 4.3 %collective-permute-start.6 = (f32[80,128]{1,0:T(8,128)S(1)}, f32[80,128]{1,0:T(8,128)S(1)}, u32[]{:S(2)}, u32[]{:S(2)}) collective-permute-start(f32[80,128]{1,0:T(8,128)S(1)} %get-tuple-element.24), channel_id=1, source_target_pairs={{0,48},{1,193},{2,50},{3,195},{4,52},{5,197},{6,54},{7,199},{8,56}... | collective-permute-start | bytes 122888 | tf_op jit(solution)/shard_map/right_sum/ppermute | solution.py:60
  60.4 4.0 %collective-permute-start.5 = (f32[80,128]{1,0:T(8,128)S(1)}, f32[80,128]{1,0:T(8,128)S(1)}, u32[]{:S(2)}, u32[]{:S(2)}) collective-permute-start(f32[80,128]{1,0:T(8,128)S(1)} %get-tuple-element.24), channel_id=1, source_target_pairs={{0,16},{1,65},{2,18},{3,67},{4,20},{5,69},{6,22},{7,71},{8,24},{9,... | collective-permute-start | bytes 122888 | tf_op jit(solution)/shard_map/right_sum/ppermute | solution.py:60
  64.4 5.6 %collective-permute-start.10 = (f32[80,128]{1,0:T(8,128)S(1)}, f32[80,128]{1,0:T(8,128)S(1)}, u32[]{:S(2)}, u32[]{:S(2)}) collective-permute-start(f32[80,128]{1,0:T(8,128)S(1)} %add_add_fusion.t0_ref), channel_id=1, source_target_pairs={{0,128},{1,33},{2,130},{3,35},{4,132},{5,37},{6,134},{7,39},{8,136... | collective-permute-start | bytes 122888 | tf_op jit(solution)/shard_map/right_sum/ppermute | solution.py:60
  65.8 5.2 %collective-permute-start.9 = (f32[80,128]{1,0:T(8,128)S(1)}, f32[80,128]{1,0:T(8,128)S(1)}, u32[]{:S(2)}, u32[]{:S(2)}) collective-permute-start(f32[80,128]{1,0:T(8,128)S(1)} %add_add_fusion.t0_ref), channel_id=1, source_target_pairs={{0,192},{1,49},{2,194},{3,51},{4,196},{5,53},{6,198},{7,55},{8,200... | collective-permute-start | bytes 122888 | tf_op jit(solution)/shard_map/right_sum/ppermute | solution.py:60
  67.7 4.0 %collective-permute-start.8 = (f32[80,128]{1,0:T(8,128)S(1)}, f32[80,128]{1,0:T(8,128)S(1)}, u32[]{:S(2)}, u32[]{:S(2)}) collective-permute-start(f32[80,128]{1,0:T(8,128)S(1)} %add_add_fusion.t0_ref), channel_id=1, source_target_pairs={{0,64},{1,17},{2,66},{3,19},{4,68},{5,21},{6,70},{7,23},{8,72},{9,... | collective-permute-start | bytes 122888 | tf_op jit(solution)/shard_map/right_sum/ppermute | solution.py:60

commit v5 on v4

--- a/solution.py
+++ b/solution.py
@@ -33,8 +33,13 @@
 CORE_SWAP = pairs(lambda x, y, z, c: (x, y, z, 1 - c))
 
 
-def z_pairs(k):
-    return pairs(lambda x, y, z, c: (x, y, z ^ (2 * k), c))
+def z_pairs(planes):
+    other = dict(planes + [(b, a) for a, b in planes])
+    return pairs(lambda x, y, z, c: (x, y, other[z], c))
+
+
+Z_NEAR = z_pairs([(1, 2), (3, 4), (5, 6), (7, 0)])
+Z_FAR = z_pairs([(1, 6), (2, 5), (0, 3), (4, 7)])
 
 
 def first_pairs(k):
@@ -46,7 +51,7 @@
 
 
 GROUPS = [
-    [device(x, y, zz * 2 + k, c) for k in range(2) for y in range(4) for x in range(4)]
+    [device(x, y, zz * 2 + (k ^ (zz & 1)), c) for k in range(2) for y in range(4) for x in range(4)]
     for zz in range(4)
     for c in range(2)
 ]
@@ -371,8 +376,8 @@
     with jax.named_scope("left_sum"):
         parts = exchange(left_own + arrived)
         part = add_up(parts)
-        p2, p3, p1 = (permute(part, z_pairs(k)) for k in (2, 3, 1))
-        part = (part + p1) + (p3 + p2)
+        part = part + permute(part, Z_NEAR)
+        part = part + permute(part, Z_FAR)
         left_own = exchange(jnp.broadcast_to(part[None], (CHUNKS,) + part.shape))
         left_other = permute(left_own, CORE_SWAP)
     t_own, terms_own, gram_own = right_part(left_own, corrected_own)

time: 76.3 us -> 75.6 us (level)
  waiting for transfers between devices: 9.56 us -> 10.6 us
  starting transfers between devices: 16.3 us -> 15.4 us
    ppermute x11 -> x10, waiting for transfers between devices: 9.56 us -> 10.6 us  [permute(): return lax.ppermute(a, AXES, perm)]
    ppermute x11 -> x10, starting transfers between devices: 16.3 us -> 15.4 us  [permute(): return lax.ppermute(a, AXES, perm)]
  transfers between devices with their start and end apart: 11 -> 10, of which waited for: 9 -> 9; matrix products, arithmetic and copies ran while one was open for 0% -> 0% of each run, Pallas kernels for 7% -> 7%
where the time goes in v5:
time: 75.6 us; the launch traced here: 75.4 us
  blocking collectives  35.7 us (47%)
  starting transfers between devices  15.4 us (20%)
  Pallas kernels  12.9 us (17%)
  waiting for transfers between devices  10.6 us (14%)
    all_to_all x2, blocking collectives, exchange(): lax.all_to_all(parts, AXES, 0, 0, axis_index_groups=GROUPS, tiled=True)  35.7 us
    ppermute x10, starting transfers between devices, permute(): return lax.ppermute(a, AXES, perm)  15.4 us
    ppermute x10, waiting for transfers between devices, permute(): return lax.ppermute(a, AXES, perm)  10.6 us
    pallas_call x2, Pallas kernels, left_part(): pl.pallas_call(left_kernel, in_specs=[pl.BlockSpec(memory_space=pltpu.SME...  4.8 us
    pallas_call x1, Pallas kernels, final_part(): pl.pallas_call(final_kernel, in_specs=[pl.BlockSpec(memory_space=pltpu.SM...  4.26 us
    pallas_call x2, Pallas kernels, right_part(): pl.pallas_call(right_own_kernel if own else right_other_kernel, in_specs=...  1.85 us
  transfers between devices with their start and end apart: 10, of which 9 were waited for; matrix products, arithmetic and copies ran while one was open for 0% of the time, Pallas kernels for 7%

profile of v5, /device:TPU:2, one launch (start us, length us, event | category | flops | bytes accessed | tf_op | source)
XLA Modules:
  0.0 75.4 jit_solution(10079734282269057144)
XLA Ops:
  0.6 2.4 %left.3 = (bf16[160,5120]{1,0:T(8,128)(2,1)S(1)}, f32[32,8,640]{2,1,0:T(8,128)S(1)}) custom-call(s32[1]{0:T(128)} %bitcast.2.m_ref, bf16[1,2,160,5120]{3,2,1,0:T(8,128)(2,1)} %grads_ref.3, bf16[1,2,160,5120]{3,2,1,0:T(8,128)(2,1)} %errors_ref.3, f32[2,32,160]{2,1,0:T(8,128)} %bitcast.4), custom_call_target="tpu_custom_call" | custom-call | flops 52428800 | bytes 5570560 | tf_op jit(solution)/shard_map/left/pallas_call | solution.py:123
  3.1 0.1 collective-permute-start
  3.2 2.4 %left.2 = (bf16[160,5120]{1,0:T(8,128)(2,1)S(1)}, f32[32,8,640]{2,1,0:T(8,128)S(1)}) custom-call(s32[1]{0:T(128)} %bitcast.m_ref.core_ref, bf16[1,2,160,5120]{3,2,1,0:T(8,128)(2,1)} %grads_ref.3, bf16[1,2,160,5120]{3,2,1,0:T(8,128)(2,1)} %errors_ref.3, f32[2,32,160]{2,1,0:T(8,128)} %bitcast.5), custom_call_target="tpu_custom_call" | custom-call | flops 52428800 | bytes 5570560 | tf_op jit(solution)/shard_map/left/pallas_call | solution.py:123
  5.5 0.0 collective-permute-done
  5.6 0.1 add.18
  5.6 21.1 %all_to_all.10.parts_ref = f32[32,8,640]{2,1,0:T(8,128)S(1)} all-to-all(f32[32,8,640]{2,1,0:T(8,128)S(1)} %add.18), channel_id=1, replica_groups={{0,16,32,48,64,80,96,112,128,144,160,176,192,208,224,240,2,18,34,50,66,..., dimensions={0} | all-to-all | bytes 1310720 | tf_op jit(solution)/shard_map/left_sum/all_to_all | solution.py:61
  26.8 5.0 %collective-permute-start.1 = (f32[8,640]{1,0:T(8,128)S(1)}, f32[8,640]{1,0:T(8,128)S(1)}, u32[]{:S(2)}, u32[]{:S(2)}) collective-permute-start(f32[8,640]{1,0:T(8,128)S(1)} %add_up.1), channel_id=1, source_target_pairs={{0,14},{1,15},{2,4},{3,5},{4,2},{5,3},{6,8},{7,9},{8,6},{9,7},{10,... | collective-permute-start | bytes 61448 | tf_op jit(solution)/shard_map/left_sum/ppermute | solution.py:65
  31.8 1.8 %collective-permute-done.1 = f32[8,640]{1,0:T(8,128)S(1)} collective-permute-done((f32[8,640]{1,0:T(8,128)S(1)}, f32[8,640]{1,0:T(8,128)S(1)}, u32[]{:S(2)}, u32[]{:S(2)}) %collective-permute-start.1) | collective-permute-done | bytes 20512 | tf_op jit(solution)/shard_map/left_sum/ppermute | solution.py:65
  33.6 1.9 %collective-permute-start.2 = (f32[8,640]{1,0:T(8,128)S(1)}, f32[8,640]{1,0:T(8,128)S(1)}, u32[]{:S(2)}, u32[]{:S(2)}) collective-permute-start(f32[8,640]{1,0:T(8,128)S(1)} %add.19), channel_id=1, source_target_pairs={{0,6},{1,7},{2,12},{3,13},{4,10},{5,11},{6,0},{7,1},{8,14},{9,15},... | collective-permute-start | bytes 61448 | tf_op jit(solution)/shard_map/left_sum/ppermute | solution.py:65
  35.5 3.7 %collective-permute-done.2 = f32[8,640]{1,0:T(8,128)S(1)} collective-permute-done((f32[8,640]{1,0:T(8,128)S(1)}, f32[8,640]{1,0:T(8,128)S(1)}, u32[]{:S(2)}, u32[]{:S(2)}) %collective-permute-start.2) | collective-permute-done | bytes 20512 | tf_op jit(solution)/shard_map/left_sum/ppermute | solution.py:65
  39.2 14.6 %all_to_all.11.left_ref = f32[32,8,640]{2,1,0:T(8,128)S(1)} all-to-all(f32[32,8,640]{2,1,0:T(8,128)S(1)} %broadcast_in_dim.15), channel_id=1, replica_groups={{0,16,32,48,64,80,96,112,128,144,160,176,192,208,224,240,2,18,34,50,66,..., dimensions={0} | all-to-all | bytes 1310720 | tf_op jit(solution)/shard_map/left_sum/all_to_all | solution.py:61
  53.8 0.0 collective-permute-start.3
  53.8 1.1 %right.2 = (f32[40,128]{1,0:T(8,128)S(1)}, bf16[96,5120]{1,0:T(8,128)(2,1)S(1)}, f32[32,32]{1,0:T(8,128)S(1)}) custom-call(f32[32,8,640]{2,1,0:T(8,128)S(1)} %all_to_all.11.left_ref, bf16[160,5120]{1,0:T(8,128)(2,1)S(1)} %get-tuple-element.22.corrected_ref.corrected_own_ref), custom_call_target="tpu_custom_call" | custom-call | flops 251658240 | bytes 3276800 | tf_op jit(solution)/shard_map/right/pallas_call | solution.py:217
  54.9 1.0 %collective-permute-done.3.left_ref = f32[32,8,640]{2,1,0:T(8,128)S(1)} collective-permute-done((f32[32,8,640]{2,1,0:T(8,128)S(1)}, f32[32,8,640]{2,1,0:T(8,128)S(1)}, u32[]{:S(2)}, u32[]{:S(2)}) %collective-permute-start.3) | collective-permute-done | bytes 655392 | tf_op jit(solution)/shard_map/left_sum/ppermute | solution.py:65
  55.9 0.8 %right.3 = (f32[80,128]{1,0:T(8,128)S(1)}, bf16[96,5120]{1,0:T(8,128)(2,1)S(1)}) custom-call(f32[32,8,640]{2,1,0:T(8,128)S(1)} %collective-permute-done.3.left_ref, bf16[160,5120]{1,0:T(8,128)(2,1)S(1)} %get-tuple-element.21.corrected_ref.corrected_other_ref, f32[40,128]{1,0:T(8,128)S(1)} %get-tuple-element.23.t_own_ref), custom_call_target="tpu_custom_call" | custom-call | flops 251658240 | bytes 3276800 | tf_op jit(solution)/shard_map/right/pallas_call | solution.py:217
  56.7 1.7 %collective-permute-start.6 = (f32[80,128]{1,0:T(8,128)S(1)}, f32[80,128]{1,0:T(8,128)S(1)}, u32[]{:S(2)}, u32[]{:S(2)}) collective-permute-start(f32[80,128]{1,0:T(8,128)S(1)} %get-tuple-element.24), channel_id=1, source_target_pairs={{0,32},{1,129},{2,34},{3,131},{4,36},{5,133},{6,38},{7,135},{8,40}... | collective-permute-start | bytes 122888 | tf_op jit(solution)/shard_map/right_sum/ppermute | solution.py:65
  58.4 1.3 %collective-permute-start.5 = (f32[80,128]{1,0:T(8,128)S(1)}, f32[80,128]{1,0:T(8,128)S(1)}, u32[]{:S(2)}, u32[]{:S(2)}) collective-permute-start(f32[80,128]{1,0:T(8,128)S(1)} %get-tuple-element.24), channel_id=1, source_target_pairs={{0,48},{1,193},{2,50},{3,195},{4,52},{5,197},{6,54},{7,199},{8,56}... | collective-permute-start | bytes 122888 | tf_op jit(solution)/shard_map/right_sum/ppermute | solution.py:65
  59.8 1.7 %collective-permute-start.4 = (f32[80,128]{1,0:T(8,128)S(1)}, f32[80,128]{1,0:T(8,128)S(1)}, u32[]{:S(2)}, u32[]{:S(2)}) collective-permute-start(f32[80,128]{1,0:T(8,128)S(1)} %get-tuple-element.24), channel_id=1, source_target_pairs={{0,16},{1,65},{2,18},{3,67},{4,20},{5,69},{6,22},{7,71},{8,24},{9,... | collective-permute-start | bytes 122888 | tf_op jit(solution)/shard_map/right_sum/ppermute | solution.py:65
  61.5 0.5 gram.1.gram_other_ref
  62.0 0.3 collective-permute-done.6
  62.3 0.4 collective-permute-done.5
  62.7 1.1 %collective-permute-done.4 = f32[80,128]{1,0:T(8,128)S(1)} collective-permute-done((f32[80,128]{1,0:T(8,128)S(1)}, f32[80,128]{1,0:T(8,128)S(1)}, u32[]{:S(2)}, u32[]{:S(2)}) %collective-permute-start.4) | collective-permute-done | bytes 40992 | tf_op jit(solution)/shard_map/right_sum/ppermute | solution.py:65
  63.8 1.4 %collective-permute-start.9 = (f32[80,128]{1,0:T(8,128)S(1)}, f32[80,128]{1,0:T(8,128)S(1)}, u32[]{:S(2)}, u32[]{:S(2)}) collective-permute-start(f32[80,128]{1,0:T(8,128)S(1)} %add_add_fusion.t0_ref), channel_id=1, source_target_pairs={{0,128},{1,33},{2,130},{3,35},{4,132},{5,37},{6,134},{7,39},{8,136... | collective-permute-start | bytes 122888 | tf_op jit(solution)/shard_map/right_sum/ppermute | solution.py:65
  65.2 1.9 %collective-permute-start.8 = (f32[80,128]{1,0:T(8,128)S(1)}, f32[80,128]{1,0:T(8,128)S(1)}, u32[]{:S(2)}, u32[]{:S(2)}) collective-permute-start(f32[80,128]{1,0:T(8,128)S(1)} %add_add_fusion.t0_ref), channel_id=1, source_target_pairs={{0,192},{1,49},{2,194},{3,51},{4,196},{5,53},{6,198},{7,55},{8,200... | collective-permute-start | bytes 122888 | tf_op jit(solution)/shard_map/right_sum/ppermute | solution.py:65
  67.1 0.2 collective-permute-start.7
  67.4 1.4 %inverse.1 = (f32[2,32,32]{2,1,0:T(8,128)S(1)}, f32[2,32,32]{2,1,0:T(8,128)S(1)}) custom-call(f32[32,32]{1,0:T(8,128)S(1)} %get-tuple-element.27.gram_own_ref, f32[32,32]{1,0:T(8,128)S(1)} %gram.1.gram_other_ref), custom_call_target="tpu_custom_call" | custom-call | flops 10000000 | bytes 8000000 | tf_op jit(solution)/shard_map/inverse/pallas_call | solution.py:274
  68.8 0.6 collective-permute-done.9.t3_ref
  69.4 1.0 %collective-permute-done.8.t2_ref = f32[80,128]{1,0:T(8,128)S(1)} collective-permute-done((f32[80,128]{1,0:T(8,128)S(1)}, f32[80,128]{1,0:T(8,128)S(1)}, u32[]{:S(2)}, u32[]{:S(2)}) %collective-permute-start.8) | collective-permute-done | bytes 40992 | tf_op jit(solution)/shard_map/right_sum/ppermute | solution.py:65
  70.4 0.7 collective-permute-done.7.t1_ref
  71.1 4.3 %final.1 = (bf16[2,160,5120]{2,1,0:T(8,128)(2,1)}, bf16[1,2,160,5120]{3,2,1,0:T(8,128)(2,1)}, f32[2,32,160]{2,1,0:T(8,128)}) custom-call(s32[1]{0:T(128)} %bitcast.m_ref.core_ref, f32[80,128]{1,0:T(8,128)S(1)} %add_add_fusion.t0_ref, f32[80,128]{1,0:T(8,128)S(1)} %collective-permute-done.7.t1_ref, f32[80,128]{1,0:T(8,128)S(1)} %collective-permute-done.8.t2_ref, ...), custom_call_target="tpu_custom_call" | custom-call | flops 629145600 | bytes 13107200 | tf_op jit(solution)/shard_map/final/pallas_call | solution.py:346
  (5 shorter events, 0.1 us)
Async XLA Ops:
  3.1 2.5 %collective-permute-start = (f32[32,8,640]{2,1,0:T(8,128)S(1)}, f32[32,8,640]{2,1,0:T(8,128)S(1)}, u32[]{:S(2)}, u32[]{:S(2)}) collective-permute-start(f32[32,8,640]{2,1,0:T(8,128)S(1)} %get-tuple-element.20), channel_id=1, source_target_pairs={{0,1},{1,0},{2,3},{3,2},{4,5},{5,4},{6,7},{7,6},{8,9},{9,8},{10,11... | collective-permute-start | bytes 1966088 | tf_op jit(solution)/shard_map/left_core_swap/ppermute | solution.py:65
  26.8 6.8 %collective-permute-start.1 = (f32[8,640]{1,0:T(8,128)S(1)}, f32[8,640]{1,0:T(8,128)S(1)}, u32[]{:S(2)}, u32[]{:S(2)}) collective-permute-start(f32[8,640]{1,0:T(8,128)S(1)} %add_up.1), channel_id=1, source_target_pairs={{0,14},{1,15},{2,4},{3,5},{4,2},{5,3},{6,8},{7,9},{8,6},{9,7},{10,... | collective-permute-start | bytes 61448 | tf_op jit(solution)/shard_map/left_sum/ppermute | solution.py:65
  33.6 5.6 %collective-permute-start.2 = (f32[8,640]{1,0:T(8,128)S(1)}, f32[8,640]{1,0:T(8,128)S(1)}, u32[]{:S(2)}, u32[]{:S(2)}) collective-permute-start(f32[8,640]{1,0:T(8,128)S(1)} %add.19), channel_id=1, source_target_pairs={{0,6},{1,7},{2,12},{3,13},{4,10},{5,11},{6,0},{7,1},{8,14},{9,15},... | collective-permute-start | bytes 61448 | tf_op jit(solution)/shard_map/left_sum/ppermute | solution.py:65
  53.8 2.1 %collective-permute-start.3 = (f32[32,8,640]{2,1,0:T(8,128)S(1)}, f32[32,8,640]{2,1,0:T(8,128)S(1)}, u32[]{:S(2)}, u32[]{:S(2)}) collective-permute-start(f32[32,8,640]{2,1,0:T(8,128)S(1)} %all_to_all.11.left_ref), channel_id=1, source_target_pairs={{0,1},{1,0},{2,3},{3,2},{4,5},{5,4},{6,7},{7,6},{8,9},{9,8},{10,11... | collective-permute-start | bytes 1966088 | tf_op jit(solution)/shard_map/left_sum/ppermute | solution.py:65
  56.7 5.6 %collective-permute-start.6 = (f32[80,128]{1,0:T(8,128)S(1)}, f32[80,128]{1,0:T(8,128)S(1)}, u32[]{:S(2)}, u32[]{:S(2)}) collective-permute-start(f32[80,128]{1,0:T(8,128)S(1)} %get-tuple-element.24), channel_id=1, source_target_pairs={{0,32},{1,129},{2,34},{3,131},{4,36},{5,133},{6,38},{7,135},{8,40}... | collective-permute-start | bytes 122888 | tf_op jit(solution)/shard_map/right_sum/ppermute | solution.py:65
  58.4 4.3 %collective-permute-start.5 = (f32[80,128]{1,0:T(8,128)S(1)}, f32[80,128]{1,0:T(8,128)S(1)}, u32[]{:S(2)}, u32[]{:S(2)}) collective-permute-start(f32[80,128]{1,0:T(8,128)S(1)} %get-tuple-element.24), channel_id=1, source_target_pairs={{0,48},{1,193},{2,50},{3,195},{4,52},{5,197},{6,54},{7,199},{8,56}... | collective-permute-start | bytes 122888 | tf_op jit(solution)/shard_map/right_sum/ppermute | solution.py:65
  59.8 4.0 %collective-permute-start.4 = (f32[80,128]{1,0:T(8,128)S(1)}, f32[80,128]{1,0:T(8,128)S(1)}, u32[]{:S(2)}, u32[]{:S(2)}) collective-permute-start(f32[80,128]{1,0:T(8,128)S(1)} %get-tuple-element.24), channel_id=1, source_target_pairs={{0,16},{1,65},{2,18},{3,67},{4,20},{5,69},{6,22},{7,71},{8,24},{9,... | collective-permute-start | bytes 122888 | tf_op jit(solution)/shard_map/right_sum/ppermute | solution.py:65
  63.8 5.6 %collective-permute-start.9 = (f32[80,128]{1,0:T(8,128)S(1)}, f32[80,128]{1,0:T(8,128)S(1)}, u32[]{:S(2)}, u32[]{:S(2)}) collective-permute-start(f32[80,128]{1,0:T(8,128)S(1)} %add_add_fusion.t0_ref), channel_id=1, source_target_pairs={{0,128},{1,33},{2,130},{3,35},{4,132},{5,37},{6,134},{7,39},{8,136... | collective-permute-start | bytes 122888 | tf_op jit(solution)/shard_map/right_sum/ppermute | solution.py:65
  65.2 5.2 %collective-permute-start.8 = (f32[80,128]{1,0:T(8,128)S(1)}, f32[80,128]{1,0:T(8,128)S(1)}, u32[]{:S(2)}, u32[]{:S(2)}) collective-permute-start(f32[80,128]{1,0:T(8,128)S(1)} %add_add_fusion.t0_ref), channel_id=1, source_target_pairs={{0,192},{1,49},{2,194},{3,51},{4,196},{5,53},{6,198},{7,55},{8,200... | collective-permute-start | bytes 122888 | tf_op jit(solution)/shard_map/right_sum/ppermute | solution.py:65
  67.1 4.0 %collective-permute-start.7 = (f32[80,128]{1,0:T(8,128)S(1)}, f32[80,128]{1,0:T(8,128)S(1)}, u32[]{:S(2)}, u32[]{:S(2)}) collective-permute-start(f32[80,128]{1,0:T(8,128)S(1)} %add_add_fusion.t0_ref), channel_id=1, source_target_pairs={{0,64},{1,17},{2,66},{3,19},{4,68},{5,21},{6,70},{7,23},{8,72},{9,... | collective-permute-start | bytes 122888 | tf_op jit(solution)/shard_map/right_sum/ppermute | solution.py:65

commit v6 on v5

--- a/solution.py
+++ b/solution.py
@@ -304,16 +304,19 @@
     core = core_ref[0]
     t = (t0_ref[...] + t1_ref[...]) + (t2_ref[...] + t3_ref[...])
     t = t * (1.0 / HOSTS)
-    copies, rights = [], []
+    copies, rights, ws = [], [], []
     for n in range(2):
         m = core if n == 0 else 1 - core
-        terms_ref = (terms_own_ref, terms_other_ref)[n]
-        corrected_ref = (corrected_own_ref, corrected_other_ref)[n]
         mine = t[40 * n : 40 * n + 40]
         mine = jnp.concatenate([mine[:, RANK * q : RANK * q + RANK] for q in range(4)], axis=0)
         rights.append((m, mine, inverse_ref[n]))
         hi, mid, lo = split3(high(mine, gram_inverse_ref[n], (((1,), (0,)), ((), ()))))
-        w = jnp.concatenate([hi, hi, hi, mid, mid, lo], axis=1)
+        ws.append(jnp.concatenate([hi, hi, hi, mid, mid, lo], axis=1))
+    for n in range(2):
+        m = core if n == 0 else 1 - core
+        w = ws[n]
+        terms_ref = (terms_own_ref, terms_other_ref)[n]
+        corrected_ref = (corrected_own_ref, corrected_other_ref)[n]
         for b in range(COL_BLOCKS):
             cols = slice(b * CHUNK_COLS, (b + 1) * CHUNK_COLS)
             hi, mid, lo = (terms_ref[i * RANK : (i + 1) * RANK, cols] for i in range(3))
@@ -376,8 +379,8 @@
     with jax.named_scope("left_sum"):
         parts = exchange(left_own + arrived)
         part = add_up(parts)
+        part = part + permute(part, Z_FAR)
         part = part + permute(part, Z_NEAR)
-        part = part + permute(part, Z_FAR)
         left_own = exchange(jnp.broadcast_to(part[None], (CHUNKS,) + part.shape))
         left_other = permute(left_own, CORE_SWAP)
     t_own, terms_own, gram_own = right_part(left_own, corrected_own)

time: 75.6 us -> 75.5 us (level)
  starting transfers between devices: 15.4 us -> 17 us
  waiting for transfers between devices: 10.6 us -> 9.22 us
    ppermute x10, starting transfers between devices: 15.4 us -> 17 us  [permute(): return lax.ppermute(a, AXES, perm)]
    ppermute x10, waiting for transfers between devices: 10.6 us -> 9.22 us  [permute(): return lax.ppermute(a, AXES, perm)]
where the time goes in v6:
time: 75.5 us; the launch traced here: 75.4 us
  blocking collectives  35.4 us (47%)
  starting transfers between devices  17 us (23%)
  Pallas kernels  12.9 us (17%)
  waiting for transfers between devices  9.22 us (12%)
    all_to_all x2, blocking collectives, exchange(): lax.all_to_all(parts, AXES, 0, 0, axis_index_groups=GROUPS, tiled=True)  35.4 us
    ppermute x10, starting transfers between devices, permute(): return lax.ppermute(a, AXES, perm)  17 us
    ppermute x10, waiting for transfers between devices, permute(): return lax.ppermute(a, AXES, perm)  9.22 us
    pallas_call x2, Pallas kernels, left_part(): pl.pallas_call(left_kernel, in_specs=[pl.BlockSpec(memory_space=pltpu.SME...  4.8 us
    pallas_call x1, Pallas kernels, final_part(): pl.pallas_call(final_kernel, in_specs=[pl.BlockSpec(memory_space=pltpu.SM...  4.22 us
    pallas_call x2, Pallas kernels, right_part(): pl.pallas_call(right_own_kernel if own else right_other_kernel, in_specs=...  1.85 us
  transfers between devices with their start and end apart: 10, of which 9 were waited for; matrix products, arithmetic and copies ran while one was open for 0% of the time, Pallas kernels for 7%

profile of v6, /device:TPU:2, one launch (start us, length us, event | category | flops | bytes accessed | tf_op | source)
XLA Modules:
  0.0 75.4 jit_solution(5223030162865597154)
XLA Ops:
  0.6 2.4 %left.3 = (bf16[160,5120]{1,0:T(8,128)(2,1)S(1)}, f32[32,8,640]{2,1,0:T(8,128)S(1)}) custom-call(s32[1]{0:T(128)} %bitcast.2.m_ref, bf16[1,2,160,5120]{3,2,1,0:T(8,128)(2,1)} %grads_ref.3, bf16[1,2,160,5120]{3,2,1,0:T(8,128)(2,1)} %errors_ref.3, f32[2,32,160]{2,1,0:T(8,128)} %bitcast.4), custom_call_target="tpu_custom_call" | custom-call | flops 52428800 | bytes 5570560 | tf_op jit(solution)/shard_map/left/pallas_call | solution.py:123
  3.1 0.1 collective-permute-start
  3.2 2.4 %left.2 = (bf16[160,5120]{1,0:T(8,128)(2,1)S(1)}, f32[32,8,640]{2,1,0:T(8,128)S(1)}) custom-call(s32[1]{0:T(128)} %bitcast.m_ref.core_ref, bf16[1,2,160,5120]{3,2,1,0:T(8,128)(2,1)} %grads_ref.3, bf16[1,2,160,5120]{3,2,1,0:T(8,128)(2,1)} %errors_ref.3, f32[2,32,160]{2,1,0:T(8,128)} %bitcast.5), custom_call_target="tpu_custom_call" | custom-call | flops 52428800 | bytes 5570560 | tf_op jit(solution)/shard_map/left/pallas_call | solution.py:123
  5.5 0.0 collective-permute-done
  5.6 0.1 add.18
  5.6 21.1 %all_to_all.10.parts_ref = f32[32,8,640]{2,1,0:T(8,128)S(1)} all-to-all(f32[32,8,640]{2,1,0:T(8,128)S(1)} %add.18), channel_id=1, replica_groups={{0,16,32,48,64,80,96,112,128,144,160,176,192,208,224,240,2,18,34,50,66,..., dimensions={0} | all-to-all | bytes 1310720 | tf_op jit(solution)/shard_map/left_sum/all_to_all | solution.py:61
  26.8 3.4 %collective-permute-start.1 = (f32[8,640]{1,0:T(8,128)S(1)}, f32[8,640]{1,0:T(8,128)S(1)}, u32[]{:S(2)}, u32[]{:S(2)}) collective-permute-start(f32[8,640]{1,0:T(8,128)S(1)} %add_up.1), channel_id=1, source_target_pairs={{0,6},{1,7},{2,12},{3,13},{4,10},{5,11},{6,0},{7,1},{8,14},{9,15},... | collective-permute-start | bytes 61448 | tf_op jit(solution)/shard_map/left_sum/ppermute | solution.py:65
  30.1 2.3 %collective-permute-done.1 = f32[8,640]{1,0:T(8,128)S(1)} collective-permute-done((f32[8,640]{1,0:T(8,128)S(1)}, f32[8,640]{1,0:T(8,128)S(1)}, u32[]{:S(2)}, u32[]{:S(2)}) %collective-permute-start.1) | collective-permute-done | bytes 20512 | tf_op jit(solution)/shard_map/left_sum/ppermute | solution.py:65
  32.4 5.2 %collective-permute-start.2 = (f32[8,640]{1,0:T(8,128)S(1)}, f32[8,640]{1,0:T(8,128)S(1)}, u32[]{:S(2)}, u32[]{:S(2)}) collective-permute-start(f32[8,640]{1,0:T(8,128)S(1)} %add.19), channel_id=1, source_target_pairs={{0,14},{1,15},{2,4},{3,5},{4,2},{5,3},{6,8},{7,9},{8,6},{9,7},{10,... | collective-permute-start | bytes 61448 | tf_op jit(solution)/shard_map/left_sum/ppermute | solution.py:65
  37.6 1.8 %collective-permute-done.2 = f32[8,640]{1,0:T(8,128)S(1)} collective-permute-done((f32[8,640]{1,0:T(8,128)S(1)}, f32[8,640]{1,0:T(8,128)S(1)}, u32[]{:S(2)}, u32[]{:S(2)}) %collective-permute-start.2) | collective-permute-done | bytes 20512 | tf_op jit(solution)/shard_map/left_sum/ppermute | solution.py:65
  39.4 14.3 %all_to_all.11.left_ref = f32[32,8,640]{2,1,0:T(8,128)S(1)} all-to-all(f32[32,8,640]{2,1,0:T(8,128)S(1)} %broadcast_in_dim.15), channel_id=1, replica_groups={{0,16,32,48,64,80,96,112,128,144,160,176,192,208,224,240,2,18,34,50,66,..., dimensions={0} | all-to-all | bytes 1310720 | tf_op jit(solution)/shard_map/left_sum/all_to_all | solution.py:61
  53.8 0.0 collective-permute-start.3
  53.8 1.1 %right.2 = (f32[40,128]{1,0:T(8,128)S(1)}, bf16[96,5120]{1,0:T(8,128)(2,1)S(1)}, f32[32,32]{1,0:T(8,128)S(1)}) custom-call(f32[32,8,640]{2,1,0:T(8,128)S(1)} %all_to_all.11.left_ref, bf16[160,5120]{1,0:T(8,128)(2,1)S(1)} %get-tuple-element.22.corrected_ref.corrected_own_ref), custom_call_target="tpu_custom_call" | custom-call | flops 251658240 | bytes 3276800 | tf_op jit(solution)/shard_map/right/pallas_call | solution.py:217
  54.8 1.0 %collective-permute-done.3.left_ref = f32[32,8,640]{2,1,0:T(8,128)S(1)} collective-permute-done((f32[32,8,640]{2,1,0:T(8,128)S(1)}, f32[32,8,640]{2,1,0:T(8,128)S(1)}, u32[]{:S(2)}, u32[]{:S(2)}) %collective-permute-start.3) | collective-permute-done | bytes 655392 | tf_op jit(solution)/shard_map/left_sum/ppermute | solution.py:65
  55.9 0.8 %right.3 = (f32[80,128]{1,0:T(8,128)S(1)}, bf16[96,5120]{1,0:T(8,128)(2,1)S(1)}) custom-call(f32[32,8,640]{2,1,0:T(8,128)S(1)} %collective-permute-done.3.left_ref, bf16[160,5120]{1,0:T(8,128)(2,1)S(1)} %get-tuple-element.21.corrected_ref.corrected_other_ref, f32[40,128]{1,0:T(8,128)S(1)} %get-tuple-element.23.t_own_ref), custom_call_target="tpu_custom_call" | custom-call | flops 251658240 | bytes 3276800 | tf_op jit(solution)/shard_map/right/pallas_call | solution.py:217
  56.7 1.8 %collective-permute-start.6 = (f32[80,128]{1,0:T(8,128)S(1)}, f32[80,128]{1,0:T(8,128)S(1)}, u32[]{:S(2)}, u32[]{:S(2)}) collective-permute-start(f32[80,128]{1,0:T(8,128)S(1)} %get-tuple-element.24), channel_id=1, source_target_pairs={{0,32},{1,129},{2,34},{3,131},{4,36},{5,133},{6,38},{7,135},{8,40}... | collective-permute-start | bytes 122888 | tf_op jit(solution)/shard_map/right_sum/ppermute | solution.py:65
  58.4 1.3 %collective-permute-start.5 = (f32[80,128]{1,0:T(8,128)S(1)}, f32[80,128]{1,0:T(8,128)S(1)}, u32[]{:S(2)}, u32[]{:S(2)}) collective-permute-start(f32[80,128]{1,0:T(8,128)S(1)} %get-tuple-element.24), channel_id=1, source_target_pairs={{0,48},{1,193},{2,50},{3,195},{4,52},{5,197},{6,54},{7,199},{8,56}... | collective-permute-start | bytes 122888 | tf_op jit(solution)/shard_map/right_sum/ppermute | solution.py:65
  59.8 1.7 %collective-permute-start.4 = (f32[80,128]{1,0:T(8,128)S(1)}, f32[80,128]{1,0:T(8,128)S(1)}, u32[]{:S(2)}, u32[]{:S(2)}) collective-permute-start(f32[80,128]{1,0:T(8,128)S(1)} %get-tuple-element.24), channel_id=1, source_target_pairs={{0,16},{1,65},{2,18},{3,67},{4,20},{5,69},{6,22},{7,71},{8,24},{9,... | collective-permute-start | bytes 122888 | tf_op jit(solution)/shard_map/right_sum/ppermute | solution.py:65
  61.5 0.5 gram.1.gram_other_ref
  62.0 0.3 collective-permute-done.6
  62.3 0.4 collective-permute-done.5
  62.7 1.1 %collective-permute-done.4 = f32[80,128]{1,0:T(8,128)S(1)} collective-permute-done((f32[80,128]{1,0:T(8,128)S(1)}, f32[80,128]{1,0:T(8,128)S(1)}, u32[]{:S(2)}, u32[]{:S(2)}) %collective-permute-start.4) | collective-permute-done | bytes 40992 | tf_op jit(solution)/shard_map/right_sum/ppermute | solution.py:65
  63.8 1.4 %collective-permute-start.9 = (f32[80,128]{1,0:T(8,128)S(1)}, f32[80,128]{1,0:T(8,128)S(1)}, u32[]{:S(2)}, u32[]{:S(2)}) collective-permute-start(f32[80,128]{1,0:T(8,128)S(1)} %add_add_fusion.t0_ref), channel_id=1, source_target_pairs={{0,128},{1,33},{2,130},{3,35},{4,132},{5,37},{6,134},{7,39},{8,136... | collective-permute-start | bytes 122888 | tf_op jit(solution)/shard_map/right_sum/ppermute | solution.py:65
  65.2 1.9 %collective-permute-start.8 = (f32[80,128]{1,0:T(8,128)S(1)}, f32[80,128]{1,0:T(8,128)S(1)}, u32[]{:S(2)}, u32[]{:S(2)}) collective-permute-start(f32[80,128]{1,0:T(8,128)S(1)} %add_add_fusion.t0_ref), channel_id=1, source_target_pairs={{0,192},{1,49},{2,194},{3,51},{4,196},{5,53},{6,198},{7,55},{8,200... | collective-permute-start | bytes 122888 | tf_op jit(solution)/shard_map/right_sum/ppermute | solution.py:65
  67.1 0.2 collective-permute-start.7
  67.4 1.4 %inverse.1 = (f32[2,32,32]{2,1,0:T(8,128)S(1)}, f32[2,32,32]{2,1,0:T(8,128)S(1)}) custom-call(f32[32,32]{1,0:T(8,128)S(1)} %get-tuple-element.27.gram_own_ref, f32[32,32]{1,0:T(8,128)S(1)} %gram.1.gram_other_ref), custom_call_target="tpu_custom_call" | custom-call | flops 10000000 | bytes 8000000 | tf_op jit(solution)/shard_map/inverse/pallas_call | solution.py:274
  68.8 0.6 collective-permute-done.9.t3_ref
  69.4 1.0 %collective-permute-done.8.t2_ref = f32[80,128]{1,0:T(8,128)S(1)} collective-permute-done((f32[80,128]{1,0:T(8,128)S(1)}, f32[80,128]{1,0:T(8,128)S(1)}, u32[]{:S(2)}, u32[]{:S(2)}) %collective-permute-start.8) | collective-permute-done | bytes 40992 | tf_op jit(solution)/shard_map/right_sum/ppermute | solution.py:65
  70.4 0.7 collective-permute-done.7.t1_ref
  71.1 4.2 %final.1 = (bf16[2,160,5120]{2,1,0:T(8,128)(2,1)}, bf16[1,2,160,5120]{3,2,1,0:T(8,128)(2,1)}, f32[2,32,160]{2,1,0:T(8,128)}) custom-call(s32[1]{0:T(128)} %bitcast.m_ref.core_ref, f32[80,128]{1,0:T(8,128)S(1)} %add_add_fusion.t0_ref, f32[80,128]{1,0:T(8,128)S(1)} %collective-permute-done.7.t1_ref, f32[80,128]{1,0:T(8,128)S(1)} %collective-permute-done.8.t2_ref, ...), custom_call_target="tpu_custom_call" | custom-call | flops 629145600 | bytes 13107200 | tf_op jit(solution)/shard_map/final/pallas_call | solution.py:349
  (5 shorter events, 0.1 us)
Async XLA Ops:
  3.1 2.5 %collective-permute-start = (f32[32,8,640]{2,1,0:T(8,128)S(1)}, f32[32,8,640]{2,1,0:T(8,128)S(1)}, u32[]{:S(2)}, u32[]{:S(2)}) collective-permute-start(f32[32,8,640]{2,1,0:T(8,128)S(1)} %get-tuple-element.20), channel_id=1, source_target_pairs={{0,1},{1,0},{2,3},{3,2},{4,5},{5,4},{6,7},{7,6},{8,9},{9,8},{10,11... | collective-permute-start | bytes 1966088 | tf_op jit(solution)/shard_map/left_core_swap/ppermute | solution.py:65
  26.8 5.7 %collective-permute-start.1 = (f32[8,640]{1,0:T(8,128)S(1)}, f32[8,640]{1,0:T(8,128)S(1)}, u32[]{:S(2)}, u32[]{:S(2)}) collective-permute-start(f32[8,640]{1,0:T(8,128)S(1)} %add_up.1), channel_id=1, source_target_pairs={{0,6},{1,7},{2,12},{3,13},{4,10},{5,11},{6,0},{7,1},{8,14},{9,15},... | collective-permute-start | bytes 61448 | tf_op jit(solution)/shard_map/left_sum/ppermute | solution.py:65
  32.4 6.9 %collective-permute-start.2 = (f32[8,640]{1,0:T(8,128)S(1)}, f32[8,640]{1,0:T(8,128)S(1)}, u32[]{:S(2)}, u32[]{:S(2)}) collective-permute-start(f32[8,640]{1,0:T(8,128)S(1)} %add.19), channel_id=1, source_target_pairs={{0,14},{1,15},{2,4},{3,5},{4,2},{5,3},{6,8},{7,9},{8,6},{9,7},{10,... | collective-permute-start | bytes 61448 | tf_op jit(solution)/shard_map/left_sum/ppermute | solution.py:65
  53.8 2.1 %collective-permute-start.3 = (f32[32,8,640]{2,1,0:T(8,128)S(1)}, f32[32,8,640]{2,1,0:T(8,128)S(1)}, u32[]{:S(2)}, u32[]{:S(2)}) collective-permute-start(f32[32,8,640]{2,1,0:T(8,128)S(1)} %all_to_all.11.left_ref), channel_id=1, source_target_pairs={{0,1},{1,0},{2,3},{3,2},{4,5},{5,4},{6,7},{7,6},{8,9},{9,8},{10,11... | collective-permute-start | bytes 1966088 | tf_op jit(solution)/shard_map/left_sum/ppermute | solution.py:65
  56.7 5.6 %collective-permute-start.6 = (f32[80,128]{1,0:T(8,128)S(1)}, f32[80,128]{1,0:T(8,128)S(1)}, u32[]{:S(2)}, u32[]{:S(2)}) collective-permute-start(f32[80,128]{1,0:T(8,128)S(1)} %get-tuple-element.24), channel_id=1, source_target_pairs={{0,32},{1,129},{2,34},{3,131},{4,36},{5,133},{6,38},{7,135},{8,40}... | collective-permute-start | bytes 122888 | tf_op jit(solution)/shard_map/right_sum/ppermute | solution.py:65
  58.4 4.3 %collective-permute-start.5 = (f32[80,128]{1,0:T(8,128)S(1)}, f32[80,128]{1,0:T(8,128)S(1)}, u32[]{:S(2)}, u32[]{:S(2)}) collective-permute-start(f32[80,128]{1,0:T(8,128)S(1)} %get-tuple-element.24), channel_id=1, source_target_pairs={{0,48},{1,193},{2,50},{3,195},{4,52},{5,197},{6,54},{7,199},{8,56}... | collective-permute-start | bytes 122888 | tf_op jit(solution)/shard_map/right_sum/ppermute | solution.py:65
  59.8 4.0 %collective-permute-start.4 = (f32[80,128]{1,0:T(8,128)S(1)}, f32[80,128]{1,0:T(8,128)S(1)}, u32[]{:S(2)}, u32[]{:S(2)}) collective-permute-start(f32[80,128]{1,0:T(8,128)S(1)} %get-tuple-element.24), channel_id=1, source_target_pairs={{0,16},{1,65},{2,18},{3,67},{4,20},{5,69},{6,22},{7,71},{8,24},{9,... | collective-permute-start | bytes 122888 | tf_op jit(solution)/shard_map/right_sum/ppermute | solution.py:65
  63.8 5.6 %collective-permute-start.9 = (f32[80,128]{1,0:T(8,128)S(1)}, f32[80,128]{1,0:T(8,128)S(1)}, u32[]{:S(2)}, u32[]{:S(2)}) collective-permute-start(f32[80,128]{1,0:T(8,128)S(1)} %add_add_fusion.t0_ref), channel_id=1, source_target_pairs={{0,128},{1,33},{2,130},{3,35},{4,132},{5,37},{6,134},{7,39},{8,136... | collective-permute-start | bytes 122888 | tf_op jit(solution)/shard_map/right_sum/ppermute | solution.py:65
  65.2 5.2 %collective-permute-start.8 = (f32[80,128]{1,0:T(8,128)S(1)}, f32[80,128]{1,0:T(8,128)S(1)}, u32[]{:S(2)}, u32[]{:S(2)}) collective-permute-start(f32[80,128]{1,0:T(8,128)S(1)} %add_add_fusion.t0_ref), channel_id=1, source_target_pairs={{0,192},{1,49},{2,194},{3,51},{4,196},{5,53},{6,198},{7,55},{8,200... | collective-permute-start | bytes 122888 | tf_op jit(solution)/shard_map/right_sum/ppermute | solution.py:65
  67.1 4.0 %collective-permute-start.7 = (f32[80,128]{1,0:T(8,128)S(1)}, f32[80,128]{1,0:T(8,128)S(1)}, u32[]{:S(2)}, u32[]{:S(2)}) collective-permute-start(f32[80,128]{1,0:T(8,128)S(1)} %add_add_fusion.t0_ref), channel_id=1, source_target_pairs={{0,64},{1,17},{2,66},{3,19},{4,68},{5,21},{6,70},{7,23},{8,72},{9,... | collective-permute-start | bytes 122888 | tf_op jit(solution)/shard_map/right_sum/ppermute | solution.py:65

commit v7 on v6

--- a/solution.py
+++ b/solution.py
@@ -33,13 +33,8 @@
 CORE_SWAP = pairs(lambda x, y, z, c: (x, y, z, 1 - c))
 
 
-def z_pairs(planes):
-    other = dict(planes + [(b, a) for a, b in planes])
-    return pairs(lambda x, y, z, c: (x, y, other[z], c))
-
-
-Z_NEAR = z_pairs([(1, 2), (3, 4), (5, 6), (7, 0)])
-Z_FAR = z_pairs([(1, 6), (2, 5), (0, 3), (4, 7)])
+def z_pairs(k):
+    return pairs(lambda x, y, z, c: (x, y, z ^ k, c))
 
 
 def first_pairs(k):
@@ -51,7 +46,7 @@
 
 
 GROUPS = [
-    [device(x, y, zz * 2 + (k ^ (zz & 1)), c) for k in range(2) for y in range(4) for x in range(4)]
+    [device(x, y, zz * 2 + k, c) for k in range(2) for y in range(4) for x in range(4)]
     for zz in range(4)
     for c in range(2)
 ]
@@ -379,8 +374,8 @@
     with jax.named_scope("left_sum"):
         parts = exchange(left_own + arrived)
         part = add_up(parts)
-        part = part + permute(part, Z_FAR)
-        part = part + permute(part, Z_NEAR)
+        part = part + permute(part, z_pairs(2))
+        part = part + permute(part, z_pairs(6))
         left_own = exchange(jnp.broadcast_to(part[None], (CHUNKS,) + part.shape))
         left_other = permute(left_own, CORE_SWAP)
     t_own, terms_own, gram_own = right_part(left_own, corrected_own)

time: 75.5 us -> 75.2 us (level)
  no operation moved by 1% of the time
where the time goes in v7:
time: 75.2 us; the launch traced here: 75 us
  blocking collectives  35.8 us (48%)
  starting transfers between devices  16.6 us (22%)
  Pallas kernels  12.9 us (17%)
  waiting for transfers between devices  8.84 us (12%)
    all_to_all x2, blocking collectives, exchange(): lax.all_to_all(parts, AXES, 0, 0, axis_index_groups=GROUPS, tiled=True)  35.8 us
    ppermute x10, starting transfers between devices, permute(): return lax.ppermute(a, AXES, perm)  16.6 us
    ppermute x10, waiting for transfers between devices, permute(): return lax.ppermute(a, AXES, perm)  8.84 us
    pallas_call x2, Pallas kernels, left_part(): pl.pallas_call(left_kernel, in_specs=[pl.BlockSpec(memory_space=pltpu.SME...  4.8 us
    pallas_call x1, Pallas kernels, final_part(): pl.pallas_call(final_kernel, in_specs=[pl.BlockSpec(memory_space=pltpu.SM...  4.22 us
    pallas_call x2, Pallas kernels, right_part(): pl.pallas_call(right_own_kernel if own else right_other_kernel, in_specs=...  1.86 us
  transfers between devices with their start and end apart: 10, of which 9 were waited for; matrix products, arithmetic and copies ran while one was open for 0% of the time, Pallas kernels for 7%

profile of v7, /device:TPU:2, one launch (start us, length us, event | category | flops | bytes accessed | tf_op | source)
XLA Modules:
  0.0 75.0 jit_solution(6262102845352415393)
XLA Ops:
  0.6 2.4 %left.3 = (bf16[160,5120]{1,0:T(8,128)(2,1)S(1)}, f32[32,8,640]{2,1,0:T(8,128)S(1)}) custom-call(s32[1]{0:T(128)} %bitcast.2.m_ref, bf16[1,2,160,5120]{3,2,1,0:T(8,128)(2,1)} %grads_ref.3, bf16[1,2,160,5120]{3,2,1,0:T(8,128)(2,1)} %errors_ref.3, f32[2,32,160]{2,1,0:T(8,128)} %bitcast.4), custom_call_target="tpu_custom_call" | custom-call | flops 52428800 | bytes 5570560 | tf_op jit(solution)/shard_map/left/pallas_call | solution.py:118
  3.1 0.1 collective-permute-start
  3.2 2.4 %left.2 = (bf16[160,5120]{1,0:T(8,128)(2,1)S(1)}, f32[32,8,640]{2,1,0:T(8,128)S(1)}) custom-call(s32[1]{0:T(128)} %bitcast.m_ref.core_ref, bf16[1,2,160,5120]{3,2,1,0:T(8,128)(2,1)} %grads_ref.3, bf16[1,2,160,5120]{3,2,1,0:T(8,128)(2,1)} %errors_ref.3, f32[2,32,160]{2,1,0:T(8,128)} %bitcast.5), custom_call_target="tpu_custom_call" | custom-call | flops 52428800 | bytes 5570560 | tf_op jit(solution)/shard_map/left/pallas_call | solution.py:118
  5.5 0.0 collective-permute-done
  5.6 0.1 add.18
  5.6 21.1 %all_to_all.10.parts_ref = f32[32,8,640]{2,1,0:T(8,128)S(1)} all-to-all(f32[32,8,640]{2,1,0:T(8,128)S(1)} %add.18), channel_id=1, replica_groups={{0,16,32,48,64,80,96,112,128,144,160,176,192,208,224,240,2,18,34,50,66,..., dimensions={0} | all-to-all | bytes 1310720 | tf_op jit(solution)/shard_map/left_sum/all_to_all | solution.py:56
  26.8 3.4 %collective-permute-start.1 = (f32[8,640]{1,0:T(8,128)S(1)}, f32[8,640]{1,0:T(8,128)S(1)}, u32[]{:S(2)}, u32[]{:S(2)}) collective-permute-start(f32[8,640]{1,0:T(8,128)S(1)} %add_up.1), channel_id=1, source_target_pairs={{0,4},{1,5},{2,6},{3,7},{4,0},{5,1},{6,2},{7,3},{8,12},{9,13},{10,... | collective-permute-start | bytes 61448 | tf_op jit(solution)/shard_map/left_sum/ppermute | solution.py:60
  30.1 2.0 %collective-permute-done.1 = f32[8,640]{1,0:T(8,128)S(1)} collective-permute-done((f32[8,640]{1,0:T(8,128)S(1)}, f32[8,640]{1,0:T(8,128)S(1)}, u32[]{:S(2)}, u32[]{:S(2)}) %collective-permute-start.1) | collective-permute-done | bytes 20512 | tf_op jit(solution)/shard_map/left_sum/ppermute | solution.py:60
  32.1 4.8 %collective-permute-start.2 = (f32[8,640]{1,0:T(8,128)S(1)}, f32[8,640]{1,0:T(8,128)S(1)}, u32[]{:S(2)}, u32[]{:S(2)}) collective-permute-start(f32[8,640]{1,0:T(8,128)S(1)} %add.19), channel_id=1, source_target_pairs={{0,12},{1,13},{2,14},{3,15},{4,8},{5,9},{6,10},{7,11},{8,4},{9,5},... | collective-permute-start | bytes 61448 | tf_op jit(solution)/shard_map/left_sum/ppermute | solution.py:60
  36.9 1.8 %collective-permute-done.2 = f32[8,640]{1,0:T(8,128)S(1)} collective-permute-done((f32[8,640]{1,0:T(8,128)S(1)}, f32[8,640]{1,0:T(8,128)S(1)}, u32[]{:S(2)}, u32[]{:S(2)}) %collective-permute-start.2) | collective-permute-done | bytes 20512 | tf_op jit(solution)/shard_map/left_sum/ppermute | solution.py:60
  38.8 14.7 %all_to_all.11.left_ref = f32[32,8,640]{2,1,0:T(8,128)S(1)} all-to-all(f32[32,8,640]{2,1,0:T(8,128)S(1)} %broadcast_in_dim.15), channel_id=1, replica_groups={{0,16,32,48,64,80,96,112,128,144,160,176,192,208,224,240,2,18,34,50,66,..., dimensions={0} | all-to-all | bytes 1310720 | tf_op jit(solution)/shard_map/left_sum/all_to_all | solution.py:56
  53.5 0.0 collective-permute-start.3
  53.5 1.1 %right.2 = (f32[40,128]{1,0:T(8,128)S(1)}, bf16[96,5120]{1,0:T(8,128)(2,1)S(1)}, f32[32,32]{1,0:T(8,128)S(1)}) custom-call(f32[32,8,640]{2,1,0:T(8,128)S(1)} %all_to_all.11.left_ref, bf16[160,5120]{1,0:T(8,128)(2,1)S(1)} %get-tuple-element.22.corrected_ref.corrected_own_ref), custom_call_target="tpu_custom_call" | custom-call | flops 251658240 | bytes 3276800 | tf_op jit(solution)/shard_map/right/pallas_call | solution.py:212
  54.6 1.0 %collective-permute-done.3.left_ref = f32[32,8,640]{2,1,0:T(8,128)S(1)} collective-permute-done((f32[32,8,640]{2,1,0:T(8,128)S(1)}, f32[32,8,640]{2,1,0:T(8,128)S(1)}, u32[]{:S(2)}, u32[]{:S(2)}) %collective-permute-start.3) | collective-permute-done | bytes 655392 | tf_op jit(solution)/shard_map/left_sum/ppermute | solution.py:60
  55.6 0.8 %right.3 = (f32[80,128]{1,0:T(8,128)S(1)}, bf16[96,5120]{1,0:T(8,128)(2,1)S(1)}) custom-call(f32[32,8,640]{2,1,0:T(8,128)S(1)} %collective-permute-done.3.left_ref, bf16[160,5120]{1,0:T(8,128)(2,1)S(1)} %get-tuple-element.21.corrected_ref.corrected_other_ref, f32[40,128]{1,0:T(8,128)S(1)} %get-tuple-element.23.t_own_ref), custom_call_target="tpu_custom_call" | custom-call | flops 251658240 | bytes 3276800 | tf_op jit(solution)/shard_map/right/pallas_call | solution.py:212
  56.4 1.7 %collective-permute-start.6 = (f32[80,128]{1,0:T(8,128)S(1)}, f32[80,128]{1,0:T(8,128)S(1)}, u32[]{:S(2)}, u32[]{:S(2)}) collective-permute-start(f32[80,128]{1,0:T(8,128)S(1)} %get-tuple-element.24), channel_id=1, source_target_pairs={{0,32},{1,129},{2,34},{3,131},{4,36},{5,133},{6,38},{7,135},{8,40}... | collective-permute-start | bytes 122888 | tf_op jit(solution)/shard_map/right_sum/ppermute | solution.py:60
  58.1 1.4 %collective-permute-start.5 = (f32[80,128]{1,0:T(8,128)S(1)}, f32[80,128]{1,0:T(8,128)S(1)}, u32[]{:S(2)}, u32[]{:S(2)}) collective-permute-start(f32[80,128]{1,0:T(8,128)S(1)} %get-tuple-element.24), channel_id=1, source_target_pairs={{0,48},{1,193},{2,50},{3,195},{4,52},{5,197},{6,54},{7,199},{8,56}... | collective-permute-start | bytes 122888 | tf_op jit(solution)/shard_map/right_sum/ppermute | solution.py:60
  59.5 1.7 %collective-permute-start.4 = (f32[80,128]{1,0:T(8,128)S(1)}, f32[80,128]{1,0:T(8,128)S(1)}, u32[]{:S(2)}, u32[]{:S(2)}) collective-permute-start(f32[80,128]{1,0:T(8,128)S(1)} %get-tuple-element.24), channel_id=1, source_target_pairs={{0,16},{1,65},{2,18},{3,67},{4,20},{5,69},{6,22},{7,71},{8,24},{9,... | collective-permute-start | bytes 122888 | tf_op jit(solution)/shard_map/right_sum/ppermute | solution.py:60
  61.2 0.5 gram.1.gram_other_ref
  61.7 0.3 collective-permute-done.6
  62.0 0.4 collective-permute-done.5
  62.4 1.1 %collective-permute-done.4 = f32[80,128]{1,0:T(8,128)S(1)} collective-permute-done((f32[80,128]{1,0:T(8,128)S(1)}, f32[80,128]{1,0:T(8,128)S(1)}, u32[]{:S(2)}, u32[]{:S(2)}) %collective-permute-start.4) | collective-permute-done | bytes 40992 | tf_op jit(solution)/shard_map/right_sum/ppermute | solution.py:60
  63.5 1.4 %collective-permute-start.9 = (f32[80,128]{1,0:T(8,128)S(1)}, f32[80,128]{1,0:T(8,128)S(1)}, u32[]{:S(2)}, u32[]{:S(2)}) collective-permute-start(f32[80,128]{1,0:T(8,128)S(1)} %add_add_fusion.t0_ref), channel_id=1, source_target_pairs={{0,128},{1,33},{2,130},{3,35},{4,132},{5,37},{6,134},{7,39},{8,136... | collective-permute-start | bytes 122888 | tf_op jit(solution)/shard_map/right_sum/ppermute | solution.py:60
  64.9 1.9 %collective-permute-start.8 = (f32[80,128]{1,0:T(8,128)S(1)}, f32[80,128]{1,0:T(8,128)S(1)}, u32[]{:S(2)}, u32[]{:S(2)}) collective-permute-start(f32[80,128]{1,0:T(8,128)S(1)} %add_add_fusion.t0_ref), channel_id=1, source_target_pairs={{0,192},{1,49},{2,194},{3,51},{4,196},{5,53},{6,198},{7,55},{8,200... | collective-permute-start | bytes 122888 | tf_op jit(solution)/shard_map/right_sum/ppermute | solution.py:60
  66.8 0.3 collective-permute-start.7
  67.1 1.4 %inverse.1 = (f32[2,32,32]{2,1,0:T(8,128)S(1)}, f32[2,32,32]{2,1,0:T(8,128)S(1)}) custom-call(f32[32,32]{1,0:T(8,128)S(1)} %get-tuple-element.27.gram_own_ref, f32[32,32]{1,0:T(8,128)S(1)} %gram.1.gram_other_ref), custom_call_target="tpu_custom_call" | custom-call | flops 10000000 | bytes 8000000 | tf_op jit(solution)/shard_map/inverse/pallas_call | solution.py:269
  68.5 0.6 collective-permute-done.9.t3_ref
  69.1 1.0 %collective-permute-done.8.t2_ref = f32[80,128]{1,0:T(8,128)S(1)} collective-permute-done((f32[80,128]{1,0:T(8,128)S(1)}, f32[80,128]{1,0:T(8,128)S(1)}, u32[]{:S(2)}, u32[]{:S(2)}) %collective-permute-start.8) | collective-permute-done | bytes 40992 | tf_op jit(solution)/shard_map/right_sum/ppermute | solution.py:60
  70.1 0.7 collective-permute-done.7.t1_ref
  70.8 4.2 %final.1 = (bf16[2,160,5120]{2,1,0:T(8,128)(2,1)}, bf16[1,2,160,5120]{3,2,1,0:T(8,128)(2,1)}, f32[2,32,160]{2,1,0:T(8,128)}) custom-call(s32[1]{0:T(128)} %bitcast.m_ref.core_ref, f32[80,128]{1,0:T(8,128)S(1)} %add_add_fusion.t0_ref, f32[80,128]{1,0:T(8,128)S(1)} %collective-permute-done.7.t1_ref, f32[80,128]{1,0:T(8,128)S(1)} %collective-permute-done.8.t2_ref, ...), custom_call_target="tpu_custom_call" | custom-call | flops 629145600 | bytes 13107200 | tf_op jit(solution)/shard_map/final/pallas_call | solution.py:344
  (5 shorter events, 0.1 us)
Async XLA Ops:
  3.1 2.5 %collective-permute-start = (f32[32,8,640]{2,1,0:T(8,128)S(1)}, f32[32,8,640]{2,1,0:T(8,128)S(1)}, u32[]{:S(2)}, u32[]{:S(2)}) collective-permute-start(f32[32,8,640]{2,1,0:T(8,128)S(1)} %get-tuple-element.20), channel_id=1, source_target_pairs={{0,1},{1,0},{2,3},{3,2},{4,5},{5,4},{6,7},{7,6},{8,9},{9,8},{10,11... | collective-permute-start | bytes 1966088 | tf_op jit(solution)/shard_map/left_core_swap/ppermute | solution.py:60
  26.8 5.3 %collective-permute-start.1 = (f32[8,640]{1,0:T(8,128)S(1)}, f32[8,640]{1,0:T(8,128)S(1)}, u32[]{:S(2)}, u32[]{:S(2)}) collective-permute-start(f32[8,640]{1,0:T(8,128)S(1)} %add_up.1), channel_id=1, source_target_pairs={{0,4},{1,5},{2,6},{3,7},{4,0},{5,1},{6,2},{7,3},{8,12},{9,13},{10,... | collective-permute-start | bytes 61448 | tf_op jit(solution)/shard_map/left_sum/ppermute | solution.py:60
  32.1 6.6 %collective-permute-start.2 = (f32[8,640]{1,0:T(8,128)S(1)}, f32[8,640]{1,0:T(8,128)S(1)}, u32[]{:S(2)}, u32[]{:S(2)}) collective-permute-start(f32[8,640]{1,0:T(8,128)S(1)} %add.19), channel_id=1, source_target_pairs={{0,12},{1,13},{2,14},{3,15},{4,8},{5,9},{6,10},{7,11},{8,4},{9,5},... | collective-permute-start | bytes 61448 | tf_op jit(solution)/shard_map/left_sum/ppermute | solution.py:60
  53.5 2.1 %collective-permute-start.3 = (f32[32,8,640]{2,1,0:T(8,128)S(1)}, f32[32,8,640]{2,1,0:T(8,128)S(1)}, u32[]{:S(2)}, u32[]{:S(2)}) collective-permute-start(f32[32,8,640]{2,1,0:T(8,128)S(1)} %all_to_all.11.left_ref), channel_id=1, source_target_pairs={{0,1},{1,0},{2,3},{3,2},{4,5},{5,4},{6,7},{7,6},{8,9},{9,8},{10,11... | collective-permute-start | bytes 1966088 | tf_op jit(solution)/shard_map/left_sum/ppermute | solution.py:60
  56.4 5.6 %collective-permute-start.6 = (f32[80,128]{1,0:T(8,128)S(1)}, f32[80,128]{1,0:T(8,128)S(1)}, u32[]{:S(2)}, u32[]{:S(2)}) collective-permute-start(f32[80,128]{1,0:T(8,128)S(1)} %get-tuple-element.24), channel_id=1, source_target_pairs={{0,32},{1,129},{2,34},{3,131},{4,36},{5,133},{6,38},{7,135},{8,40}... | collective-permute-start | bytes 122888 | tf_op jit(solution)/shard_map/right_sum/ppermute | solution.py:60
  58.1 4.3 %collective-permute-start.5 = (f32[80,128]{1,0:T(8,128)S(1)}, f32[80,128]{1,0:T(8,128)S(1)}, u32[]{:S(2)}, u32[]{:S(2)}) collective-permute-start(f32[80,128]{1,0:T(8,128)S(1)} %get-tuple-element.24), channel_id=1, source_target_pairs={{0,48},{1,193},{2,50},{3,195},{4,52},{5,197},{6,54},{7,199},{8,56}... | collective-permute-start | bytes 122888 | tf_op jit(solution)/shard_map/right_sum/ppermute | solution.py:60
  59.5 4.0 %collective-permute-start.4 = (f32[80,128]{1,0:T(8,128)S(1)}, f32[80,128]{1,0:T(8,128)S(1)}, u32[]{:S(2)}, u32[]{:S(2)}) collective-permute-start(f32[80,128]{1,0:T(8,128)S(1)} %get-tuple-element.24), channel_id=1, source_target_pairs={{0,16},{1,65},{2,18},{3,67},{4,20},{5,69},{6,22},{7,71},{8,24},{9,... | collective-permute-start | bytes 122888 | tf_op jit(solution)/shard_map/right_sum/ppermute | solution.py:60
  63.5 5.6 %collective-permute-start.9 = (f32[80,128]{1,0:T(8,128)S(1)}, f32[80,128]{1,0:T(8,128)S(1)}, u32[]{:S(2)}, u32[]{:S(2)}) collective-permute-start(f32[80,128]{1,0:T(8,128)S(1)} %add_add_fusion.t0_ref), channel_id=1, source_target_pairs={{0,128},{1,33},{2,130},{3,35},{4,132},{5,37},{6,134},{7,39},{8,136... | collective-permute-start | bytes 122888 | tf_op jit(solution)/shard_map/right_sum/ppermute | solution.py:60
  64.9 5.2 %collective-permute-start.8 = (f32[80,128]{1,0:T(8,128)S(1)}, f32[80,128]{1,0:T(8,128)S(1)}, u32[]{:S(2)}, u32[]{:S(2)}) collective-permute-start(f32[80,128]{1,0:T(8,128)S(1)} %add_add_fusion.t0_ref), channel_id=1, source_target_pairs={{0,192},{1,49},{2,194},{3,51},{4,196},{5,53},{6,198},{7,55},{8,200... | collective-permute-start | bytes 122888 | tf_op jit(solution)/shard_map/right_sum/ppermute | solution.py:60
  66.8 4.0 %collective-permute-start.7 = (f32[80,128]{1,0:T(8,128)S(1)}, f32[80,128]{1,0:T(8,128)S(1)}, u32[]{:S(2)}, u32[]{:S(2)}) collective-permute-start(f32[80,128]{1,0:T(8,128)S(1)} %add_add_fusion.t0_ref), channel_id=1, source_target_pairs={{0,64},{1,17},{2,66},{3,19},{4,68},{5,21},{6,70},{7,23},{8,72},{9,... | collective-permute-start | bytes 122888 | tf_op jit(solution)/shard_map/right_sum/ppermute | solution.py:60

commit v8 on v7

--- a/solution.py
+++ b/solution.py
@@ -87,8 +87,8 @@
     basis_copy = pltpu.make_async_copy(basis_ref.at[m], basis_at, basis_sem)
     basis_copy.start()
     copies = []
-    for b in range(2):
-        cols = pl.ds(b * (D // 2), D // 2)
+    for b, (at, width) in enumerate(((0, 3200), (3200, 1920))):
+        cols = pl.ds(at, width)
         pair = (
             pltpu.make_async_copy(grads_ref.at[0, m, :, cols], grads_at.at[:, cols], sems.at[b, 0]),
             pltpu.make_async_copy(
@@ -101,8 +101,8 @@
     basis_copy.wait()
     basis = basis_at[...].astype(jnp.bfloat16)
     for b in range(COL_BLOCKS):
-        if b % (COL_BLOCKS // 2) == 0:
-            for copy in copies[b // (COL_BLOCKS // 2)]:
+        if b in (0, 5):
+            for copy in copies[b // 5]:
                 copy.wait()
         cols = slice(b * CHUNK_COLS, (b + 1) * CHUNK_COLS)
         corrected = (

time: 75.2 us -> 75.2 us (level)
  no operation moved by 1% of the time
where the time goes in v8:
time: 75.2 us; the launch traced here: 75 us
  blocking collectives  35.8 us (48%)
  starting transfers between devices  16.9 us (22%)
  Pallas kernels  12.9 us (17%)
  waiting for transfers between devices  8.63 us (11%)
    all_to_all x2, blocking collectives, exchange(): lax.all_to_all(parts, AXES, 0, 0, axis_index_groups=GROUPS, tiled=True)  35.8 us
    ppermute x10, starting transfers between devices, permute(): return lax.ppermute(a, AXES, perm)  16.9 us
    ppermute x10, waiting for transfers between devices, permute(): return lax.ppermute(a, AXES, perm)  8.63 us
    pallas_call x2, Pallas kernels, left_part(): pl.pallas_call(left_kernel, in_specs=[pl.BlockSpec(memory_space=pltpu.SME...  4.83 us
    pallas_call x1, Pallas kernels, final_part(): pl.pallas_call(final_kernel, in_specs=[pl.BlockSpec(memory_space=pltpu.SM...  4.22 us
    pallas_call x2, Pallas kernels, right_part(): pl.pallas_call(right_own_kernel if own else right_other_kernel, in_specs=...  1.86 us
  transfers between devices with their start and end apart: 10, of which 9 were waited for; matrix products, arithmetic and copies ran while one was open for 0% of the time, Pallas kernels for 7%

profile of v8, /device:TPU:2, one launch (start us, length us, event | category | flops | bytes accessed | tf_op | source)
XLA Modules:
  0.0 75.0 jit_solution(6280285512086626545)
XLA Ops:
  0.6 2.5 %left.3 = (bf16[160,5120]{1,0:T(8,128)(2,1)S(1)}, f32[32,8,640]{2,1,0:T(8,128)S(1)}) custom-call(s32[1]{0:T(128)} %bitcast.2.m_ref, bf16[1,2,160,5120]{3,2,1,0:T(8,128)(2,1)} %grads_ref.3, bf16[1,2,160,5120]{3,2,1,0:T(8,128)(2,1)} %errors_ref.3, f32[2,32,160]{2,1,0:T(8,128)} %bitcast.4), custom_call_target="tpu_custom_call" | custom-call | flops 52428800 | bytes 5570560 | tf_op jit(solution)/shard_map/left/pallas_call | solution.py:118
  3.1 0.1 collective-permute-start
  3.2 2.4 %left.2 = (bf16[160,5120]{1,0:T(8,128)(2,1)S(1)}, f32[32,8,640]{2,1,0:T(8,128)S(1)}) custom-call(s32[1]{0:T(128)} %bitcast.m_ref.core_ref, bf16[1,2,160,5120]{3,2,1,0:T(8,128)(2,1)} %grads_ref.3, bf16[1,2,160,5120]{3,2,1,0:T(8,128)(2,1)} %errors_ref.3, f32[2,32,160]{2,1,0:T(8,128)} %bitcast.5), custom_call_target="tpu_custom_call" | custom-call | flops 52428800 | bytes 5570560 | tf_op jit(solution)/shard_map/left/pallas_call | solution.py:118
  5.6 0.0 collective-permute-done
  5.6 0.1 add.18
  5.7 21.1 %all_to_all.10.parts_ref = f32[32,8,640]{2,1,0:T(8,128)S(1)} all-to-all(f32[32,8,640]{2,1,0:T(8,128)S(1)} %add.18), channel_id=1, replica_groups={{0,16,32,48,64,80,96,112,128,144,160,176,192,208,224,240,2,18,34,50,66,..., dimensions={0} | all-to-all | bytes 1310720 | tf_op jit(solution)/shard_map/left_sum/all_to_all | solution.py:56
  26.8 3.4 %collective-permute-start.1 = (f32[8,640]{1,0:T(8,128)S(1)}, f32[8,640]{1,0:T(8,128)S(1)}, u32[]{:S(2)}, u32[]{:S(2)}) collective-permute-start(f32[8,640]{1,0:T(8,128)S(1)} %add_up.1), channel_id=1, source_target_pairs={{0,4},{1,5},{2,6},{3,7},{4,0},{5,1},{6,2},{7,3},{8,12},{9,13},{10,... | collective-permute-start | bytes 61448 | tf_op jit(solution)/shard_map/left_sum/ppermute | solution.py:60
  30.1 1.8 %collective-permute-done.1 = f32[8,640]{1,0:T(8,128)S(1)} collective-permute-done((f32[8,640]{1,0:T(8,128)S(1)}, f32[8,640]{1,0:T(8,128)S(1)}, u32[]{:S(2)}, u32[]{:S(2)}) %collective-permute-start.1) | collective-permute-done | bytes 20512 | tf_op jit(solution)/shard_map/left_sum/ppermute | solution.py:60
  31.9 5.0 %collective-permute-start.2 = (f32[8,640]{1,0:T(8,128)S(1)}, f32[8,640]{1,0:T(8,128)S(1)}, u32[]{:S(2)}, u32[]{:S(2)}) collective-permute-start(f32[8,640]{1,0:T(8,128)S(1)} %add.19), channel_id=1, source_target_pairs={{0,12},{1,13},{2,14},{3,15},{4,8},{5,9},{6,10},{7,11},{8,4},{9,5},... | collective-permute-start | bytes 61448 | tf_op jit(solution)/shard_map/left_sum/ppermute | solution.py:60
  37.0 1.8 %collective-permute-done.2 = f32[8,640]{1,0:T(8,128)S(1)} collective-permute-done((f32[8,640]{1,0:T(8,128)S(1)}, f32[8,640]{1,0:T(8,128)S(1)}, u32[]{:S(2)}, u32[]{:S(2)}) %collective-permute-start.2) | collective-permute-done | bytes 20512 | tf_op jit(solution)/shard_map/left_sum/ppermute | solution.py:60
  38.8 14.7 %all_to_all.11.left_ref = f32[32,8,640]{2,1,0:T(8,128)S(1)} all-to-all(f32[32,8,640]{2,1,0:T(8,128)S(1)} %broadcast_in_dim.15), channel_id=1, replica_groups={{0,16,32,48,64,80,96,112,128,144,160,176,192,208,224,240,2,18,34,50,66,..., dimensions={0} | all-to-all | bytes 1310720 | tf_op jit(solution)/shard_map/left_sum/all_to_all | solution.py:56
  53.5 0.0 collective-permute-start.3
  53.5 1.1 %right.2 = (f32[40,128]{1,0:T(8,128)S(1)}, bf16[96,5120]{1,0:T(8,128)(2,1)S(1)}, f32[32,32]{1,0:T(8,128)S(1)}) custom-call(f32[32,8,640]{2,1,0:T(8,128)S(1)} %all_to_all.11.left_ref, bf16[160,5120]{1,0:T(8,128)(2,1)S(1)} %get-tuple-element.22.corrected_ref.corrected_own_ref), custom_call_target="tpu_custom_call" | custom-call | flops 251658240 | bytes 3276800 | tf_op jit(solution)/shard_map/right/pallas_call | solution.py:212
  54.6 1.0 %collective-permute-done.3.left_ref = f32[32,8,640]{2,1,0:T(8,128)S(1)} collective-permute-done((f32[32,8,640]{2,1,0:T(8,128)S(1)}, f32[32,8,640]{2,1,0:T(8,128)S(1)}, u32[]{:S(2)}, u32[]{:S(2)}) %collective-permute-start.3) | collective-permute-done | bytes 655392 | tf_op jit(solution)/shard_map/left_sum/ppermute | solution.py:60
  55.6 0.8 %right.3 = (f32[80,128]{1,0:T(8,128)S(1)}, bf16[96,5120]{1,0:T(8,128)(2,1)S(1)}) custom-call(f32[32,8,640]{2,1,0:T(8,128)S(1)} %collective-permute-done.3.left_ref, bf16[160,5120]{1,0:T(8,128)(2,1)S(1)} %get-tuple-element.21.corrected_ref.corrected_other_ref, f32[40,128]{1,0:T(8,128)S(1)} %get-tuple-element.23.t_own_ref), custom_call_target="tpu_custom_call" | custom-call | flops 251658240 | bytes 3276800 | tf_op jit(solution)/shard_map/right/pallas_call | solution.py:212
  56.4 1.7 %collective-permute-start.6 = (f32[80,128]{1,0:T(8,128)S(1)}, f32[80,128]{1,0:T(8,128)S(1)}, u32[]{:S(2)}, u32[]{:S(2)}) collective-permute-start(f32[80,128]{1,0:T(8,128)S(1)} %get-tuple-element.24), channel_id=1, source_target_pairs={{0,32},{1,129},{2,34},{3,131},{4,36},{5,133},{6,38},{7,135},{8,40}... | collective-permute-start | bytes 122888 | tf_op jit(solution)/shard_map/right_sum/ppermute | solution.py:60
  58.1 1.4 %collective-permute-start.5 = (f32[80,128]{1,0:T(8,128)S(1)}, f32[80,128]{1,0:T(8,128)S(1)}, u32[]{:S(2)}, u32[]{:S(2)}) collective-permute-start(f32[80,128]{1,0:T(8,128)S(1)} %get-tuple-element.24), channel_id=1, source_target_pairs={{0,48},{1,193},{2,50},{3,195},{4,52},{5,197},{6,54},{7,199},{8,56}... | collective-permute-start | bytes 122888 | tf_op jit(solution)/shard_map/right_sum/ppermute | solution.py:60
  59.5 1.7 %collective-permute-start.4 = (f32[80,128]{1,0:T(8,128)S(1)}, f32[80,128]{1,0:T(8,128)S(1)}, u32[]{:S(2)}, u32[]{:S(2)}) collective-permute-start(f32[80,128]{1,0:T(8,128)S(1)} %get-tuple-element.24), channel_id=1, source_target_pairs={{0,16},{1,65},{2,18},{3,67},{4,20},{5,69},{6,22},{7,71},{8,24},{9,... | collective-permute-start | bytes 122888 | tf_op jit(solution)/shard_map/right_sum/ppermute | solution.py:60
  61.2 0.5 gram.1.gram_other_ref
  61.7 0.3 collective-permute-done.6
  62.0 0.4 collective-permute-done.5
  62.4 1.1 %collective-permute-done.4 = f32[80,128]{1,0:T(8,128)S(1)} collective-permute-done((f32[80,128]{1,0:T(8,128)S(1)}, f32[80,128]{1,0:T(8,128)S(1)}, u32[]{:S(2)}, u32[]{:S(2)}) %collective-permute-start.4) | collective-permute-done | bytes 40992 | tf_op jit(solution)/shard_map/right_sum/ppermute | solution.py:60
  63.5 1.4 %collective-permute-start.9 = (f32[80,128]{1,0:T(8,128)S(1)}, f32[80,128]{1,0:T(8,128)S(1)}, u32[]{:S(2)}, u32[]{:S(2)}) collective-permute-start(f32[80,128]{1,0:T(8,128)S(1)} %add_add_fusion.t0_ref), channel_id=1, source_target_pairs={{0,128},{1,33},{2,130},{3,35},{4,132},{5,37},{6,134},{7,39},{8,136... | collective-permute-start | bytes 122888 | tf_op jit(solution)/shard_map/right_sum/ppermute | solution.py:60
  64.9 1.9 %collective-permute-start.8 = (f32[80,128]{1,0:T(8,128)S(1)}, f32[80,128]{1,0:T(8,128)S(1)}, u32[]{:S(2)}, u32[]{:S(2)}) collective-permute-start(f32[80,128]{1,0:T(8,128)S(1)} %add_add_fusion.t0_ref), channel_id=1, source_target_pairs={{0,192},{1,49},{2,194},{3,51},{4,196},{5,53},{6,198},{7,55},{8,200... | collective-permute-start | bytes 122888 | tf_op jit(solution)/shard_map/right_sum/ppermute | solution.py:60
  66.8 0.3 collective-permute-start.7
  67.1 1.4 %inverse.1 = (f32[2,32,32]{2,1,0:T(8,128)S(1)}, f32[2,32,32]{2,1,0:T(8,128)S(1)}) custom-call(f32[32,32]{1,0:T(8,128)S(1)} %get-tuple-element.27.gram_own_ref, f32[32,32]{1,0:T(8,128)S(1)} %gram.1.gram_other_ref), custom_call_target="tpu_custom_call" | custom-call | flops 10000000 | bytes 8000000 | tf_op jit(solution)/shard_map/inverse/pallas_call | solution.py:269
  68.5 0.6 collective-permute-done.9.t3_ref
  69.1 1.0 %collective-permute-done.8.t2_ref = f32[80,128]{1,0:T(8,128)S(1)} collective-permute-done((f32[80,128]{1,0:T(8,128)S(1)}, f32[80,128]{1,0:T(8,128)S(1)}, u32[]{:S(2)}, u32[]{:S(2)}) %collective-permute-start.8) | collective-permute-done | bytes 40992 | tf_op jit(solution)/shard_map/right_sum/ppermute | solution.py:60
  70.1 0.7 collective-permute-done.7.t1_ref
  70.8 4.2 %final.1 = (bf16[2,160,5120]{2,1,0:T(8,128)(2,1)}, bf16[1,2,160,5120]{3,2,1,0:T(8,128)(2,1)}, f32[2,32,160]{2,1,0:T(8,128)}) custom-call(s32[1]{0:T(128)} %bitcast.m_ref.core_ref, f32[80,128]{1,0:T(8,128)S(1)} %add_add_fusion.t0_ref, f32[80,128]{1,0:T(8,128)S(1)} %collective-permute-done.7.t1_ref, f32[80,128]{1,0:T(8,128)S(1)} %collective-permute-done.8.t2_ref, ...), custom_call_target="tpu_custom_call" | custom-call | flops 629145600 | bytes 13107200 | tf_op jit(solution)/shard_map/final/pallas_call | solution.py:344
  (5 shorter events, 0.1 us)
Async XLA Ops:
  3.1 2.5 %collective-permute-start = (f32[32,8,640]{2,1,0:T(8,128)S(1)}, f32[32,8,640]{2,1,0:T(8,128)S(1)}, u32[]{:S(2)}, u32[]{:S(2)}) collective-permute-start(f32[32,8,640]{2,1,0:T(8,128)S(1)} %get-tuple-element.20), channel_id=1, source_target_pairs={{0,1},{1,0},{2,3},{3,2},{4,5},{5,4},{6,7},{7,6},{8,9},{9,8},{10,11... | collective-permute-start | bytes 1966088 | tf_op jit(solution)/shard_map/left_core_swap/ppermute | solution.py:60
  26.8 5.1 %collective-permute-start.1 = (f32[8,640]{1,0:T(8,128)S(1)}, f32[8,640]{1,0:T(8,128)S(1)}, u32[]{:S(2)}, u32[]{:S(2)}) collective-permute-start(f32[8,640]{1,0:T(8,128)S(1)} %add_up.1), channel_id=1, source_target_pairs={{0,4},{1,5},{2,6},{3,7},{4,0},{5,1},{6,2},{7,3},{8,12},{9,13},{10,... | collective-permute-start | bytes 61448 | tf_op jit(solution)/shard_map/left_sum/ppermute | solution.py:60
  31.9 6.8 %collective-permute-start.2 = (f32[8,640]{1,0:T(8,128)S(1)}, f32[8,640]{1,0:T(8,128)S(1)}, u32[]{:S(2)}, u32[]{:S(2)}) collective-permute-start(f32[8,640]{1,0:T(8,128)S(1)} %add.19), channel_id=1, source_target_pairs={{0,12},{1,13},{2,14},{3,15},{4,8},{5,9},{6,10},{7,11},{8,4},{9,5},... | collective-permute-start | bytes 61448 | tf_op jit(solution)/shard_map/left_sum/ppermute | solution.py:60
  53.5 2.1 %collective-permute-start.3 = (f32[32,8,640]{2,1,0:T(8,128)S(1)}, f32[32,8,640]{2,1,0:T(8,128)S(1)}, u32[]{:S(2)}, u32[]{:S(2)}) collective-permute-start(f32[32,8,640]{2,1,0:T(8,128)S(1)} %all_to_all.11.left_ref), channel_id=1, source_target_pairs={{0,1},{1,0},{2,3},{3,2},{4,5},{5,4},{6,7},{7,6},{8,9},{9,8},{10,11... | collective-permute-start | bytes 1966088 | tf_op jit(solution)/shard_map/left_sum/ppermute | solution.py:60
  56.4 5.6 %collective-permute-start.6 = (f32[80,128]{1,0:T(8,128)S(1)}, f32[80,128]{1,0:T(8,128)S(1)}, u32[]{:S(2)}, u32[]{:S(2)}) collective-permute-start(f32[80,128]{1,0:T(8,128)S(1)} %get-tuple-element.24), channel_id=1, source_target_pairs={{0,32},{1,129},{2,34},{3,131},{4,36},{5,133},{6,38},{7,135},{8,40}... | collective-permute-start | bytes 122888 | tf_op jit(solution)/shard_map/right_sum/ppermute | solution.py:60
  58.1 4.3 %collective-permute-start.5 = (f32[80,128]{1,0:T(8,128)S(1)}, f32[80,128]{1,0:T(8,128)S(1)}, u32[]{:S(2)}, u32[]{:S(2)}) collective-permute-start(f32[80,128]{1,0:T(8,128)S(1)} %get-tuple-element.24), channel_id=1, source_target_pairs={{0,48},{1,193},{2,50},{3,195},{4,52},{5,197},{6,54},{7,199},{8,56}... | collective-permute-start | bytes 122888 | tf_op jit(solution)/shard_map/right_sum/ppermute | solution.py:60
  59.5 4.0 %collective-permute-start.4 = (f32[80,128]{1,0:T(8,128)S(1)}, f32[80,128]{1,0:T(8,128)S(1)}, u32[]{:S(2)}, u32[]{:S(2)}) collective-permute-start(f32[80,128]{1,0:T(8,128)S(1)} %get-tuple-element.24), channel_id=1, source_target_pairs={{0,16},{1,65},{2,18},{3,67},{4,20},{5,69},{6,22},{7,71},{8,24},{9,... | collective-permute-start | bytes 122888 | tf_op jit(solution)/shard_map/right_sum/ppermute | solution.py:60
  63.5 5.6 %collective-permute-start.9 = (f32[80,128]{1,0:T(8,128)S(1)}, f32[80,128]{1,0:T(8,128)S(1)}, u32[]{:S(2)}, u32[]{:S(2)}) collective-permute-start(f32[80,128]{1,0:T(8,128)S(1)} %add_add_fusion.t0_ref), channel_id=1, source_target_pairs={{0,128},{1,33},{2,130},{3,35},{4,132},{5,37},{6,134},{7,39},{8,136... | collective-permute-start | bytes 122888 | tf_op jit(solution)/shard_map/right_sum/ppermute | solution.py:60
  64.9 5.2 %collective-permute-start.8 = (f32[80,128]{1,0:T(8,128)S(1)}, f32[80,128]{1,0:T(8,128)S(1)}, u32[]{:S(2)}, u32[]{:S(2)}) collective-permute-start(f32[80,128]{1,0:T(8,128)S(1)} %add_add_fusion.t0_ref), channel_id=1, source_target_pairs={{0,192},{1,49},{2,194},{3,51},{4,196},{5,53},{6,198},{7,55},{8,200... | collective-permute-start | bytes 122888 | tf_op jit(solution)/shard_map/right_sum/ppermute | solution.py:60
  66.8 4.0 %collective-permute-start.7 = (f32[80,128]{1,0:T(8,128)S(1)}, f32[80,128]{1,0:T(8,128)S(1)}, u32[]{:S(2)}, u32[]{:S(2)}) collective-permute-start(f32[80,128]{1,0:T(8,128)S(1)} %add_add_fusion.t0_ref), channel_id=1, source_target_pairs={{0,64},{1,17},{2,66},{3,19},{4,68},{5,21},{6,70},{7,23},{8,72},{9,... | collective-permute-start | bytes 122888 | tf_op jit(solution)/shard_map/right_sum/ppermute | solution.py:60
